TPU v7x, 32 devices: a whole 2x2x4 slice. The times are simulated.
32 devices in a mesh: slide: 2 (over x), space: 8 (over z, y), tensor: 2 (over core).
Axes of the slice: x: 2, y: 2, z: 4, core: 2. Of those that a mesh axis runs over, the one named last changes fastest.
Arguments:
- features: bfloat16 [64, 16, 16, 768], P(('slide', 'space'), None, None, 'tensor'), parts along dimension 0, may hold values from -6 to 6
- dw_kernel: float32 [49, 768], P(None, 'tensor'), may hold values from -0.875 to 0.875
- dw_bias: float32 [768], P('tensor'), may hold values from -3 to 3
- ln_gain: float32 [768], replicated, may hold values from 0.5 to 1.5
- ln_bias: float32 [768], replicated, may hold values from -2 to 2
- w_up: bfloat16 [768, 3072], P(None, 'tensor'), may hold values from -0.21875 to 0.21875
- up_bias: float32 [3072], P('tensor'), may hold values from -3 to 3
- w_down: bfloat16 [768, 3072], P(None, 'tensor'), may hold values from -0.109375 to 0.109375
- down_bias: float32 [768], P('tensor'), may hold values from -2 to 2
- layer_scale: float32 [768], P('tensor'), may hold values from 0.3 to 1.5
- cotangent: bfloat16 [64, 16, 16, 768], P(('slide', 'space'), None, None, 'tensor'), parts along dimension 0, may hold values from -4 to 4
- neighbors: int32 [64, 8], P('slide'), parts along dimension 0, may hold values from -1 to 31, as said below
- tissue_count: int32 [16], P('slide'), parts along dimension 0, may hold values from 1 to 4, as said below
Outputs:
- block_out: bfloat16 [64, 16, 16, 768], P(('slide', 'space'), None, None, 'tensor'), parts along dimension 0
- grad_features: bfloat16 [64, 16, 16, 768], P(('slide', 'space'), None, None, 'tensor'), parts along dimension 0
- grad_up: float32 [1536, 3072], P(('slide', 'space'), 'tensor'), parts along dimension 0
- grad_down: float32 [1536, 3072], P(('slide', 'space'), 'tensor'), parts along dimension 0
- grad_kernel: float32 [98, 768], P('slide', 'tensor'), parts along dimension 0
There are 2 independent parts, one for each index of `slide`. A program takes and returns all parts, laid end to end along the dimension named above; an argument that names none is the same for every part. Nothing has to cross between parts.
Inputs may be any that keep to these rules, and one draw needn't show every extreme that they name: `neighbors`: the tiles lie on a grid of 2 by 2 blocks with R block rows and 8 / R block columns, R the largest divisor of 8 not above its square root; device d of space holds the block at block row d // (8 / R) and block column d mod (8 / R), its slot 2 r + q (slot s belongs to device s // 4) at row r and column q of the block. Entry [s, k] is the slot of the tissue tile beside slot s's tile on this grid in direction k (0 north, 1 south, 2 west, 3 east, 4 north-west, 5 north-east, 6 south-west, 7 south-east), or -1 where that place lies outside the grid or holds no tissue; empty slots have no neighbours. The tissue tiles of device d fill its first tissue_count[d] slots; its other slots are empty.
All inputs are finite; a program needn't handle non-finite values.
Results may differ from a plain program's by a relative error of at most 0.008.
Values may be sent and summed in bfloat16 or wider, within the bound.
No kernel may reach another device: no remote copies, remote signals or barrier semaphores. Data moves between devices by JAX's collectives and lax.ppermute only.
A program may use at most 128 MiB of HBM per device.

v0:
```python
import math

import jax
import jax.numpy as jnp
from jax import lax
from jax.sharding import PartitionSpec as P

KERNEL = 7


DIRECTIONS = ((-1, 0), (1, 0), (0, -1), (0, 1), (-1, -1), (-1, 1), (1, -1), (1, 1))
root_half = 0.7071067811865476
density_norm = 0.3989422804014327


def shifted(value, axis, by):
    size = lax.axis_size(axis)
    pairs = [(i, i + by) for i in range(size) if 0 <= i + by < size]
    return lax.ppermute(value, axis, pairs)


def rim_range(side_len, facing, rim_width):
    if facing < 0:
        return (0, rim_width)
    if facing > 0:
        return (side_len - rim_width, side_len)
    return (0, side_len)


def cut_rim(blocks, direction, facing_sign, rim_width):
    step_row, step_col = DIRECTIONS[direction]
    row_lo, row_hi = rim_range(blocks.shape[1], facing_sign * step_row, rim_width)
    col_lo, col_hi = rim_range(blocks.shape[2], facing_sign * step_col, rim_width)
    return blocks[:, row_lo:row_hi, col_lo:col_hi, :]


def assemble(center, rim_parts):
    top_band = jnp.concatenate([rim_parts[4], rim_parts[0], rim_parts[5]], axis=2)
    mid_band = jnp.concatenate([rim_parts[2], center, rim_parts[3]], axis=2)
    bottom_band = jnp.concatenate([rim_parts[6], rim_parts[1], rim_parts[7]], axis=2)
    return jnp.concatenate([top_band, mid_band, bottom_band], axis=1)


def depthwise(padded, kernel, side_len, flipped):
    rim_width = KERNEL // 2
    running = jnp.zeros((padded.shape[0], side_len, side_len, padded.shape[3]), jnp.float32)
    for row_tap in range(KERNEL):
        for col_tap in range(KERNEL):
            row_at = 2 * rim_width - row_tap if flipped else row_tap
            col_at = 2 * rim_width - col_tap if flipped else col_tap
            window = padded[:, row_at : row_at + side_len, col_at : col_at + side_len, :].astype(
                jnp.float32
            )
            running = running + window * kernel[row_tap * KERNEL + col_tap]
    return running


def kernel_terms(padded, conv_grad, side_len):
    grad_values = conv_grad.astype(jnp.float32)
    rows_out = []
    for row_tap in range(KERNEL):
        for col_tap in range(KERNEL):
            window = padded[
                :, row_tap : row_tap + side_len, col_tap : col_tap + side_len, :
            ].astype(jnp.float32)
            rows_out.append(jnp.sum(window * grad_values, axis=(0, 1, 2)))
    return jnp.stack(rows_out, axis=0)


def gelu_slope(values):
    cumulative = 0.5 * (1.0 + lax.erf(values * root_half))
    density = jnp.exp(-0.5 * values * values) * density_norm
    return cumulative + values * density


def build_plan():
    plan = {}
    for offset in DIRECTIONS + ((0, 0),):
        plan[offset] = []
    for slot in range(4):
        local_row, local_col = (slot // 2, slot % 2)
        for direction in range(8):
            step_row, step_col = DIRECTIONS[direction]
            grid_row = local_row + step_row
            grid_col = local_col + step_col
            sender = grid_row % 2 * 2 + grid_col % 2
            plan[grid_row // 2, grid_col // 2].append((slot, direction, sender))
    return plan


def on_device(
    features,
    dw_kernel,
    dw_bias,
    ln_gain,
    ln_bias,
    w_up,
    up_bias,
    w_down,
    down_bias,
    layer_scale,
    cotangent,
    neighbors,
    tissue_count,
):
    tiles_dev, tile_side, _, chans = features.shape
    rim_width = KERNEL // 2
    devices = lax.axis_size("space")
    own_index = lax.axis_index("space")
    tensor_index = lax.axis_index("tensor")
    block_rows = max(
        (divisor for divisor in range(1, math.isqrt(devices) + 1) if devices % divisor == 0)
    )
    block_cols = devices // block_rows
    plan = build_plan()
    my_near = lax.dynamic_slice_in_dim(neighbors, own_index * tiles_dev, tiles_dev, 0)

    def rim_shape(direction):
        step_row, step_col = DIRECTIONS[direction]
        row_count = rim_width if step_row != 0 else tile_side
        col_count = rim_width if step_col != 0 else tile_side
        return (row_count, col_count)

    def pack_offset(blocks, offset):
        pieces = []
        for slot, direction, sender in plan[offset]:
            rim_piece = cut_rim(blocks[sender : sender + 1], direction, -1, rim_width)
            pieces.append(rim_piece.reshape(-1, chans))
        return jnp.concatenate(pieces, axis=0)

    def exchange_rims(blocks):
        packs = {}
        for offset in DIRECTIONS + ((0, 0),):
            packs[offset] = pack_offset(blocks, offset)
        arrived = {(0, 0): packs[0, 0]}
        for offset in DIRECTIONS:
            arrived[offset] = shifted(packs[offset], "space", -(offset[0] * block_cols + offset[1]))
        rim_lists = [[None] * tiles_dev for direction in range(8)]
        for offset in DIRECTIONS + ((0, 0),):
            source = arrived[offset]
            cursor = 0
            for slot, direction, sender in plan[offset]:
                row_count, col_count = rim_shape(direction)
                count = row_count * col_count
                rim_lists[direction][slot] = source[cursor : cursor + count].reshape(
                    row_count, col_count, chans
                )
                cursor = cursor + count
        rim_parts = []
        for direction in range(8):
            stacked = jnp.stack(rim_lists[direction], axis=0)
            valid = (my_near[:, direction] >= 0)[:, None, None, None]
            rim_parts.append(jnp.where(valid, stacked, jnp.zeros((), blocks.dtype)))
        return assemble(blocks, rim_parts)

    tile_ok = (jnp.arange(tiles_dev, dtype=jnp.int32) < tissue_count[own_index]).astype(jnp.float32)
    row_ok = jnp.repeat(tile_ok, tile_side * tile_side)[:, None]
    feature_pad = exchange_rims(features)
    conv_out = (depthwise(feature_pad, dw_kernel, tile_side, False) + dw_bias).astype(jnp.bfloat16)
    conv_rows = lax.all_gather(conv_out.reshape(-1, chans), "tensor", axis=1, tiled=True).astype(
        jnp.float32
    )
    total_chans = conv_rows.shape[1]
    row_mean = jnp.mean(conv_rows, axis=1, keepdims=True)
    centered = conv_rows - row_mean
    row_var = jnp.mean(centered * centered, axis=1, keepdims=True)
    inverse_std = lax.rsqrt(row_var + 1e-06)
    normalized = centered * inverse_std
    normed = (normalized * ln_gain + ln_bias).astype(jnp.bfloat16)
    hidden = jnp.dot(normed, w_up, preferred_element_type=jnp.float32) + up_bias
    active = jax.nn.gelu(hidden, approximate=False).astype(jnp.bfloat16)
    partial_value = lax.dot_general(
        active, w_down, (((1,), (1,)), ((), ())), preferred_element_type=jnp.float32
    )
    branch = (
        lax.psum_scatter(
            partial_value.astype(jnp.bfloat16), "tensor", scatter_dimension=1, tiled=True
        ).astype(jnp.float32)
        + down_bias
    )
    residual = features.reshape(-1, chans).astype(jnp.float32)
    block_out = (
        ((residual + layer_scale * branch) * row_ok).astype(jnp.bfloat16).reshape(features.shape)
    )
    grad_out = cotangent.reshape(-1, chans).astype(jnp.float32) * row_ok
    branch_grad = (grad_out * layer_scale).astype(jnp.bfloat16)
    grad_full = lax.all_gather(branch_grad, "tensor", axis=1, tiled=True)
    grad_scale = lax.rsqrt(
        jnp.float32(tile_side * tile_side) * jnp.sum(tissue_count).astype(jnp.float32)
    )
    grad_down = (
        lax.psum_scatter(
            lax.dot_general(
                grad_full, active, (((0,), (0,)), ((), ())), preferred_element_type=jnp.float32
            ),
            "space",
            scatter_dimension=0,
            tiled=True,
        )
        * grad_scale
    )
    act_grad = jnp.dot(grad_full, w_down, preferred_element_type=jnp.float32)
    pre_grad = (act_grad * gelu_slope(hidden)).astype(jnp.bfloat16)
    grad_up = (
        lax.psum_scatter(
            lax.dot_general(
                normed, pre_grad, (((0,), (0,)), ((), ())), preferred_element_type=jnp.float32
            ),
            "space",
            scatter_dimension=0,
            tiled=True,
        )
        * grad_scale
    )
    norm_part = lax.dot_general(
        pre_grad, w_up, (((1,), (1,)), ((), ())), preferred_element_type=jnp.float32
    )
    chan_start = tensor_index * chans
    norm_grad = lax.psum_scatter(norm_part, "tensor", scatter_dimension=1, tiled=True)
    my_normalized = lax.dynamic_slice_in_dim(normalized, chan_start, chans, 1)
    my_gain = lax.dynamic_slice_in_dim(ln_gain, chan_start, chans, 0)
    scaled = norm_grad * my_gain
    first_sum, second_sum = lax.psum(
        (jnp.sum(scaled, axis=1), jnp.sum(scaled * my_normalized, axis=1)), "tensor"
    )
    conv_grad = inverse_std * (
        scaled
        - first_sum[:, None] / total_chans
        - my_normalized * (second_sum[:, None] / total_chans)
    )
    conv_grad = conv_grad.astype(jnp.bfloat16).reshape(features.shape)
    grad_pad = exchange_rims(conv_grad)
    back_conv = depthwise(grad_pad, dw_kernel, tile_side, True)
    grad_features = (
        (grad_out.reshape(features.shape) + back_conv) * tile_ok[:, None, None, None]
    ).astype(jnp.bfloat16)
    kernel_local = kernel_terms(feature_pad, conv_grad, tile_side)
    grad_kernel = lax.psum(kernel_local, "space") * grad_scale
    return (block_out, grad_features, grad_up, grad_down, grad_kernel)


def solution(mesh):
    return jax.shard_map(
        on_device,
        mesh=mesh,
        in_specs=(
            P(("slide", "space"), None, None, "tensor"),
            P(None, "tensor"),
            P("tensor"),
            P(),
            P(),
            P(None, "tensor"),
            P("tensor"),
            P(None, "tensor"),
            P("tensor"),
            P("tensor"),
            P(("slide", "space"), None, None, "tensor"),
            P("slide", None),
            P("slide"),
        ),
        out_specs=(
            P(("slide", "space"), None, None, "tensor"),
            P(("slide", "space"), None, None, "tensor"),
            P(("slide", "space"), "tensor"),
            P(("slide", "space"), "tensor"),
            P("slide", "tensor"),
        ),
        check_vma=False,
    )
```

profile of v0, /device:TPU:0, one launch (start us, length us, event | category | flops | bytes accessed | tf_op | source)
XLA Modules:
  0.0 504.5 jit_solution(9583323223146272403)
XLA Ops:
  14.4 7.6 %collective-permute-start.3 = (bf16[9,384]{1,0:T(8,128)(2,1)}, bf16[9,384]{1,0:T(8,128)(2,1)}, u32[]{:S(2)}, u32[]{:S(2)}) collective-permute-start(bf16[9,384]{1,0:T(8,128)(2,1)} %reshape.298), channel_id=1, source_target_pairs={{0,6},{2,8},{4,10},{6,12},{8,14},{1,7},{3,9},{5,11},{7,13},{9,15},... | collective-permute-start | bytes 20744 | tf_op jit(solution)/shard_map/ppermute | solution.py:19
  22.6 2.3 collective-permute-start
  43.3 5.0 collective-permute-start.2
  49.6 5.2 %collective-permute-start.1 = (bf16[114,384]{1,0:T(8,128)(2,1)}, bf16[114,384]{1,0:T(8,128)(2,1)S(1)}, u32[]{:S(2)}, u32[]{:S(2)}) collective-permute-start(bf16[114,384]{1,0:T(8,128)(2,1)} %pad_maximum_fusion.4), channel_id=1, source_target_pairs={{0,8},{2,10},{4,12},{6,14},{1,9},{3,11},{5,13},{7,15},{16,24},{18,... | collective-permute-start | bytes 262664 | tf_op jit(solution)/shard_map/ppermute | solution.py:19
  81.5 13.8 %add_convert_fusion.1 = bf16[4,16,16,384]{3,2,1,0:T(8,128)(2,1)} fusion(bf16[4,16,16,384]{3,2,1,0:T(8,128)(2,1)S(1)} %copy-done.5, f32[384]{0:T(512)} %param.15, f32[384]{0:T(512)S(1)} %copy-done.33, f32[384]{0:T(512)S(1)} %copy-done.35, f32[384]{0:T(512)S(1)} %copy-done.39, f32[384]{0:T(512)S(1)} %copy-done.41, f32[384]{0:T(512)S(1)} %copy-done.43, ...), kind=kLoop, calls=%fused_computation.262 | loop fusion | flops 65273856 | bytes 34974720 | tf_op jit(solution)/shard_map/convert_element_type | solution.py:159
  95.6 13.2 %all-gather.3.cloned.1.call-done = bf16[1024,768]{1,0:T(8,128)(2,1)} async-done(((bf16[1024,384]{1,0:T(8,128)(2,1)}), bf16[1024,768]{1,0:T(8,128)(2,1)}) %all-gather.3.cloned.1.call-update) | async-done | bytes 1572880 | tf_op jit(solution)/shard_map/all_gather | solution.py:160
  111.3 18.2 %fusion.2 = (bf16[1024,1536]{1,0:T(8,128)(2,1)S(1)}, f32[1024,1536]{1,0:T(8,128)}) fusion(f32[1536]{0:T(1024)} %param.19, bf16[768,1536]{1,0:T(8,128)(2,1)S(1)} %copy-done, f32[768]{0:T(1024)} %param.17, f32[768]{0:T(1024)} %param.16, f32[1024]{0:T(1024)S(1)} %add_rsqrt_fusion, f32[1024]{0:T(1024)S(1)} %broadcast_multiply_fusion.5, ...), kind=kOutput, calls=%fused_computation.54 | convolution fusion | flops 2524446720 | bytes 13389824 | tf_op jit(solution)/shard_map/dot_general | solution.py:170
  131.1 3.7 convolution_convert_fusion
  134.8 2.6 copy.18
  140.4 7.4 %reduce-scatter.13.cloned.1.call-done = bf16[384,1024]{1,0:T(8,128)(2,1)} async-done(((bf16[768,1024]{1,0:T(8,128)(2,1)}), bf16[384,1024]{1,0:T(8,128)(2,1)}) %reduce-scatter.13.cloned.1.call-update) | async-done | bytes 786448
  147.8 2.3 copy.19
  150.1 3.1 fusion.142
  153.2 11.1 %all-gather.5.cloned.1.call-done = bf16[1024,768]{1,0:T(8,128)(2,1)} async-done(((bf16[1024,384]{1,0:T(8,128)(2,1)}), bf16[1024,768]{1,0:T(8,128)(2,1)}) %all-gather.5.cloned.1.call-update) | async-done | bytes 1572880 | tf_op jit(solution)/shard_map/all_gather | solution.py:187
  164.3 6.8 %fusion.8 = bf16[1024,1536]{1,0:T(8,128)(2,1)S(1)} fusion(f32[1024,1536]{1,0:T(8,128)} %get-tuple-element.227, bf16[1024,768]{1,0:T(8,128)(2,1)} %all-gather.5.cloned.1.call-done, bf16[768,1536]{1,0:T(8,128)(2,1)} %param.20, f32[1536]{0:T(1024)} %param.19), kind=kOutput, calls=%fused_computation.60 | convolution fusion | flops 2433220608 | bytes 13375488 | tf_op jit(solution)/shard_map/dot_general | solution.py:202
  172.7 4.3 fusion.190
  177.8 3.5 fusion.16
  181.3 7.9 %reduce-scatter.7.cloned.1.call-done = f32[1024,384]{1,0:T(8,128)} async-done(((f32[1024,768]{1,0:T(8,128)}), f32[1024,384]{1,0:T(8,128)}) %reduce-scatter.7.cloned.1.call-update) | async-done | bytes 1572880 | tf_op jit(solution)/shard_map/reduce_scatter | solution.py:219
  189.3 2.3 multiply_reduce_fusion.1
  191.5 2.7 all-reduce
  194.3 14.6 %fusion.140 = (f32[384]{0:T(512)S(1)}, f32[384]{0:T(512)S(1)}, f32[384]{0:T(512)S(1)}, f32[384]{0:T(512)S(1)}, f32[384]{0:T(512)S(1)}, /*index=5*/f32[384]{0:T(5...) fusion(bf16[4,19,22,384]{3,2,1,0:T(8,128)(2,1)} %copy-done.1, ...), kind=kLoop, calls=%fused_computation.252 | loop fusion | flops 23979264 | bytes 18129412 | tf_op jit(solution)/shard_map/reduce_sum | solution.py:66
  210.2 4.1 fusion.112
  214.3 2.2 fusion.119
  217.0 4.4 stack.265
  221.5 7.4 %fusion.153 = f32[768,1536]{1,0:T(8,128)} fusion(bf16[1024,1536]{1,0:T(8,128)(2,1)} %copy-done.101, f32[768]{0:T(1024)} %param.17, f32[768]{0:T(1024)} %param.16, bf16[1024,768]{1,0:T(8,128)(2,1)} %all-gather.3.cloned.1.call-done, f32[1024]{0:T(1024)S(1)} %add_rsqrt_fusion, f32[1024]{0:T(1024)S(1)} %broadcast_multiply_fusion.5), kind=kOutput, calls=%fused_computation.296 | convolution fusion | flops 2420637696 | bytes 9451520 | tf_op jit(solution)/shard_map/dot_general | solution.py:206
  230.8 7.2 %fusion.191 = f32[768,1536]{1,0:T(8,128)} fusion(bf16[1024,768]{1,0:T(8,128)(2,1)} %all-gather.5.cloned.1.call-done, bf16[1024,1536]{1,0:T(8,128)(2,1)} %copy-done.8), kind=kOutput, calls=%fused_computation.423 | convolution fusion | flops 2415919104 | bytes 9437184 | tf_op jit(solution)/shard_map/dot_general | solution.py:193
  248.5 4.2 collective-permute-start.8
  270.5 6.0 %collective-permute-start.15 = (bf16[9,384]{1,0:T(8,128)(2,1)}, bf16[9,384]{1,0:T(8,128)(2,1)}, u32[]{:S(2)}, u32[]{:S(2)}) collective-permute-start(bf16[9,384]{1,0:T(8,128)(2,1)} %reshape.331), channel_id=1, source_target_pairs={{0,6},{2,8},{4,10},{6,12},{8,14},{1,7},{3,9},{5,11},{7,13},{9,15},... | collective-permute-start | bytes 20744 | tf_op jit(solution)/shard_map/ppermute | solution.py:19
  280.5 3.4 collective-permute-start.13
  297.4 6.7 %collective-permute-start.14 = (bf16[114,384]{1,0:T(8,128)(2,1)}, bf16[114,384]{1,0:T(8,128)(2,1)}, u32[]{:S(2)}, u32[]{:S(2)}) collective-permute-start(bf16[114,384]{1,0:T(8,128)(2,1)} %pad_maximum_fusion.11), channel_id=1, source_target_pairs={{0,8},{2,10},{4,12},{6,14},{1,9},{3,11},{5,13},{7,15},{16,24},{18,... | collective-permute-start | bytes 262664 | tf_op jit(solution)/shard_map/ppermute | solution.py:19
  337.0 14.3 %multiply_convert_fusion = bf16[4,16,16,384]{3,2,1,0:T(8,128)(2,1)} fusion(bf16[4,16,16,384]{3,2,1,0:T(8,128)(2,1)S(1)} %bitcast.117, bf16[4,16,3,384]{3,2,1,0:T(4,128)(2,1)S(1)} %maximum_select_fusion.2, bf16[4,16,3,384]{3,2,1,0:T(4,128)(2,1)S(1)} %maximum_select_fusion.3, bf16[4,19,22,384]{3,2,1,0:T(8,128)(2,1)S(1)} %get-tuple-element.115, ...), kind=kLoop, calls=%fused_computation.259 | loop fusion | flops 66453504 | bytes 35759632 | tf_op jit(solution)/shard_map/convert_element_type | solution.py:236
  351.3 45.1 %reduce-scatter.9.cloned.1.call-done = f32[96,1536]{1,0:T(8,128)} async-done(((f32[768,1536]{1,0:T(8,128)}), f32[96,1536]{1,0:T(8,128)}) %reduce-scatter.9.cloned.1.call-update) | async-done | bytes 589840 | tf_op jit(solution)/shard_map/reduce_scatter | solution.py:205
  398.4 96.9 %reduce-scatter.11.cloned.1.call-done = f32[96,1536]{1,0:T(8,128)} async-done(((f32[768,1536]{1,0:T(8,128)}), f32[96,1536]{1,0:T(8,128)}) %reduce-scatter.11.cloned.1.call-update) | async-done | bytes 589840 | tf_op jit(solution)/shard_map/reduce_scatter | solution.py:192
  (435 shorter events, 147.9 us)
Async XLA Ops:
  7.2 104.1 %copy-start = (bf16[768,1536]{1,0:T(8,128)(2,1)S(1)}, bf16[768,1536]{1,0:T(8,128)(2,1)}, u32[]{:S(2)}) copy-start(bf16[768,1536]{1,0:T(8,128)(2,1)} %param.18) | copy-start | bytes 7077892
  7.2 27.1 %copy-start.5 = (bf16[4,16,16,384]{3,2,1,0:T(8,128)(2,1)S(1)}, bf16[4,16,16,384]{3,2,1,0:T(8,128)(2,1)}, u32[]{:S(2)}) copy-start(bf16[4,16,16,384]{3,2,1,0:T(8,128)(2,1)} %param.13) | copy-start | bytes 2359300
  7.2 101.5 %all-gather.3.cloned.1.call-start = ((), (), s32[]{:S(2)}) async-start(), calls=%async_computation.4 | async-start | bytes 2359296 | tf_op jit(solution)/shard_map/all_gather | solution.py:160
  12.5 47.5 %collective-permute-start.4 = (bf16[114,384]{1,0:T(8,128)(2,1)}, bf16[114,384]{1,0:T(8,128)(2,1)}, u32[]{:S(2)}, u32[]{:S(2)}) collective-permute-start(bf16[114,384]{1,0:T(8,128)(2,1)} %pad_maximum_fusion.6), channel_id=1, source_target_pairs={{2,0},{4,2},{6,4},{8,6},{10,8},{12,10},{14,12},{3,1},{5,3},{7,5},{... | collective-permute-start | bytes 262664 | tf_op jit(solution)/shard_map/ppermute | solution.py:19
  14.4 28.9 %collective-permute-start.3 = (bf16[9,384]{1,0:T(8,128)(2,1)}, bf16[9,384]{1,0:T(8,128)(2,1)}, u32[]{:S(2)}, u32[]{:S(2)}) collective-permute-start(bf16[9,384]{1,0:T(8,128)(2,1)} %reshape.298), channel_id=1, source_target_pairs={{0,6},{2,8},{4,10},{6,12},{8,14},{1,7},{3,9},{5,11},{7,13},{9,15},... | collective-permute-start | bytes 20744 | tf_op jit(solution)/shard_map/ppermute | solution.py:19
  22.6 27.0 %collective-permute-start = (bf16[9,384]{1,0:T(8,128)(2,1)}, bf16[9,384]{1,0:T(8,128)(2,1)}, u32[]{:S(2)}, u32[]{:S(2)}) collective-permute-start(bf16[9,384]{1,0:T(8,128)(2,1)} %reshape.289), channel_id=1, source_target_pairs={{0,10},{2,12},{4,14},{1,11},{3,13},{5,15},{16,26},{18,28},{20,30},... | collective-permute-start | bytes 20744 | tf_op jit(solution)/shard_map/ppermute | solution.py:19
  25.5 30.6 %collective-permute-start.7 = (bf16[9,384]{1,0:T(8,128)(2,1)}, bf16[9,384]{1,0:T(8,128)(2,1)}, u32[]{:S(2)}, u32[]{:S(2)}) collective-permute-start(bf16[9,384]{1,0:T(8,128)(2,1)} %reshape.308), channel_id=1, source_target_pairs={{10,0},{12,2},{14,4},{11,1},{13,3},{15,5},{26,16},{28,18},{30,20},... | collective-permute-start | bytes 20744 | tf_op jit(solution)/shard_map/ppermute | solution.py:19
  27.4 31.3 %collective-permute-start.5 = (bf16[9,384]{1,0:T(8,128)(2,1)}, bf16[9,384]{1,0:T(8,128)(2,1)}, u32[]{:S(2)}, u32[]{:S(2)}) collective-permute-start(bf16[9,384]{1,0:T(8,128)(2,1)} %reshape.303), channel_id=1, source_target_pairs={{6,0},{8,2},{10,4},{12,6},{14,8},{7,1},{9,3},{11,5},{13,7},{15,9},... | collective-permute-start | bytes 20744 | tf_op jit(solution)/shard_map/ppermute | solution.py:19
  43.3 18.2 %collective-permute-start.2 = (bf16[114,384]{1,0:T(8,128)(2,1)}, bf16[114,384]{1,0:T(8,128)(2,1)}, u32[]{:S(2)}, u32[]{:S(2)}) collective-permute-start(bf16[114,384]{1,0:T(8,128)(2,1)} %pad_maximum_fusion.5), channel_id=1, source_target_pairs={{0,2},{2,4},{4,6},{6,8},{8,10},{10,12},{12,14},{1,3},{3,5},{5,7},{... | collective-permute-start | bytes 262664 | tf_op jit(solution)/shard_map/ppermute | solution.py:19
  49.6 13.5 %collective-permute-start.1 = (bf16[114,384]{1,0:T(8,128)(2,1)}, bf16[114,384]{1,0:T(8,128)(2,1)S(1)}, u32[]{:S(2)}, u32[]{:S(2)}) collective-permute-start(bf16[114,384]{1,0:T(8,128)(2,1)} %pad_maximum_fusion.4), channel_id=1, source_target_pairs={{0,8},{2,10},{4,12},{6,14},{1,9},{3,11},{5,13},{7,15},{16,24},{18,... | collective-permute-start | bytes 262664 | tf_op jit(solution)/shard_map/ppermute | solution.py:19
  56.1 12.2 %collective-permute-start.6 = (bf16[114,384]{1,0:T(8,128)(2,1)}, bf16[114,384]{1,0:T(8,128)(2,1)}, u32[]{:S(2)}, u32[]{:S(2)}) collective-permute-start(bf16[114,384]{1,0:T(8,128)(2,1)} %pad_maximum_fusion.7), channel_id=1, source_target_pairs={{8,0},{10,2},{12,4},{14,6},{9,1},{11,3},{13,5},{15,7},{24,16},{26,... | collective-permute-start | bytes 262664 | tf_op jit(solution)/shard_map/ppermute | solution.py:19
  95.3 52.4 %reduce-scatter.13.cloned.1.call-start = ((), (), s32[]{:S(2)}) async-start(), calls=%async_computation.10 | async-start | bytes 2359296
  111.3 19.8 %copy-start.98 = (bf16[768,1536]{1,0:T(8,128)(2,1)S(1)}, bf16[768,1536]{1,0:T(8,128)(2,1)}, u32[]{:S(2)}) copy-start(bf16[768,1536]{1,0:T(8,128)(2,1)} %param.20) | copy-start | bytes 7077892
  137.4 26.9 %all-gather.5.cloned.1.call-start = ((), (), s32[]{:S(2)}) async-start(), calls=%async_computation.5 | async-start | bytes 2359296 | tf_op jit(solution)/shard_map/all_gather | solution.py:187
  153.2 36.1 %reduce-scatter.7.cloned.1.call-start = ((), (), s32[]{:S(2)}) async-start(), calls=%async_computation.6 | async-start | bytes 4718592 | tf_op jit(solution)/shard_map/reduce_scatter | solution.py:219
  177.1 129.6 %all-reduce.3.cloned.1.call-start = ((), (), s32[]{:S(2)}) async-start(), calls=%async_computation.9 | async-start | bytes 172032 | tf_op jit(solution)/shard_map/psum | solution.py:238
  194.3 14.6 %copy-start.2 = (bf16[4,19,22,384]{3,2,1,0:T(8,128)(2,1)S(1)}, bf16[4,19,22,384]{3,2,1,0:T(8,128)(2,1)}, u32[]{:S(2)}) copy-start(bf16[4,19,22,384]{3,2,1,0:T(8,128)(2,1)} %copy-done.1) | copy-start | bytes 3852292
  221.4 175.0 %reduce-scatter.9.cloned.1.call-start = ((), (), s32[]{:S(2)}) async-start(), calls=%async_computation.7 | async-start | bytes 5308416 | tf_op jit(solution)/shard_map/reduce_scatter | solution.py:205
  228.9 266.4 %reduce-scatter.11.cloned.1.call-start = ((), (), s32[]{:S(2)}) async-start(), calls=%async_computation.8 | async-start | bytes 5308416 | tf_op jit(solution)/shard_map/reduce_scatter | solution.py:192
  248.5 60.9 %collective-permute-start.8 = (bf16[114,384]{1,0:T(8,128)(2,1)}, bf16[114,384]{1,0:T(8,128)(2,1)}, u32[]{:S(2)}, u32[]{:S(2)}) collective-permute-start(bf16[114,384]{1,0:T(8,128)(2,1)} %pad_maximum_fusion.8), channel_id=1, source_target_pairs={{0,2},{2,4},{4,6},{6,8},{8,10},{10,12},{12,14},{1,3},{3,5},{5,7},{... | collective-permute-start | bytes 262664 | tf_op jit(solution)/shard_map/ppermute | solution.py:19
  262.6 29.5 %collective-permute-start.12 = (bf16[9,384]{1,0:T(8,128)(2,1)}, bf16[9,384]{1,0:T(8,128)(2,1)}, u32[]{:S(2)}, u32[]{:S(2)}) collective-permute-start(bf16[9,384]{1,0:T(8,128)(2,1)} %reshape.325), channel_id=1, source_target_pairs={{10,0},{12,2},{14,4},{11,1},{13,3},{15,5},{26,16},{28,18},{30,20},... | collective-permute-start | bytes 20744 | tf_op jit(solution)/shard_map/ppermute | solution.py:19
  267.9 26.9 %collective-permute-start.10 = (bf16[9,384]{1,0:T(8,128)(2,1)}, bf16[9,384]{1,0:T(8,128)(2,1)}, u32[]{:S(2)}, u32[]{:S(2)}) collective-permute-start(bf16[9,384]{1,0:T(8,128)(2,1)} %reshape.320), channel_id=1, source_target_pairs={{6,0},{8,2},{10,4},{12,6},{14,8},{7,1},{9,3},{11,5},{13,7},{15,9},... | collective-permute-start | bytes 20744 | tf_op jit(solution)/shard_map/ppermute | solution.py:19
  270.5 26.9 %collective-permute-start.15 = (bf16[9,384]{1,0:T(8,128)(2,1)}, bf16[9,384]{1,0:T(8,128)(2,1)}, u32[]{:S(2)}, u32[]{:S(2)}) collective-permute-start(bf16[9,384]{1,0:T(8,128)(2,1)} %reshape.331), channel_id=1, source_target_pairs={{0,6},{2,8},{4,10},{6,12},{8,14},{1,7},{3,9},{5,11},{7,13},{9,15},... | collective-permute-start | bytes 20744 | tf_op jit(solution)/shard_map/ppermute | solution.py:19
  280.5 24.9 %collective-permute-start.13 = (bf16[9,384]{1,0:T(8,128)(2,1)}, bf16[9,384]{1,0:T(8,128)(2,1)}, u32[]{:S(2)}, u32[]{:S(2)}) collective-permute-start(bf16[9,384]{1,0:T(8,128)(2,1)} %reshape.326), channel_id=1, source_target_pairs={{0,10},{2,12},{4,14},{1,11},{3,13},{5,15},{16,26},{18,28},{20,30},... | collective-permute-start | bytes 20744 | tf_op jit(solution)/shard_map/ppermute | solution.py:19
  290.7 40.1 %copy-start.15 = (bf16[1,3,16,384]{3,2,1,0:T(8,128)(2,1)S(1)}, bf16[1,3,16,384]{3,2,1,0:T(8,128)(2,1)}, u32[]{:S(2)}) copy-start(bf16[1,3,16,384]{3,2,1,0:T(8,128)(2,1)} %get-tuple-element.162) | copy-start | bytes 110596
  290.7 40.9 %copy-start.13 = (bf16[1,3,16,384]{3,2,1,0:T(8,128)(2,1)S(1)}, bf16[1,3,16,384]{3,2,1,0:T(8,128)(2,1)}, u32[]{:S(2)}) copy-start(bf16[1,3,16,384]{3,2,1,0:T(8,128)(2,1)} %get-tuple-element.171) | copy-start | bytes 110596
  290.7 40.9 %copy-start.14 = (bf16[1,3,16,384]{3,2,1,0:T(8,128)(2,1)S(1)}, bf16[1,3,16,384]{3,2,1,0:T(8,128)(2,1)}, u32[]{:S(2)}) copy-start(bf16[1,3,16,384]{3,2,1,0:T(8,128)(2,1)} %get-tuple-element.169) | copy-start | bytes 110596
  290.7 42.7 %copy-start.11 = (bf16[1,16,3,384]{3,2,1,0:T(4,128)(2,1)S(1)}, bf16[1,16,3,384]{3,2,1,0:T(4,128)(2,1)}, u32[]{:S(2)}) copy-start(bf16[1,16,3,384]{3,2,1,0:T(4,128)(2,1)} %get-tuple-element.178) | copy-start | bytes 110596
  290.7 42.7 %copy-start.12 = (bf16[1,16,3,384]{3,2,1,0:T(4,128)(2,1)S(1)}, bf16[1,16,3,384]{3,2,1,0:T(4,128)(2,1)}, u32[]{:S(2)}) copy-start(bf16[1,16,3,384]{3,2,1,0:T(4,128)(2,1)} %get-tuple-element.176) | copy-start | bytes 110596
  292.1 16.1 %collective-permute-start.9 = (bf16[114,384]{1,0:T(8,128)(2,1)}, bf16[114,384]{1,0:T(8,128)(2,1)S(1)}, u32[]{:S(2)}, u32[]{:S(2)}) collective-permute-start(bf16[114,384]{1,0:T(8,128)(2,1)} %pad_maximum_fusion.9), channel_id=1, source_target_pairs={{2,0},{4,2},{6,4},{8,6},{10,8},{12,10},{14,12},{3,1},{5,3},{7,5},{... | collective-permute-start | bytes 262664 | tf_op jit(solution)/shard_map/ppermute | solution.py:19
  294.7 16.9 %collective-permute-start.11 = (bf16[114,384]{1,0:T(8,128)(2,1)}, bf16[114,384]{1,0:T(8,128)(2,1)}, u32[]{:S(2)}, u32[]{:S(2)}) collective-permute-start(bf16[114,384]{1,0:T(8,128)(2,1)} %pad_maximum_fusion.10), channel_id=1, source_target_pairs={{8,0},{10,2},{12,4},{14,6},{9,1},{11,3},{13,5},{15,7},{24,16},{26,... | collective-permute-start | bytes 262664 | tf_op jit(solution)/shard_map/ppermute | solution.py:19
  297.4 23.1 %collective-permute-start.14 = (bf16[114,384]{1,0:T(8,128)(2,1)}, bf16[114,384]{1,0:T(8,128)(2,1)}, u32[]{:S(2)}, u32[]{:S(2)}) collective-permute-start(bf16[114,384]{1,0:T(8,128)(2,1)} %pad_maximum_fusion.11), channel_id=1, source_target_pairs={{0,8},{2,10},{4,12},{6,14},{1,9},{3,11},{5,13},{7,15},{16,24},{18,... | collective-permute-start | bytes 262664 | tf_op jit(solution)/shard_map/ppermute | solution.py:19
  (93 other events, 254.2 us)
Sparse Core Ops, SparseCore 0:
  95.5 13.2 all-gather.2
  137.5 10.2 reduce-scatter.12
  153.3 10.9 all-gather.4
  177.2 12.0 reduce-scatter.6
  221.5 69.9 all-reduce.2
  295.0 101.3 reduce-scatter.8
  400.1 95.1 reduce-scatter.10
where the time goes:
time: 515 us; the launch traced here: 504 us
  waiting for transfers between devices  182 us (35%)
  local copies, waits for them, and re-layouts  109 us (21%)
  other arithmetic  94.9 us (18%)
  starting transfers between devices  51.3 us (10%)
  matrix products  47.5 us (9%)
  between operations  17.4 us (3%)
    reduce_scatter x1, waiting for transfers between devices, on_device(): lax.psum_scatter(lax.dot_general(grad_full, active, (((0,), (0,)), ((), (...  96.9 us
    ppermute x16, starting transfers between devices, shifted(): return lax.ppermute(value, axis, pairs)  50.6 us
    reduce_scatter x1, waiting for transfers between devices, on_device(): lax.psum_scatter(lax.dot_general(normed, pre_grad, (((0,), (0,)), ((), ()...  45.1 us
    another operation x32, local copies, waits for them, and re-layouts, exchange_rims(): stacked = jnp.stack(rim_lists[direction], axis=0)  28.3 us
    reshape x32, local copies, waits for them, and re-layouts, pack_offset(): pieces.append(rim_piece.reshape(-1, chans))  27.9 us
    reduce_sum x4, other arithmetic, kernel_terms(): rows_out.append(jnp.sum(window * grad_values, axis=(0, 1, 2)))  22.2 us
    dot_general x1, matrix products, on_device(): hidden = jnp.dot(normed, w_up, preferred_element_type=jnp.float32) + up_bias  18.2 us
    slice x16, local copies, waits for them, and re-layouts, cut_rim(): return blocks[:, row_lo:row_hi, col_lo:col_hi, :]  15.4 us
  transfers between devices with their start and end apart: 23, of which 6 were waited for; matrix products, arithmetic and copies ran while one was open for 28% of the time, Pallas kernels for 0%

commit v1 on v0

v1 whole, which is shorter than its diff:
```python
import functools
import math

import jax
import jax.numpy as jnp
from jax import lax
from jax.experimental import pallas as pl
from jax.experimental.pallas import tpu as pltpu
from jax.sharding import PartitionSpec as P

KERNEL = 7
RIM = 3
LANES = 128
F32 = jnp.float32
BF16 = jnp.bfloat16
VMEM_BYTES = 60 * 1024 * 1024

TAIL_P = 0.39
TAIL = (
    0.2353252521737435,
    0.0913882086982987,
    0.6495599070595628,
    -0.635400901941762,
    0.8866647490628095,
    -0.2275372167464003,
)
ROOT_HALF = 0.7071067811865476
DENSITY = 0.3989422804014327


def smem():
    return pl.BlockSpec(memory_space=pltpu.SMEM)


def whole(shape):
    return pl.BlockSpec(shape, lambda *_: (0,) * len(shape))


def call(body, grid, ins, outs, shapes, scratch, flops, nbytes, args):
    return pl.pallas_call(
        body,
        grid=grid,
        in_specs=ins,
        out_specs=outs,
        out_shape=shapes,
        scratch_shapes=scratch,
        compiler_params=pltpu.CompilerParams(vmem_limit_bytes=VMEM_BYTES),
        cost_estimate=pl.CostEstimate(flops=flops, bytes_accessed=nbytes, transcendentals=0),
    )(*args)


def phi_pair(h):
    e = jnp.exp(h * h * -0.5)
    den = 1.0 + (TAIL_P * ROOT_HALF) * jnp.abs(h)
    t = pl.reciprocal(den, approx=True)
    t = t * (2.0 - den * t)
    acc = jnp.full_like(h, 0.5 * TAIL[5])
    for coef in TAIL[4::-1]:
        acc = acc * t + 0.5 * coef
    tail = acc * t * e
    return jnp.where(h >= 0, 1.0 - tail, tail), e


def store_rims(odd_row, top, bottom, near_ref, far_ref):
    @pl.when(odd_row == 0)
    def _():
        for side in range(2):
            near_ref[:, side * 16 : side * 16 + 16, :] = bottom[side]
            far_ref[:, side * 16 : side * 16 + 16, :] = top[side]

    @pl.when(odd_row == 1)
    def _():
        for side in range(2):
            near_ref[:, side * 16 : side * 16 + 16, :] = top[side]
            far_ref[:, side * 16 : side * 16 + 16, :] = bottom[side]


def prep_body(info, x_ref, cot_ref, scale_ref, near_ref, far_ref, bg_ref):
    count = info[3]

    def masked(slot, lo, hi):
        return (x_ref[slot, lo:hi].astype(F32) * (slot < count).astype(F32)).astype(BF16)

    store_rims(
        info[1],
        [masked(0, 0, 3), masked(1, 0, 3)],
        [masked(2, 13, 16), masked(3, 13, 16)],
        near_ref,
        far_ref,
    )
    for slot in range(4):
        rows = slice(slot * 256, slot * 256 + 256)
        ok = (slot < count).astype(F32)
        bg_ref[rows, :] = (cot_ref[rows, :].astype(F32) * (ok * scale_ref[...])).astype(BF16)


def side_body(masked, info, x_ref, near_ref, far_ref, a_ref, b_ref, east, west, packed):
    count = info[3]
    odd_row = info[1]
    for slot in range(4):
        value = x_ref[slot].astype(F32)
        if masked:
            value = value * (slot < count).astype(F32)
        rows = slice(RIM + (slot // 2) * 16, RIM + (slot // 2) * 16 + 16)
        if slot % 2:
            east[rows] = value[:, 8:16, :]
        else:
            west[rows] = value[:, 0:8, :]
    near = near_ref[...].astype(F32)
    far = far_ref[...].astype(F32)
    is_odd = (odd_row == 1).astype(F32)
    north = near * is_odd + far * (1.0 - is_odd)
    south = near * (1.0 - is_odd) + far * is_odd
    east[0:3] = north[:, 24:32, :]
    west[0:3] = north[:, 0:8, :]
    east[35:38] = south[:, 24:32, :]
    west[35:38] = south[:, 0:8, :]
    zero = jnp.zeros_like(east[38:40])
    east[38:40] = zero
    west[38:40] = zero

    def pack(out_ref, source, at):
        packed[:, 0:4, :] = source[0:20, at : at + 4, :]
        packed[:, 4:8, :] = source[20:40, at : at + 4, :]
        out_ref[...] = packed[...].reshape(out_ref.shape).astype(BF16)

    @pl.when(info[2] == 0)
    def _():
        pack(a_ref, east, 4)
        pack(b_ref, west, 0)

    @pl.when(info[2] == 1)
    def _():
        pack(a_ref, west, 0)
        pack(b_ref, east, 4)


def conv_body(backward, info, x_ref, near_ref, far_ref, a_ref, b_ref, w_ref, last_ref, out_ref, left_ref, image, weights):
    count = info[3]
    for slot in range(4):
        value = x_ref[slot].astype(F32)
        if not backward:
            value = value * (slot < count).astype(F32)
        r, q = slot // 2, slot % 2
        image[RIM + 16 * r : RIM + 16 * r + 16, 8 + 16 * q : 24 + 16 * q, :] = value
    near = near_ref[...].astype(F32)
    far = far_ref[...].astype(F32)
    is_odd = (info[1] == 1).astype(F32)
    image[0:3, 8:40, :] = near * is_odd + far * (1.0 - is_odd)
    image[35:38, 8:40, :] = near * (1.0 - is_odd) + far * is_odd
    first = a_ref[...].astype(F32).reshape(20, 8, LANES)
    second = b_ref[...].astype(F32).reshape(20, 8, LANES)
    odd_col = (info[2] == 1).astype(F32)
    from_left = first * odd_col + second * (1.0 - odd_col)
    from_right = first * (1.0 - odd_col) + second * odd_col
    image[20:40, 0:8, :] = from_left
    image[0:20, 4:8, :] = from_left[:, 0:4, :]
    image[0:20, 40:48, :] = from_right
    image[20:40, 40:44, :] = from_right[:, 4:8, :]

    for b in range(KERNEL):
        value = image[0:38, 5 + b : 37 + b, :].astype(BF16).reshape(19, 2, 32, LANES)
        for par in range(2):
            at = b * 256 + par * LANES
            left_ref[0, :, at : at + LANES] = value[:, par].reshape(608, LANES)

    eye = lax.broadcasted_iota(jnp.int32, (LANES, LANES), 0) == lax.broadcasted_iota(
        jnp.int32, (LANES, LANES), 1
    )
    empty = jnp.zeros((LANES, LANES), BF16)
    for a in range(-1, KERNEL + 1):
        for b in range(KERNEL):
            if 0 <= a < KERNEL:
                tap = (KERNEL - 1 - a) * KERNEL + KERNEL - 1 - b if backward else a * KERNEL + b
                block = jnp.where(eye, w_ref[tap : tap + 1, :], 0.0).astype(BF16)
            else:
                block = empty
            for o in range(2):
                r = a + o
                if 0 <= r < 8:
                    at = (r // 2) * 1792 + b * 256 + (r % 2) * LANES
                    weights[at : at + LANES, o * LANES : (o + 1) * LANES] = block
    acc = None
    for q in range(4):
        term = jnp.dot(
            left_ref[0, 32 * q : 32 * q + 512, :],
            weights[1792 * q : 1792 * (q + 1), :],
            preferred_element_type=F32,
        )
        acc = term if acc is None else acc + term
    acc = acc.reshape(16, 32, 256)
    for slot in range(4):
        r, q = slot // 2, slot % 2
        for o in range(2):
            value = acc[8 * r : 8 * r + 8, 16 * q : 16 * q + 16, o * LANES : (o + 1) * LANES]
            if backward:
                value = (value + last_ref[slot, :, o].astype(F32)) * (slot < count).astype(F32)
            else:
                value = value + last_ref[...].reshape(1, 1, LANES)
            out_ref[slot, :, o] = value.astype(BF16)


def taps_body(g_ref, left_ref, out_ref, paired):
    for slot in range(4):
        r, q = slot // 2, slot % 2
        for o in range(2):
            paired[8 * r : 8 * r + 8, 16 * q : 16 * q + 16, o * LANES : (o + 1) * LANES] = g_ref[slot, :, o].astype(F32)
    turned = paired[...].reshape(512, 256).T.astype(BF16)
    eye = lax.broadcasted_iota(jnp.int32, (LANES, LANES), 0) == lax.broadcasted_iota(
        jnp.int32, (LANES, LANES), 1
    )
    sums = {}
    for q in range(4):
        prod = jnp.dot(turned, left_ref[0, 32 * q : 32 * q + 512, :], preferred_element_type=F32)
        for b in range(KERNEL):
            for par in range(2):
                for o in range(2):
                    a = 2 * q + par - o
                    if 0 <= a < KERNEL:
                        block = prod[o * LANES : (o + 1) * LANES, b * 256 + par * LANES : b * 256 + (par + 1) * LANES]
                        row = jnp.sum(jnp.where(eye, block, 0.0), axis=0, keepdims=True)
                        key = a * KERNEL + b
                        if key in sums:
                            out_ref[key : key + 1, :] = sums.pop(key) + row
                        else:
                            sums[key] = row
    out_ref[49:56, :] = jnp.zeros((7, LANES), F32)


def pick(second, own, other):
    s = second.astype(F32)
    own = own.astype(F32)
    other = other.astype(F32)
    low = own * (1.0 - s) + other * s
    high = own * s + other * (1.0 - s)
    return jnp.concatenate([low, high], axis=1)


def grad_in_body(info, own_ref, other_ref, w_ref, out_ref, turned_ref):
    full = pick(info[0] == 1, own_ref[...], other_ref[...])
    turned_ref[...] = full.T.astype(BF16)
    out_ref[...] = jnp.dot(full.astype(BF16), w_ref[...], preferred_element_type=F32)


def mlp_body(
    info, own_ref, other_ref, gain_ref, shift_ref, up_ref, bias_ref, down_ref, in_ref,
    turned_ref, act_ref, pre_ref, keep_ref, send_ref, sums_ref, bkeep_ref, bsend_ref,
):
    second = info[0] == 1
    rows = pick(second, own_ref[...], other_ref[...])
    mean = jnp.mean(rows, axis=1, keepdims=True)
    centered = rows - mean
    var = jnp.mean(centered * centered, axis=1, keepdims=True)
    normalized = centered * lax.rsqrt(var + 1e-06)
    value = normalized * gain_ref[...] + shift_ref[...]
    turned_ref[...] = value.T.astype(BF16)
    normed = value.astype(BF16)
    units = up_ref.shape[1]
    step = 512
    back = None
    branch = None
    dims = (((1,), (1,)), ((), ()))
    for at in range(0, units, step):
        cols = slice(at, at + step)
        hidden = jnp.dot(normed, up_ref[:, cols], preferred_element_type=F32) + bias_ref[:, cols]
        phi, e = phi_pair(hidden)
        active = (hidden * phi).astype(BF16)
        act_ref[:, cols] = active
        pre = (in_ref[:, cols] * (phi + hidden * (e * DENSITY))).astype(BF16)
        pre_ref[:, cols] = pre
        one = lax.dot_general(pre, up_ref[:, cols], dims, preferred_element_type=F32)
        two = lax.dot_general(active, down_ref[:, cols], dims, preferred_element_type=F32)
        back = one if back is None else back + one
        branch = two if branch is None else branch + two
    scaled = back * gain_ref[...]
    first = jnp.sum(scaled, axis=1, keepdims=True)
    other = jnp.sum(scaled * normalized, axis=1, keepdims=True)
    lane = lax.broadcasted_iota(jnp.int32, sums_ref.shape, 1)
    sums_ref[...] = jnp.where(lane == 0, first, other)
    half = keep_ref.shape[1]
    s = second.astype(F32)

    def split(value):
        low, high = value[:, :half], value[:, half:]
        return low * (1.0 - s) + high * s, low * s + high * (1.0 - s)

    keep, send = split(back)
    keep_ref[...] = keep
    send_ref[...] = send.astype(BF16)
    keep, send = split(branch)
    bkeep_ref[...] = keep
    bsend_ref[...] = send.astype(BF16)


def outer_body(left_ref, right_ref, out_ref):
    out_ref[...] = jnp.dot(left_ref[...], right_ref[...], preferred_element_type=F32).astype(BF16)


def norm_back_body(info, own_ref, other_ref, keep_ref, got_ref, mine_ref, sums_ref, gain_ref, out_ref, near_ref, far_ref):
    own = own_ref[...].astype(F32)
    other = other_ref[...].astype(F32)
    total = 2.0 * own.shape[1]
    mean = (jnp.sum(own, axis=1, keepdims=True) + jnp.sum(other, axis=1, keepdims=True)) / total
    own = own - mean
    other = other - mean
    var = (jnp.sum(own * own, axis=1, keepdims=True) + jnp.sum(other * other, axis=1, keepdims=True)) / total
    inverse = lax.rsqrt(var + 1e-06)
    normalized = own * inverse
    scaled = (keep_ref[...] + got_ref[...].astype(F32)) * gain_ref[...]
    both = (mine_ref[...] + sums_ref[...]) / total
    grad = inverse * (scaled - both[:, 0:1] - normalized * both[:, 1:2])
    out_ref[...] = grad.astype(BF16)
    tile = grad.reshape(16, 16, grad.shape[1])
    odd_row = info[1]
    slot = pl.program_id(0)
    for side in range(2):
        cols = slice(side * 16, side * 16 + 16)

        @pl.when(slot == side)
        def _():
            top = tile[0:3].astype(BF16)

            @pl.when(odd_row == 0)
            def _():
                far_ref[:, cols, :] = top

            @pl.when(odd_row == 1)
            def _():
                near_ref[:, cols, :] = top

        @pl.when(slot == side + 2)
        def _():
            bottom = tile[13:16].astype(BF16)

            @pl.when(odd_row == 0)
            def _():
                near_ref[:, cols, :] = bottom

            @pl.when(odd_row == 1)
            def _():
                far_ref[:, cols, :] = bottom


def on_device(
    features, dw_kernel, dw_bias, ln_gain, ln_bias, w_up, up_bias, w_down, down_bias, layer_scale,
    cotangent, neighbors, tissue_count,
):
    tiles_dev, side, _, chans = features.shape
    units = w_up.shape[1]
    cells = tiles_dev * side * side
    devices = lax.axis_size("space")
    me = lax.axis_index("space")
    tensor_index = lax.axis_index("tensor")
    block_rows = max(d for d in range(1, math.isqrt(devices) + 1) if devices % d == 0)
    block_cols = devices // block_rows
    count = lax.dynamic_index_in_dim(tissue_count, me, 0, keepdims=False)
    info = jnp.stack([tensor_index, (me // block_cols) % 2, (me % block_cols) % 2, count]).astype(jnp.int32)
    blocks = chans // LANES

    def sds(shape, dtype):
        return jax.ShapeDtypeStruct(shape, dtype)

    def across(value):
        return lax.ppermute(value, "tensor", [(0, 1), (1, 0)])

    def paired(value, along_rows, round_at):
        size = block_rows if along_rows else block_cols
        pairs = []
        for d in range(devices):
            place = d // block_cols if along_rows else d % block_cols
            other = place + 1 if place % 2 == round_at else place - 1
            if 0 <= other < size:
                pairs.append((d, d + (other - place) * (block_cols if along_rows else 1)))
        if not pairs:
            return jnp.zeros_like(value)
        return lax.ppermute(value, "space", pairs)

    rim_shape = (RIM, 2 * side, chans)
    pack_shape = (160, chans)

    def sides(x, near, far, masked):
        return call(
            functools.partial(side_body, masked),
            (1,),
            [smem(), whole(features.shape), whole(rim_shape), whole(rim_shape)],
            [whole(pack_shape)] * 2,
            [sds(pack_shape, BF16)] * 2,
            [pltpu.VMEM((40, 8, chans), F32), pltpu.VMEM((40, 8, chans), F32), pltpu.VMEM((20, 8, chans), F32)],
            1000000, 2000000, (info, x, near, far),
        )

    split_shape = (4, 8, 2, side, chans)
    split_spec = pl.BlockSpec((4, 8, 2, side, LANES), lambda c: (0, 0, 0, 0, c))

    def conv(x, near, far, one, two, last, backward):
        if backward:
            last_spec = split_spec
        else:
            last_spec = pl.BlockSpec((1, LANES), lambda c: (0, c))
        rim_spec = pl.BlockSpec((RIM, 2 * side, LANES), lambda c: (0, 0, c))
        pack_spec = pl.BlockSpec((160, LANES), lambda c: (0, c))
        outs = [split_spec]
        shapes = [sds(split_shape, BF16)]
        scratch = [pltpu.VMEM((40, 48, LANES), F32), pltpu.VMEM((4 * 1792, 256), BF16)]
        if backward:
            scratch = [pltpu.VMEM((1, 608, 1792), BF16)] + scratch
        else:
            outs.append(pl.BlockSpec((1, 608, 1792), lambda c: (c, 0, 0)))
            shapes.append(sds((blocks, 608, 1792), BF16))
        return call(
            functools.partial(conv_body, backward),
            (blocks,),
            [
                smem(),
                pl.BlockSpec((4, side, side, LANES), lambda c: (0, 0, 0, c)),
                rim_spec, rim_spec, pack_spec, pack_spec,
                pl.BlockSpec((KERNEL * KERNEL, LANES), lambda c: (0, c)),
                last_spec,
            ],
            outs, shapes, scratch,
            5600000000, 10000000, (info, x, near, far, one, two, dw_kernel, last),
        )

    near_send, far_send, branch_grad = call(
        prep_body,
        (1,),
        [smem(), whole(features.shape), whole((cells, chans)), whole((1, chans))],
        [whole(rim_shape), whole(rim_shape), whole((cells, chans))],
        [sds(rim_shape, BF16), sds(rim_shape, BF16), sds((cells, chans), BF16)],
        [], 1000000, 3000000,
        (info, features, cotangent.reshape(cells, chans), layer_scale.reshape(1, chans)),
    )
    near = paired(near_send, True, 0)
    far = paired(far_send, True, 1)
    other_grad = across(branch_grad)
    one_send, two_send = sides(features, near, far, True)
    one = paired(one_send, False, 0)
    two = paired(two_send, False, 1)

    row_block = pl.BlockSpec((256, chans), lambda i: (i, 0))
    unit_rows = pl.BlockSpec((256, units), lambda i: (i, 0))
    turned_spec = pl.BlockSpec((2 * chans, 256), lambda i: (0, i))
    weight_spec = whole((2 * chans, units))
    act_grad, grad_turned = call(
        grad_in_body,
        (tiles_dev,),
        [smem(), row_block, row_block, weight_spec],
        [unit_rows, turned_spec],
        [sds((cells, units), F32), sds((2 * chans, cells), BF16)],
        [], 2400000000, 12000000, (info, branch_grad, other_grad, w_down),
    )

    conv_out, left = conv(features, near, far, one, two, dw_bias.reshape(1, chans), False)
    conv_own = conv_out.reshape(cells, chans)
    conv_other = across(conv_own)

    gain_row = ln_gain.reshape(1, 2 * chans)
    full_row = whole((1, 2 * chans))
    normed_turned, active, pre_grad, back_keep, back_send, sums, branch_keep, branch_send = call(
        mlp_body,
        (tiles_dev,),
        [smem(), row_block, row_block, full_row, full_row, weight_spec, whole((1, units)), weight_spec, unit_rows],
        [turned_spec, unit_rows, unit_rows, row_block, row_block, pl.BlockSpec((256, LANES), lambda i: (i, 0)), row_block, row_block],
        [
            sds((2 * chans, cells), BF16), sds((cells, units), BF16), sds((cells, units), BF16),
            sds((cells, chans), F32), sds((cells, chans), BF16), sds((cells, LANES), F32),
            sds((cells, chans), F32), sds((cells, chans), BF16),
        ],
        [], 7200000000, 25000000,
        (info, conv_own, conv_other, gain_row, ln_bias.reshape(1, 2 * chans), w_up, up_bias.reshape(1, units), w_down, act_grad),
    )
    back_got = across(back_send)
    sums_got = across(sums)
    branch_got = across(branch_send)

    def outer(turned, right):
        return call(
            outer_body,
            (3,),
            [whole((2 * chans, cells)), pl.BlockSpec((cells, units // 3), lambda i: (0, i))],
            pl.BlockSpec((2 * chans, units // 3), lambda i: (0, i)),
            sds((2 * chans, units), BF16),
            [], 2400000000, 8000000, (turned, right),
        )

    grad_scale = lax.rsqrt(F32(side * side) * jnp.sum(tissue_count).astype(F32))

    def scattered(value):
        if devices & (devices - 1):
            return lax.psum_scatter(value.astype(F32), "space", scatter_dimension=0, tiled=True) * grad_scale
        value = value.reshape(devices, -1, units)
        bit = 1
        while bit < devices:
            halves = value.reshape(-1, 2, *value.shape[1:])
            high = (me // bit) % 2 == 1
            send = jnp.where(high, halves[:, 0], halves[:, 1])
            keep = jnp.where(high, halves[:, 1], halves[:, 0])
            got = lax.ppermute(send, "space", [(d, d ^ bit) for d in range(devices)])
            value = keep.astype(F32) + got.astype(F32)
            bit *= 2
            if bit < devices:
                value = value.astype(BF16)
        return value.reshape(-1, units) * grad_scale

    grad_down = scattered(outer(grad_turned, active))
    grad_up = scattered(outer(normed_turned, pre_grad))

    my_gain = lax.dynamic_slice_in_dim(gain_row, tensor_index * chans, chans, 1)
    sums_spec = pl.BlockSpec((256, LANES), lambda i: (i, 0))
    conv_grad, near_send, far_send = call(
        norm_back_body,
        (tiles_dev,),
        [smem(), row_block, row_block, row_block, row_block, sums_spec, sums_spec, whole((1, chans))],
        [row_block, whole(rim_shape), whole(rim_shape)],
        [sds((cells, chans), BF16), sds(rim_shape, BF16), sds(rim_shape, BF16)],
        [], 10000000, 6000000,
        (info, conv_own, conv_other, back_keep, back_got, sums, sums_got, my_gain),
    )
    near = paired(near_send, True, 0)
    far = paired(far_send, True, 1)
    conv_grad_tiles = conv_grad.reshape(features.shape)
    one_send, two_send = sides(conv_grad_tiles, near, far, False)
    one = paired(one_send, False, 0)
    two = paired(two_send, False, 1)
    taps = call(
        taps_body,
        (blocks,),
        [split_spec, pl.BlockSpec((1, 608, 1792), lambda c: (c, 0, 0))],
        pl.BlockSpec((56, LANES), lambda c: (0, c)),
        sds((56, chans), F32),
        [pltpu.VMEM((16, 32, 256), F32)], 5600000000, 9000000,
        (conv_grad.reshape(split_shape), left),
    )
    if devices & (devices - 1):
        taps = lax.psum(taps, "space")
    else:
        bit = 1
        while bit < devices:
            taps = taps + lax.ppermute(taps, "space", [(d, d ^ bit) for d in range(devices)])
            bit *= 2
    grad_kernel = taps[: KERNEL * KERNEL] * grad_scale

    tile_ok = (jnp.arange(tiles_dev, dtype=jnp.int32) < count).astype(F32)
    row_ok = jnp.repeat(tile_ok, side * side)[:, None]
    branch = branch_keep + branch_got.astype(F32) + down_bias
    block_out = ((features.reshape(cells, chans).astype(F32) + layer_scale * branch) * row_ok).astype(BF16)
    block_out = block_out.reshape(features.shape)

    (grad_features,) = conv(
        conv_grad_tiles, near, far, one, two, cotangent.reshape(split_shape), True
    )
    grad_features = grad_features.reshape(features.shape)
    return (block_out, grad_features, grad_up, grad_down, grad_kernel)


def solution(mesh):
    return jax.shard_map(
        on_device,
        mesh=mesh,
        in_specs=(
            P(("slide", "space"), None, None, "tensor"),
            P(None, "tensor"),
            P("tensor"),
            P(),
            P(),
            P(None, "tensor"),
            P("tensor"),
            P(None, "tensor"),
            P("tensor"),
            P("tensor"),
            P(("slide", "space"), None, None, "tensor"),
            P("slide", None),
            P("slide"),
        ),
        out_specs=(
            P(("slide", "space"), None, None, "tensor"),
            P(("slide", "space"), None, None, "tensor"),
            P(("slide", "space"), "tensor"),
            P(("slide", "space"), "tensor"),
            P("slide", "tensor"),
        ),
        check_vma=False,
    )
```

time: 515 us -> 202 us (0.39); the launches traced: 504 us -> 201 us
  waiting for transfers between devices: 182 us -> 62.2 us
  local copies, waits for them, and re-layouts: 109 us -> 10.4 us
  other arithmetic: 94.9 us -> 16.5 us
  Pallas kernels: 0 us -> 77.1 us
  matrix products: 47.5 us -> 0 us
  starting transfers between devices: 51.3 us -> 33.3 us
  between operations: 17.4 us -> 1.6 us
    reduce_scatter x3 -> x0, waiting for transfers between devices: 150 us -> none  [the longest x1 96.9 us: on_device(): lax.psum_scatter(lax.dot_general(grad_full, active, (((0,), (0,)), ((), (...]
    pallas_call x0 -> x11, Pallas kernels: none -> 77.1 us  [call(): pl.pallas_call(body, grid=grid, in_specs=ins, out_specs=outs, out_shape=s...]
    ppermute x16 -> x20, waiting for transfers between devices: 0.04 us -> 62.2 us  [the longest x6 37.6 us: scattered(): got = lax.ppermute(send, 'space', [(d, d ^ bit) for d in range(devices)])]
    dot_general x6 -> x0, matrix products: 47.5 us -> none  [the longest x1 18.2 us: on_device(): hidden = jnp.dot(normed, w_up, preferred_element_type=jnp.float32) + up_bias]
    slice x36 -> x0, local copies, waits for them, and re-layouts: 35.6 us -> none  [the longest x16 15.4 us: cut_rim(): return blocks[:, row_lo:row_hi, col_lo:col_hi, :]]
    another operation x82 -> x2, local copies, waits for them, and re-layouts: 32.8 us -> 0.73 us  [the longest x32 28.3 us: exchange_rims(): stacked = jnp.stack(rim_lists[direction], axis=0)]
    reduce_sum x8 -> x1, other arithmetic: 27.5 us -> 0.63 us  [on_device(): grad_scale = lax.rsqrt(F32(side * side) * jnp.sum(tissue_count).astype(F32))]
    reshape x32 -> x4, local copies, waits for them, and re-layouts: 27.9 us -> 2.35 us  [the longest x1 0.6 us: on_device(): up_bias.reshape(1, units)]
  transfers between devices with their start and end apart: 23 -> 20, of which waited for: 6 -> 8; matrix products, arithmetic and copies ran while one was open for 28% -> 9% of each run, Pallas kernels for 0% -> 27%
where the time goes in v1:
time: 202 us; the launch traced here: 201 us
  Pallas kernels  77.1 us (38%)
  waiting for transfers between devices  62.2 us (31%)
  starting transfers between devices  33.3 us (16%)
  other arithmetic  16.5 us (8%)
  local copies, waits for them, and re-layouts  10.4 us (5%)
    pallas_call x11, Pallas kernels, call(): pl.pallas_call(body, grid=grid, in_specs=ins, out_specs=outs, out_shape=s...  77.1 us
    ppermute x6, waiting for transfers between devices, scattered(): got = lax.ppermute(send, 'space', [(d, d ^ bit) for d in range(devices)])  37.6 us
    ppermute x6, waiting for transfers between devices, paired(): return lax.ppermute(value, 'space', pairs)  22.8 us
    ppermute x6, starting transfers between devices, scattered(): got = lax.ppermute(send, 'space', [(d, d ^ bit) for d in range(devices)])  14.6 us
    ppermute x6, starting transfers between devices, paired(): return lax.ppermute(value, 'space', pairs)  14.6 us
    unnamed x36, local copies, waits for them, and re-layouts  4.25 us
    select_n x6, other arithmetic, scattered(): send = jnp.where(high, halves[:, 0], halves[:, 1])  4.17 us
    convert_element_type x2, other arithmetic, scattered(): value = value.astype(BF16)  4.13 us
  transfers between devices with their start and end apart: 20, of which 8 were waited for; matrix products, arithmetic and copies ran while one was open for 9% of the time, Pallas kernels for 27%

profile of v1, /device:TPU:0, one launch (start us, length us, event | category | flops | bytes accessed | tf_op | source)
XLA Modules:
  0.0 201.1 jit_solution(2535763721289624689)
XLA Ops:
  4.4 2.4 %shard_map.155 = (bf16[3,32,384]{2,1,0:T(8,128)(2,1)}, bf16[3,32,384]{2,1,0:T(8,128)(2,1)}, bf16[1024,384]{1,0:T(8,128)(2,1)}) custom-call(s32[4]{0:T(128)} %pad_add_fusion.info, bf16[4,16,16,384]{3,2,1,0:T(8,128)(2,1)} %x_ref.5, bf16[1024,384]{1,0:T(8,128)(2,1)} %bitcast.122, f32[1,384]{1,0:T(1,128)} %broadcast_in_dim.7.scale_ref), custom_call_target="tpu_custom_call" | custom-call | flops 1000000 | bytes 3000000 | tf_op jit(solution)/shard_map/pallas_call | solution.py:40
  6.9 4.0 %collective-permute-start = (bf16[3,32,384]{2,1,0:T(8,128)(2,1)}, bf16[3,32,384]{2,1,0:T(8,128)(2,1)S(1)}, u32[]{:S(2)}, u32[]{:S(2)}) collective-permute-start(bf16[3,32,384]{2,1,0:T(8,128)(2,1)} %get-tuple-element.25), channel_id=1, source_target_pairs={{0,8},{2,10},{4,12},{6,14},{8,0},{10,2},{12,4},{14,6},{1,9},{3,11}... | collective-permute-start | bytes 221192 | tf_op jit(solution)/shard_map/ppermute | solution.py:376
  10.9 4.1 %collective-permute-done.near_ref = bf16[3,32,384]{2,1,0:T(8,128)(2,1)S(1)} collective-permute-done((bf16[3,32,384]{2,1,0:T(8,128)(2,1)}, bf16[3,32,384]{2,1,0:T(8,128)(2,1)S(1)}, u32[]{:S(2)}, u32[]{:S(2)}) %collective-permute-start) | collective-permute-done | bytes 73760 | tf_op jit(solution)/shard_map/ppermute | solution.py:376
  15.7 2.1 %shard_map.156 = (bf16[160,384]{1,0:T(8,128)(2,1)}, bf16[160,384]{1,0:T(8,128)(2,1)}) custom-call(s32[4]{0:T(128)} %pad_add_fusion.info, bf16[4,16,16,384]{3,2,1,0:T(8,128)(2,1)} %x_ref.5, bf16[3,32,384]{2,1,0:T(8,128)(2,1)} %copy-done.6, bf16[3,32,384]{2,1,0:T(8,128)(2,1)} %broadcast_1_far_ref.2.far_ref), custom_call_target="tpu_custom_call" | custom-call | flops 1000000 | bytes 2000000 | tf_op jit(solution)/shard_map/pallas_call | solution.py:40
  17.8 1.7 collective-permute-start.1
  20.9 2.7 %collective-permute-done.1.a_ref = bf16[160,384]{1,0:T(8,128)(2,1)S(1)} collective-permute-done((bf16[160,384]{1,0:T(8,128)(2,1)}, bf16[160,384]{1,0:T(8,128)(2,1)S(1)}, u32[]{:S(2)}, u32[]{:S(2)}) %collective-permute-start.1) | collective-permute-done | bytes 122912 | tf_op jit(solution)/shard_map/ppermute | solution.py:376
  24.9 9.3 %shard_map.157 = (bf16[4,8,2,16,384]{4,3,2,1,0:T(8,128)(2,1)}, bf16[3,608,1792]{2,1,0:T(8,128)(2,1)}) custom-call(s32[4]{0:T(128)} %pad_add_fusion.info, bf16[4,16,16,384]{3,2,1,0:T(8,128)(2,1)} %x_ref.5, bf16[3,32,384]{2,1,0:T(8,128)(2,1)} %copy-done.6, bf16[3,32,384]{2,1,0:T(8,128)(2,1)} %broadcast_1_far_ref.2.far_ref, bf16[160,384]{1,0:T(8,128)(2,1)} %copy-done.14, ...), custom_call_target="tpu_custom_call" | custom-call | flops 5600000000 | bytes 10000000 | tf_op jit(solution)/shard_map/pallas_call | solution.py:40
  39.5 7.3 %shard_map.158 = (f32[1024,1536]{1,0:T(8,128)}, bf16[768,1024]{1,0:T(8,128)(2,1)}) custom-call(s32[4]{0:T(128)} %pad_add_fusion.info, bf16[1024,384]{1,0:T(8,128)(2,1)} %get-tuple-element.29.own_ref, bf16[1024,384]{1,0:T(8,128)(2,1)} %copy-done.13, bf16[768,1536]{1,0:T(8,128)(2,1)} %down_ref.1), custom_call_target="tpu_custom_call" | custom-call | flops 2400000000 | bytes 12000000 | tf_op jit(solution)/shard_map/pallas_call | solution.py:40
  47.6 18.6 %shard_map.159 = (bf16[768,1024]{1,0:T(8,128)(2,1)}, bf16[1024,1536]{1,0:T(8,128)(2,1)}, bf16[1024,1536]{1,0:T(8,128)(2,1)}, f32[1024,384]{1,0:T(8,128)}, bf16[1...) custom-call(s32[4]{0:T(128)} %pad_add_fusion.info, ...), custom_call_target="tpu_custom_call" | custom-call | flops 7200000000 | bytes 25000000 | tf_op jit(solution)/shard_map/pallas_call | solution.py:40
  66.9 6.2 %shard_map.164 = bf16[768,1536]{1,0:T(8,128)(2,1)} custom-call(bf16[768,1024]{1,0:T(8,128)(2,1)} %get-tuple-element.42.left_ref, bf16[1024,1536]{1,0:T(8,128)(2,1)} %get-tuple-element.43.right_ref), custom_call_target="tpu_custom_call" | custom-call | flops 2400000000 | bytes 8000000 | tf_op jit(solution)/shard_map/pallas_call | solution.py:40
  73.1 2.8 %select_bitcast_fusion = bf16[4,96,1536]{2,1,0:T(8,128)(2,1)} fusion(pred[]{:T(512)S(6)} %eq.24, bf16[4,2,96,1536]{3,2,1,0:T(8,128)(2,1)} %bitcast.117), kind=kLoop, calls=%fused_computation.15 | loop fusion | flops 589824 | bytes 3538945 | tf_op jit(solution)/shard_map/jit(_where)/select_n | solution.py:496
  75.8 3.5 %collective-permute-start.14 = (bf16[4,96,1536]{2,1,0:T(8,128)(2,1)}, bf16[4,96,1536]{2,1,0:T(8,128)(2,1)}, u32[]{:S(2)}, u32[]{:S(2)}) collective-permute-start(bf16[4,96,1536]{2,1,0:T(8,128)(2,1)} %select_bitcast_fusion), channel_id=1, source_target_pairs={{0,2},{2,0},{4,6},{6,4},{8,10},{10,8},{12,14},{14,12},{1,3},{3,1},... | collective-permute-start | bytes 3538952 | tf_op jit(solution)/shard_map/ppermute | solution.py:498
  79.5 6.1 %shard_map.163 = bf16[768,1536]{1,0:T(8,128)(2,1)} custom-call(bf16[768,1024]{1,0:T(8,128)(2,1)} %get-tuple-element.40.left_ref, bf16[1024,1536]{1,0:T(8,128)(2,1)} %get-tuple-element.41.right_ref), custom_call_target="tpu_custom_call" | custom-call | flops 2400000000 | bytes 8000000 | tf_op jit(solution)/shard_map/pallas_call | solution.py:40
  86.7 5.1 %shard_map.160 = (bf16[1024,384]{1,0:T(8,128)(2,1)}, bf16[3,32,384]{2,1,0:T(8,128)(2,1)}, bf16[3,32,384]{2,1,0:T(8,128)(2,1)}) custom-call(s32[4]{0:T(128)} %pad_add_fusion.info, bf16[1024,384]{1,0:T(8,128)(2,1)} %bitcast.121, bf16[1024,384]{1,0:T(8,128)(2,1)} %copy-done.2, f32[1024,384]{1,0:T(8,128)} %get-tuple-element.33.keep_ref, ...), custom_call_target="tpu_custom_call" | custom-call | flops 10000000 | bytes 6000000 | tf_op jit(solution)/shard_map/pallas_call | solution.py:40
  91.8 8.9 %shard_map.165 = f32[56,384]{1,0:T(8,128)} custom-call(bf16[4,8,2,16,384]{4,3,2,1,0:T(8,128)(2,1)} %bitcast.124, bf16[3,608,1792]{2,1,0:T(8,128)(2,1)} %get-tuple-element.44.left_ref), custom_call_target="tpu_custom_call" | custom-call | flops 5600000000 | bytes 9000000 | tf_op jit(solution)/shard_map/pallas_call | solution.py:40
  101.0 2.2 %collective-permute-start.8 = (bf16[3,32,384]{2,1,0:T(8,128)(2,1)}, bf16[3,32,384]{2,1,0:T(8,128)(2,1)}, u32[]{:S(2)}, u32[]{:S(2)}) collective-permute-start(bf16[3,32,384]{2,1,0:T(8,128)(2,1)} %get-tuple-element.37), channel_id=1, source_target_pairs={{0,8},{2,10},{4,12},{6,14},{8,0},{10,2},{12,4},{14,6},{1,9},{3,11}... | collective-permute-start | bytes 221192 | tf_op jit(solution)/shard_map/ppermute | solution.py:376
  104.4 1.8 collective-permute-start.11
  106.5 2.2 %shard_map.161 = (bf16[160,384]{1,0:T(8,128)(2,1)}, bf16[160,384]{1,0:T(8,128)(2,1)}) custom-call(s32[4]{0:T(128)} %pad_add_fusion.info, bf16[4,16,16,384]{3,2,1,0:T(8,128)(2,1)} %bitcast.125, bf16[3,32,384]{2,1,0:T(8,128)(2,1)} %collective-permute-done.8.near_ref, bf16[3,32,384]{2,1,0:T(8,128)(2,1)} %broadcast_1_far_ref.2.far_ref), custom_call_target="tpu_custom_call" | custom-call | flops 1000000 | bytes 2000000 | tf_op jit(solution)/shard_map/pallas_call | solution.py:40
  110.1 4.6 %collective-permute-start.9 = (bf16[160,384]{1,0:T(8,128)(2,1)}, bf16[160,384]{1,0:T(8,128)(2,1)}, u32[]{:S(2)}, u32[]{:S(2)}) collective-permute-start(bf16[160,384]{1,0:T(8,128)(2,1)} %get-tuple-element.38), channel_id=1, source_target_pairs={{0,2},{2,0},{4,6},{6,4},{8,10},{10,8},{12,14},{14,12},{1,3},{3,1},... | collective-permute-start | bytes 368648 | tf_op jit(solution)/shard_map/ppermute | solution.py:376
  115.6 2.7 %fusion.3 = bf16[1024,384]{1,0:T(8,128)(2,1)} fusion(f32[1024,384]{1,0:T(8,128)} %get-tuple-element.31, bf16[1024,384]{1,0:T(8,128)(2,1)S(1)} %collective-permute-done.5, bf16[4,16,16,384]{3,2,1,0:T(8,128)(2,1)S(1)} %copy-done.1, f32[1024]{0:T(1024)S(1)} %bitcast.128, f32[384]{0:T(512)S(1)} %copy-done.11, f32[384]{0:T(512)S(1)} %copy-done.8), kind=kLoop, calls=%fused_computation.6 | loop fusion | flops 3145728 | bytes 3939328 | tf_op jit(solution)/shard_map/convert_element_type | solution.py:546
  118.3 1.8 collective-permute-done.18
  120.1 2.2 %collective-permute-start.19 = (f32[56,384]{1,0:T(8,128)S(1)}, f32[56,384]{1,0:T(8,128)S(1)}, u32[]{:S(2)}, u32[]{:S(2)}) collective-permute-start(f32[56,384]{1,0:T(8,128)S(1)} %add.89), channel_id=1, source_target_pairs={{0,8},{2,10},{4,12},{6,14},{8,0},{10,2},{12,4},{14,6},{1,9},{3,11}... | collective-permute-start | bytes 258056 | tf_op jit(solution)/shard_map/ppermute | solution.py:539
  122.3 15.6 %collective-permute-done.9.a_ref = bf16[160,384]{1,0:T(8,128)(2,1)} collective-permute-done((bf16[160,384]{1,0:T(8,128)(2,1)}, bf16[160,384]{1,0:T(8,128)(2,1)}, u32[]{:S(2)}, u32[]{:S(2)}) %collective-permute-start.9) | collective-permute-done | bytes 122912 | tf_op jit(solution)/shard_map/ppermute | solution.py:376
  137.8 8.9 %shard_map.162 = bf16[4,8,2,16,384]{4,3,2,1,0:T(8,128)(2,1)} custom-call(s32[4]{0:T(128)} %pad_add_fusion.info, bf16[4,16,16,384]{3,2,1,0:T(8,128)(2,1)} %bitcast.126, bf16[3,32,384]{2,1,0:T(8,128)(2,1)} %collective-permute-done.8.near_ref, bf16[3,32,384]{2,1,0:T(8,128)(2,1)} %broadcast_1_far_ref.2.far_ref, bf16[160,384]{1,0:T(8,128)(2,1)} %collective-permute-done.9.a_ref, ...), custom_call_target="tpu_custom_call" | custom-call | flops 5600000000 | bytes 10000000 | tf_op jit(solution)/shard_map/pallas_call | solution.py:40
  147.4 2.4 %fusion = bf16[4,96,1536]{2,1,0:T(8,128)(2,1)S(1)} fusion(bf16[4,96,1536]{2,1,0:T(8,128)(2,1)} %collective-permute-done.14, pred[]{:T(512)S(6)} %eq.24, bf16[4,2,96,1536]{3,2,1,0:T(8,128)(2,1)} %bitcast.118), kind=kLoop, calls=%fused_computation.1 | loop fusion | flops 2949120 | bytes 4718593 | tf_op jit(solution)/shard_map/convert_element_type | solution.py:502
  149.9 2.9 %collective-permute-start.15 = (bf16[2,96,1536]{2,1,0:T(8,128)(2,1)S(1)}, bf16[2,96,1536]{2,1,0:T(8,128)(2,1)S(1)}, u32[]{:S(2)}, u32[]{:S(2)}) collective-permute-start(bf16[2,96,1536]{2,1,0:T(8,128)(2,1)S(1)} %select_bitcast_fusion.2), channel_id=1, source_target_pairs={{0,4},{2,6},{4,0},{6,2},{8,12},{10,14},{12,8},{14,10},{1,5},{3,7},... | collective-permute-start | bytes 1769480 | tf_op jit(solution)/shard_map/ppermute | solution.py:498
  152.8 1.7 fusion.1
  154.7 12.4 %collective-permute-done.15 = bf16[2,96,1536]{2,1,0:T(8,128)(2,1)S(1)} collective-permute-done((bf16[2,96,1536]{2,1,0:T(8,128)(2,1)S(1)}, bf16[2,96,1536]{2,1,0:T(8,128)(2,1)S(1)}, u32[]{:S(2)}, u32[]{:S(2)}) %collective-permute-start.15) | collective-permute-done | bytes 589856 | tf_op jit(solution)/shard_map/ppermute | solution.py:498
  167.3 3.1 %collective-permute-start.16 = (bf16[1,96,1536]{2,1,0:T(8,128)(2,1)S(1)}, bf16[1,96,1536]{2,1,0:T(8,128)(2,1)S(1)}, u32[]{:S(2)}, u32[]{:S(2)}) collective-permute-start(bf16[1,96,1536]{2,1,0:T(8,128)(2,1)S(1)} %select_bitcast_fusion.3), channel_id=1, source_target_pairs={{0,8},{2,10},{4,12},{6,14},{8,0},{10,2},{12,4},{14,6},{1,9},{3,11}... | collective-permute-start | bytes 884744 | tf_op jit(solution)/shard_map/ppermute | solution.py:498
  170.5 13.7 %collective-permute-done.12 = bf16[2,96,1536]{2,1,0:T(8,128)(2,1)S(1)} collective-permute-done((bf16[2,96,1536]{2,1,0:T(8,128)(2,1)S(1)}, bf16[2,96,1536]{2,1,0:T(8,128)(2,1)S(1)}, u32[]{:S(2)}, u32[]{:S(2)}) %collective-permute-start.12) | collective-permute-done | bytes 589856 | tf_op jit(solution)/shard_map/ppermute | solution.py:498
  184.5 3.2 %collective-permute-start.13 = (bf16[1,96,1536]{2,1,0:T(8,128)(2,1)S(1)}, bf16[1,96,1536]{2,1,0:T(8,128)(2,1)S(1)}, u32[]{:S(2)}, u32[]{:S(2)}) collective-permute-start(bf16[1,96,1536]{2,1,0:T(8,128)(2,1)S(1)} %select_bitcast_fusion.4), channel_id=1, source_target_pairs={{0,8},{2,10},{4,12},{6,14},{8,0},{10,2},{12,4},{14,6},{1,9},{3,11}... | collective-permute-start | bytes 884744 | tf_op jit(solution)/shard_map/ppermute | solution.py:498
  188.6 11.5 %collective-permute-done.13 = bf16[1,96,1536]{2,1,0:T(8,128)(2,1)S(1)} collective-permute-done((bf16[1,96,1536]{2,1,0:T(8,128)(2,1)S(1)}, bf16[1,96,1536]{2,1,0:T(8,128)(2,1)S(1)}, u32[]{:S(2)}, u32[]{:S(2)}) %collective-permute-start.13) | collective-permute-done | bytes 294944 | tf_op jit(solution)/shard_map/ppermute | solution.py:498
  (83 shorter events, 21.7 us)
Async XLA Ops:
  0.6 19.6 %copy-start.12 = (f32[384]{0:T(512)S(1)}, f32[384]{0:T(512)}, u32[]{:S(2)}) copy-start(f32[384]{0:T(512)} %param.15) | copy-start | bytes 4612
  6.9 8.2 %collective-permute-start = (bf16[3,32,384]{2,1,0:T(8,128)(2,1)}, bf16[3,32,384]{2,1,0:T(8,128)(2,1)S(1)}, u32[]{:S(2)}, u32[]{:S(2)}) collective-permute-start(bf16[3,32,384]{2,1,0:T(8,128)(2,1)} %get-tuple-element.25), channel_id=1, source_target_pairs={{0,8},{2,10},{4,12},{6,14},{8,0},{10,2},{12,4},{14,6},{1,9},{3,11}... | collective-permute-start | bytes 221192 | tf_op jit(solution)/shard_map/ppermute | solution.py:376
  17.8 5.8 %collective-permute-start.1 = (bf16[160,384]{1,0:T(8,128)(2,1)}, bf16[160,384]{1,0:T(8,128)(2,1)S(1)}, u32[]{:S(2)}, u32[]{:S(2)}) collective-permute-start(bf16[160,384]{1,0:T(8,128)(2,1)} %get-tuple-element.26), channel_id=1, source_target_pairs={{0,2},{2,0},{4,6},{6,4},{8,10},{10,8},{12,14},{14,12},{1,3},{3,1},... | collective-permute-start | bytes 368648 | tf_op jit(solution)/shard_map/ppermute | solution.py:376
  19.5 4.1 %collective-permute-start.2 = (bf16[160,384]{1,0:T(8,128)(2,1)}, bf16[160,384]{1,0:T(8,128)(2,1)S(1)}, u32[]{:S(2)}, u32[]{:S(2)}) collective-permute-start(bf16[160,384]{1,0:T(8,128)(2,1)} %get-tuple-element.27), channel_id=1, source_target_pairs={{2,4},{4,2},{10,12},{12,10},{3,5},{5,3},{11,13},{13,11},{18,20},{2... | collective-permute-start | bytes 368648 | tf_op jit(solution)/shard_map/ppermute | solution.py:376
  20.2 18.4 %collective-permute-start.4 = (bf16[1024,384]{1,0:T(8,128)(2,1)}, bf16[1024,384]{1,0:T(8,128)(2,1)S(1)}, u32[]{:S(2)}, u32[]{:S(2)}) collective-permute-start(bf16[1024,384]{1,0:T(8,128)(2,1)} %get-tuple-element.29.own_ref), channel_id=1, source_target_pairs={{0,1},{1,0},{2,3},{3,2},{4,5},{5,4},{6,7},{7,6},{8,9},{9,8},{10,11... | collective-permute-start | bytes 2359304 | tf_op jit(solution)/shard_map/ppermute | solution.py:364
  20.8 13.3 %copy-start.16 = (s32[8]{0:T(128)S(1)}, s32[8]{0:T(128)}, u32[]{:S(2)}) copy-start(s32[8]{0:T(128)} %param.24) | copy-start | bytes 100
  20.8 13.9 %copy-start.9 = (f32[1536]{0:T(1024)S(1)}, f32[1536]{0:T(1024)}, u32[]{:S(2)}) copy-start(f32[1536]{0:T(1024)} %param.19) | copy-start | bytes 18436
  20.8 14.5 %copy-start.7 = (f32[768]{0:T(1024)S(1)}, f32[768]{0:T(1024)}, u32[]{:S(2)}) copy-start(f32[768]{0:T(1024)} %param.16) | copy-start | bytes 9220
  20.9 15.1 %copy-start.10 = (f32[768]{0:T(1024)S(1)}, f32[768]{0:T(1024)}, u32[]{:S(2)}) copy-start(f32[768]{0:T(1024)} %param.17) | copy-start | bytes 9220
  34.1 12.6 %collective-permute-start.3 = (bf16[1024,384]{1,0:T(8,128)(2,1)}, bf16[1024,384]{1,0:T(8,128)(2,1)S(1)}, u32[]{:S(2)}, u32[]{:S(2)}) collective-permute-start(bf16[1024,384]{1,0:T(8,128)(2,1)} %bitcast.119), channel_id=1, source_target_pairs={{0,1},{1,0},{2,3},{3,2},{4,5},{5,4},{6,7},{7,6},{8,9},{9,8},{10,11... | collective-permute-start | bytes 2359304 | tf_op jit(solution)/shard_map/ppermute | solution.py:364
  38.6 0.9 copy-start.13
  66.3 19.3 %collective-permute-start.6 = (bf16[1024,384]{1,0:T(8,128)(2,1)}, bf16[1024,384]{1,0:T(8,128)(2,1)S(1)}, u32[]{:S(2)}, u32[]{:S(2)}) collective-permute-start(bf16[1024,384]{1,0:T(8,128)(2,1)} %get-tuple-element.34), channel_id=1, source_target_pairs={{0,1},{1,0},{2,3},{3,2},{4,5},{5,4},{6,7},{7,6},{8,9},{9,8},{10,11... | collective-permute-start | bytes 2359304 | tf_op jit(solution)/shard_map/ppermute | solution.py:364
  66.8 18.8 %collective-permute-start.7 = (f32[1024,128]{1,0:T(8,128)}, f32[1024,128]{1,0:T(8,128)S(1)}, u32[]{:S(2)}, u32[]{:S(2)}) collective-permute-start(f32[1024,128]{1,0:T(8,128)} %get-tuple-element.35.mine_ref), channel_id=1, source_target_pairs={{0,1},{1,0},{2,3},{3,2},{4,5},{5,4},{6,7},{7,6},{8,9},{9,8},{10,11... | collective-permute-start | bytes 1572872 | tf_op jit(solution)/shard_map/ppermute | solution.py:364
  75.8 71.6 %collective-permute-start.14 = (bf16[4,96,1536]{2,1,0:T(8,128)(2,1)}, bf16[4,96,1536]{2,1,0:T(8,128)(2,1)}, u32[]{:S(2)}, u32[]{:S(2)}) collective-permute-start(bf16[4,96,1536]{2,1,0:T(8,128)(2,1)} %select_bitcast_fusion), channel_id=1, source_target_pairs={{0,2},{2,0},{4,6},{6,4},{8,10},{10,8},{12,14},{14,12},{1,3},{3,1},... | collective-permute-start | bytes 3538952 | tf_op jit(solution)/shard_map/ppermute | solution.py:498
  79.3 35.5 %collective-permute-start.5 = (bf16[1024,384]{1,0:T(8,128)(2,1)}, bf16[1024,384]{1,0:T(8,128)(2,1)S(1)}, u32[]{:S(2)}, u32[]{:S(2)}) collective-permute-start(bf16[1024,384]{1,0:T(8,128)(2,1)} %get-tuple-element.32), channel_id=1, source_target_pairs={{0,1},{1,0},{2,3},{3,2},{4,5},{5,4},{6,7},{7,6},{8,9},{9,8},{10,11... | collective-permute-start | bytes 2359304 | tf_op jit(solution)/shard_map/ppermute | solution.py:364
  85.6 1.1 copy-start.3
  91.8 11.4 %copy-start = (bf16[768,1536]{1,0:T(8,128)(2,1)S(1)}, bf16[768,1536]{1,0:T(8,128)(2,1)}, u32[]{:S(2)}) copy-start(bf16[768,1536]{1,0:T(8,128)(2,1)} %shard_map.163) | copy-start | bytes 7077892
  100.7 9.4 %collective-permute-start.17 = (f32[56,384]{1,0:T(8,128)}, f32[56,384]{1,0:T(8,128)S(1)}, u32[]{:S(2)}, u32[]{:S(2)}) collective-permute-start(f32[56,384]{1,0:T(8,128)} %shard_map.165), channel_id=1, source_target_pairs={{0,2},{2,0},{4,6},{6,4},{8,10},{10,8},{12,14},{14,12},{1,3},{3,1},... | collective-permute-start | bytes 258056 | tf_op jit(solution)/shard_map/ppermute | solution.py:539
  101.0 5.6 %collective-permute-start.8 = (bf16[3,32,384]{2,1,0:T(8,128)(2,1)}, bf16[3,32,384]{2,1,0:T(8,128)(2,1)}, u32[]{:S(2)}, u32[]{:S(2)}) collective-permute-start(bf16[3,32,384]{2,1,0:T(8,128)(2,1)} %get-tuple-element.37), channel_id=1, source_target_pairs={{0,8},{2,10},{4,12},{6,14},{8,0},{10,2},{12,4},{14,6},{1,9},{3,11}... | collective-permute-start | bytes 221192 | tf_op jit(solution)/shard_map/ppermute | solution.py:376
  103.2 11.6 %copy-start.5 = (f32[56,384]{1,0:T(8,128)S(1)}, f32[56,384]{1,0:T(8,128)}, u32[]{:S(2)}) copy-start(f32[56,384]{1,0:T(8,128)} %shard_map.165) | copy-start | bytes 258052
  103.2 12.4 %copy-start.1 = (bf16[4,16,16,384]{3,2,1,0:T(8,128)(2,1)S(1)}, bf16[4,16,16,384]{3,2,1,0:T(8,128)(2,1)}, u32[]{:S(2)}) copy-start(bf16[4,16,16,384]{3,2,1,0:T(8,128)(2,1)} %x_ref.5) | copy-start | bytes 2359300
  103.2 12.4 %copy-start.8 = (f32[384]{0:T(512)S(1)}, f32[384]{0:T(512)}, u32[]{:S(2)}) copy-start(f32[384]{0:T(512)} %param.22) | copy-start | bytes 4612
  103.2 12.4 %copy-start.11 = (f32[384]{0:T(512)S(1)}, f32[384]{0:T(512)}, u32[]{:S(2)}) copy-start(f32[384]{0:T(512)} %param.21) | copy-start | bytes 4612
  104.4 48.4 %collective-permute-start.11 = (bf16[4,96,1536]{2,1,0:T(8,128)(2,1)}, bf16[4,96,1536]{2,1,0:T(8,128)(2,1)}, u32[]{:S(2)}, u32[]{:S(2)}) collective-permute-start(bf16[4,96,1536]{2,1,0:T(8,128)(2,1)} %select_bitcast_fusion.1), channel_id=1, source_target_pairs={{0,2},{2,0},{4,6},{6,4},{8,10},{10,8},{12,14},{14,12},{1,3},{3,1},... | collective-permute-start | bytes 3538952 | tf_op jit(solution)/shard_map/ppermute | solution.py:498
  108.8 13.5 %collective-permute-start.10 = (bf16[160,384]{1,0:T(8,128)(2,1)}, bf16[160,384]{1,0:T(8,128)(2,1)}, u32[]{:S(2)}, u32[]{:S(2)}) collective-permute-start(bf16[160,384]{1,0:T(8,128)(2,1)} %get-tuple-element.39), channel_id=1, source_target_pairs={{2,4},{4,2},{10,12},{12,10},{3,5},{5,3},{11,13},{13,11},{18,20},{2... | collective-permute-start | bytes 368648 | tf_op jit(solution)/shard_map/ppermute | solution.py:376
  110.1 27.7 %collective-permute-start.9 = (bf16[160,384]{1,0:T(8,128)(2,1)}, bf16[160,384]{1,0:T(8,128)(2,1)}, u32[]{:S(2)}, u32[]{:S(2)}) collective-permute-start(bf16[160,384]{1,0:T(8,128)(2,1)} %get-tuple-element.38), channel_id=1, source_target_pairs={{0,2},{2,0},{4,6},{6,4},{8,10},{10,8},{12,14},{14,12},{1,3},{3,1},... | collective-permute-start | bytes 368648 | tf_op jit(solution)/shard_map/ppermute | solution.py:376
  114.8 5.3 %collective-permute-start.18 = (f32[56,384]{1,0:T(8,128)S(1)}, f32[56,384]{1,0:T(8,128)S(1)}, u32[]{:S(2)}, u32[]{:S(2)}) collective-permute-start(f32[56,384]{1,0:T(8,128)S(1)} %add.88), channel_id=1, source_target_pairs={{0,4},{2,6},{4,0},{6,2},{8,12},{10,14},{12,8},{14,10},{1,5},{3,7},... | collective-permute-start | bytes 258056 | tf_op jit(solution)/shard_map/ppermute | solution.py:539
  120.1 26.7 %collective-permute-start.19 = (f32[56,384]{1,0:T(8,128)S(1)}, f32[56,384]{1,0:T(8,128)S(1)}, u32[]{:S(2)}, u32[]{:S(2)}) collective-permute-start(f32[56,384]{1,0:T(8,128)S(1)} %add.89), channel_id=1, source_target_pairs={{0,8},{2,10},{4,12},{6,14},{8,0},{10,2},{12,4},{14,6},{1,9},{3,11}... | collective-permute-start | bytes 258056 | tf_op jit(solution)/shard_map/ppermute | solution.py:539
  149.9 17.2 %collective-permute-start.15 = (bf16[2,96,1536]{2,1,0:T(8,128)(2,1)S(1)}, bf16[2,96,1536]{2,1,0:T(8,128)(2,1)S(1)}, u32[]{:S(2)}, u32[]{:S(2)}) collective-permute-start(bf16[2,96,1536]{2,1,0:T(8,128)(2,1)S(1)} %select_bitcast_fusion.2), channel_id=1, source_target_pairs={{0,4},{2,6},{4,0},{6,2},{8,12},{10,14},{12,8},{14,10},{1,5},{3,7},... | collective-permute-start | bytes 1769480 | tf_op jit(solution)/shard_map/ppermute | solution.py:498
  154.6 29.6 %collective-permute-start.12 = (bf16[2,96,1536]{2,1,0:T(8,128)(2,1)S(1)}, bf16[2,96,1536]{2,1,0:T(8,128)(2,1)S(1)}, u32[]{:S(2)}, u32[]{:S(2)}) collective-permute-start(bf16[2,96,1536]{2,1,0:T(8,128)(2,1)S(1)} %fusion.6), channel_id=1, source_target_pairs={{0,4},{2,6},{4,0},{6,2},{8,12},{10,14},{12,8},{14,10},{1,5},{3,7},... | collective-permute-start | bytes 1769480 | tf_op jit(solution)/shard_map/ppermute | solution.py:498
  167.3 20.4 %collective-permute-start.16 = (bf16[1,96,1536]{2,1,0:T(8,128)(2,1)S(1)}, bf16[1,96,1536]{2,1,0:T(8,128)(2,1)S(1)}, u32[]{:S(2)}, u32[]{:S(2)}) collective-permute-start(bf16[1,96,1536]{2,1,0:T(8,128)(2,1)S(1)} %select_bitcast_fusion.3), channel_id=1, source_target_pairs={{0,8},{2,10},{4,12},{6,14},{8,0},{10,2},{12,4},{14,6},{1,9},{3,11}... | collective-permute-start | bytes 884744 | tf_op jit(solution)/shard_map/ppermute | solution.py:498
  184.5 15.7 %collective-permute-start.13 = (bf16[1,96,1536]{2,1,0:T(8,128)(2,1)S(1)}, bf16[1,96,1536]{2,1,0:T(8,128)(2,1)S(1)}, u32[]{:S(2)}, u32[]{:S(2)}) collective-permute-start(bf16[1,96,1536]{2,1,0:T(8,128)(2,1)S(1)} %select_bitcast_fusion.4), channel_id=1, source_target_pairs={{0,8},{2,10},{4,12},{6,14},{8,0},{10,2},{12,4},{14,6},{1,9},{3,11}... | collective-permute-start | bytes 884744 | tf_op jit(solution)/shard_map/ppermute | solution.py:498
  (5 other events, 3.6 us)

commit v2 on v1

v2 whole, which is shorter than its diff:
```python
import functools
import math

import jax
import jax.numpy as jnp
from jax import lax
from jax.experimental import pallas as pl
from jax.experimental.pallas import tpu as pltpu
from jax.sharding import PartitionSpec as P

KERNEL = 7
RIM = 3
LANES = 128
F32 = jnp.float32
BF16 = jnp.bfloat16
VMEM_BYTES = 12 * 1024 * 1024
CONV_BYTES = 24 * 1024 * 1024
CHUNKS = 3

TAIL_P = 0.39
TAIL = (
    0.2353252521737435,
    0.0913882086982987,
    0.6495599070595628,
    -0.635400901941762,
    0.8866647490628095,
    -0.2275372167464003,
)
ROOT_HALF = 0.7071067811865476
DENSITY = 0.3989422804014327


def smem():
    return pl.BlockSpec(memory_space=pltpu.SMEM)


def whole(shape):
    return pl.BlockSpec(shape, lambda *_: (0,) * len(shape))


class Chain:
    def __init__(self):
        self.token = None

    def __call__(self, body, grid, ins, outs, shapes, scratch, args, limit=VMEM_BYTES, nbytes=1000):
        label = getattr(body, "func", body).__name__.removesuffix("_body")
        first = [] if self.token is None else [self.token]
        n_in, n_out = len(args), len(outs)

        def run(*refs):
            refs = refs[len(first) :]
            body(*refs[: n_in + n_out], *refs[n_in + n_out + 1 :])

        *got, self.token = pl.pallas_call(
            run,
            grid=grid,
            in_specs=[pl.BlockSpec(memory_space=pl.ANY)] * len(first) + list(ins),
            out_specs=list(outs) + [whole((8, LANES))],
            out_shape=list(shapes) + [jax.ShapeDtypeStruct((8, LANES), F32)],
            name=label,
            scratch_shapes=scratch,
            compiler_params=pltpu.CompilerParams(vmem_limit_bytes=limit),
            cost_estimate=pl.CostEstimate(flops=nbytes * 100, bytes_accessed=nbytes, transcendentals=0),
        )(*first, *args)
        return got


def phi_pair(h):
    e = jnp.exp(h * h * -0.5)
    den = 1.0 + (TAIL_P * ROOT_HALF) * jnp.abs(h)
    t = pl.reciprocal(den, approx=True)
    t = t * (2.0 - den * t)
    acc = jnp.full_like(h, 0.5 * TAIL[5])
    for coef in TAIL[4::-1]:
        acc = acc * t + 0.5 * coef
    tail = acc * t * e
    return jnp.where(h >= 0, 1.0 - tail, tail), e


def place(cols, tissue_ref):
    me = lax.axis_index("space")
    return (me // cols) % 2, (me % cols) % 2, tissue_ref[me]


def store_rims(odd_row, top, bottom, near_ref, far_ref):
    @pl.when(odd_row == 0)
    def _():
        for side in range(2):
            near_ref[:, side * 16 : side * 16 + 16, :] = bottom[side]
            far_ref[:, side * 16 : side * 16 + 16, :] = top[side]

    @pl.when(odd_row == 1)
    def _():
        for side in range(2):
            near_ref[:, side * 16 : side * 16 + 16, :] = top[side]
            far_ref[:, side * 16 : side * 16 + 16, :] = bottom[side]


def rims_body(cols, tissue_ref, x_ref, cot_ref, scale_ref, near_ref, far_ref, grad_ref):
    odd_row, _, count = place(cols, tissue_ref)

    def masked(slot, lo, hi):
        return (x_ref[slot, lo:hi].astype(F32) * (slot < count).astype(F32)).astype(BF16)

    store_rims(
        odd_row,
        [masked(0, 0, 3), masked(1, 0, 3)],
        [masked(2, 13, 16), masked(3, 13, 16)],
        near_ref,
        far_ref,
    )
    scale = scale_ref[...].reshape(1, -1)
    for slot in range(4):
        rows = slice(slot * 256, slot * 256 + 256)
        ok = (slot < count).astype(F32)
        grad_ref[rows, :] = (cot_ref[rows, :].astype(F32) * (ok * scale)).astype(BF16)


def side_body(masked, cols, tissue_ref, x_ref, near_ref, far_ref, a_ref, b_ref, east, west, packed):
    odd_row, odd_col, count = place(cols, tissue_ref)
    for slot in range(4):
        value = x_ref[slot].astype(F32)
        if masked:
            value = value * (slot < count).astype(F32)
        rows = slice(RIM + (slot // 2) * 16, RIM + (slot // 2) * 16 + 16)
        if slot % 2:
            east[rows] = value[:, 8:16, :]
        else:
            west[rows] = value[:, 0:8, :]
    near = near_ref[...].astype(F32)
    far = far_ref[...].astype(F32)
    is_odd = (odd_row == 1).astype(F32)
    north = near * is_odd + far * (1.0 - is_odd)
    south = near * (1.0 - is_odd) + far * is_odd
    east[0:3] = north[:, 24:32, :]
    west[0:3] = north[:, 0:8, :]
    east[35:38] = south[:, 24:32, :]
    west[35:38] = south[:, 0:8, :]
    zero = jnp.zeros_like(east[38:40])
    east[38:40] = zero
    west[38:40] = zero

    def pack(out_ref, source, at):
        packed[:, 0:4, :] = source[0:20, at : at + 4, :]
        packed[:, 4:8, :] = source[20:40, at : at + 4, :]
        out_ref[...] = packed[...].reshape(out_ref.shape).astype(BF16)

    @pl.when(odd_col == 0)
    def _():
        pack(a_ref, east, 4)
        pack(b_ref, west, 0)

    @pl.when(odd_col == 1)
    def _():
        pack(a_ref, west, 0)
        pack(b_ref, east, 4)


def conv_body(backward, cols, tissue_ref, x_ref, near_ref, far_ref, a_ref, b_ref, w_ref, last_ref, out_ref, *rest):
    blocks = x_ref.shape[3] // LANES
    if backward:
        image, *scratch = rest
        lefts = [ref.at[0] for ref in scratch[:2]]
        lefts = [lefts[c % 2] for c in range(blocks)]
        scratch = scratch[2:]
    else:
        left_ref, image, *scratch = rest
        lefts = [left_ref.at[c] for c in range(blocks)]
    weights = [scratch[c % 2] for c in range(blocks)]
    odd_row, odd_col, count = place(cols, tissue_ref)
    row_odd = (odd_row == 1).astype(F32)
    col_odd = (odd_col == 1).astype(F32)
    eye = lax.broadcasted_iota(jnp.int32, (LANES, LANES), 0) == lax.broadcasted_iota(
        jnp.int32, (LANES, LANES), 1
    )
    empty = jnp.zeros((LANES, LANES), BF16)

    def fill(c):
        lanes = slice(c * LANES, (c + 1) * LANES)
        for slot in range(4):
            value = x_ref[slot, :, :, lanes].astype(F32)
            if not backward:
                value = value * (slot < count).astype(F32)
            r, q = slot // 2, slot % 2
            image[RIM + 16 * r : RIM + 16 * r + 16, 8 + 16 * q : 24 + 16 * q, :] = value
        near = near_ref[:, :, lanes].astype(F32)
        far = far_ref[:, :, lanes].astype(F32)
        image[0:3, 8:40, :] = near * row_odd + far * (1.0 - row_odd)
        image[35:38, 8:40, :] = near * (1.0 - row_odd) + far * row_odd
        first = a_ref[:, lanes].astype(F32).reshape(20, 8, LANES)
        second = b_ref[:, lanes].astype(F32).reshape(20, 8, LANES)
        from_left = first * col_odd + second * (1.0 - col_odd)
        from_right = first * (1.0 - col_odd) + second * col_odd
        image[20:40, 0:8, :] = from_left
        image[0:20, 4:8, :] = from_left[:, 0:4, :]
        image[0:20, 40:48, :] = from_right
        image[20:40, 40:44, :] = from_right[:, 4:8, :]

    def windows(c, b):
        value = image[0:38, 5 + b : 37 + b, :].astype(BF16).reshape(19, 2, 32, LANES)
        for par in range(2):
            at = b * 256 + par * LANES
            lefts[c][:, at : at + LANES] = value[:, par].reshape(608, LANES)

    def diagonals(c, b):
        lanes = slice(c * LANES, (c + 1) * LANES)
        for a in range(-1, KERNEL + 1):
            if 0 <= a < KERNEL:
                tap = (KERNEL - 1 - a) * KERNEL + KERNEL - 1 - b if backward else a * KERNEL + b
                block = jnp.where(eye, w_ref[tap : tap + 1, lanes], 0.0).astype(BF16)
            elif c < 2:
                block = empty
            else:
                continue
            for o in range(2):
                r = a + o
                if 0 <= r < 8:
                    at = (r // 2) * 1792 + b * 256 + (r % 2) * LANES
                    weights[c][at : at + LANES, o * LANES : (o + 1) * LANES] = block

    def product(c, q):
        return jnp.dot(
            lefts[c][32 * q : 32 * q + 512, :],
            weights[c][1792 * q : 1792 * (q + 1), :],
            preferred_element_type=F32,
        )

    def finish(c, acc):
        lanes = slice(c * LANES, (c + 1) * LANES)
        acc = acc.reshape(16, 32, 256)
        for slot in range(4):
            r, q = slot // 2, slot % 2
            for o in range(2):
                value = acc[8 * r : 8 * r + 8, 16 * q : 16 * q + 16, o * LANES : (o + 1) * LANES]
                if backward:
                    value = (value + last_ref[slot, :, o, :, lanes].astype(F32)) * (slot < count).astype(F32)
                else:
                    value = value + last_ref[:, lanes].reshape(1, 1, LANES)
                out_ref[slot, :, o, :, lanes] = value.astype(BF16)

    for c in range(blocks + 1):
        acc = None
        if c < blocks:
            fill(c)
        for q in range(4):
            if c:
                term = product(c - 1, q)
                acc = term if acc is None else acc + term
            if c < blocks:
                for b in range(2 * q, min(2 * q + 2, KERNEL)):
                    windows(c, b)
                    diagonals(c, b)
        if c:
            finish(c - 1, acc)


def taps_body(g_ref, left_ref, out_ref, paired, sums):
    for slot in range(4):
        r, q = slot // 2, slot % 2
        for o in range(2):
            paired[8 * r : 8 * r + 8, 16 * q : 16 * q + 16, o * LANES : (o + 1) * LANES] = g_ref[slot, :, o].astype(F32)
    turned = paired[...].reshape(512, 256).T.astype(BF16)
    group = lax.broadcasted_iota(jnp.int32, (8, LANES), 1) // 8
    place_in = lax.broadcasted_iota(jnp.int32, (8, LANES), 1) % 8 == lax.broadcasted_iota(jnp.int32, (8, LANES), 0)

    def product(q):
        return jnp.dot(turned, left_ref[0, 32 * q : 32 * q + 512, :], preferred_element_type=F32)

    def diagonals(q, prod):
        for b in range(KERNEL):
            for par in range(2):
                for o in range(2):
                    a = 2 * q + par - o
                    if not 0 <= a < KERNEL:
                        continue
                    cols = slice(b * 256 + par * LANES, b * 256 + (par + 1) * LANES)
                    value = prod[o * LANES : o * LANES + 8, cols]
                    for k in range(1, 16):
                        row = o * LANES + 8 * k
                        value = jnp.where(group == k, prod[row : row + 8, cols], value)
                    key = a * KERNEL + b
                    if o == 0:
                        sums[key] = value
                    else:
                        sums[key] = sums[key] + value

    ahead = product(0)
    for q in range(4):
        prod = ahead
        if q < 3:
            ahead = product(q + 1)
        diagonals(q, prod)
    total = jnp.sum(jnp.where(place_in[None], sums[...], 0.0), axis=1)
    out_ref[0:49, :] = total
    out_ref[49:64, :] = jnp.zeros((15, LANES), F32)


def pick(second, own, other):
    s = second.astype(F32)
    own = own.astype(F32)
    other = other.astype(F32)
    low = own * (1.0 - s) + other * s
    high = own * s + other * (1.0 - s)
    return jnp.concatenate([low, high], axis=1)


def store_turned(devices, out_ref, turned, cols):
    per = turned.shape[0] // devices
    if per % 16:
        out_ref[:, cols] = turned
        return
    odd = lax.axis_index("space") % 2
    half = turned.shape[0] // 2
    for d in range(devices):
        at = (d // 2) * per + jnp.where(odd == d % 2, 0, half)
        out_ref[pl.ds(pl.multiple_of(at, 16), per), cols] = turned[d * per : (d + 1) * per]


def grad_in_body(devices, own_ref, other_ref, w_ref, out_ref, turned_ref, full_ref):
    second = lax.axis_index("tensor") == 1
    for slot in range(4):
        rows = slice(slot * 256, slot * 256 + 256)
        full = pick(second, own_ref[rows, :], other_ref[rows, :]).astype(BF16)
        full_ref[rows, :] = full
        store_turned(devices, turned_ref, full.T, rows)
        out_ref[rows, :] = jnp.dot(full, w_ref[...], preferred_element_type=F32)


def grad_more_body(full_ref, w_ref, out_ref):
    out_ref[...] = jnp.dot(full_ref[...], w_ref[...], preferred_element_type=F32)


def in_lanes(columns, lanes):
    lane = lax.broadcasted_iota(jnp.int32, (columns[0].shape[0], lanes), 1)
    value = jnp.zeros(lane.shape, F32)
    for at, column in enumerate(columns):
        value = jnp.where(lane == at, column, value)
    return value


def norm_body(devices, own_ref, other_ref, gain_ref, shift_ref, out_ref, turned_ref, stats_ref):
    gain = gain_ref[...].reshape(1, -1)
    shift = shift_ref[...].reshape(1, -1)
    second = lax.axis_index("tensor") == 1
    for slot in range(4):
        rows = slice(slot * 256, slot * 256 + 256)
        full = pick(second, own_ref[rows, :], other_ref[rows, :])
        mean = jnp.mean(full, axis=1, keepdims=True)
        centered = full - mean
        var = jnp.mean(centered * centered, axis=1, keepdims=True)
        inverse = lax.rsqrt(var + 1e-06)
        stats_ref[rows, :] = in_lanes((mean, inverse), stats_ref.shape[1])
        value = (centered * inverse * gain + shift).astype(BF16)
        out_ref[rows, :] = value
        store_turned(devices, turned_ref, value.T, rows)


def chunk_body(normed_ref, up_ref, bias_ref, in_ref, grad_turned_ref, turned_ref, act_ref, pre_ref, keep_ref, send_ref):
    bias = bias_ref[...]
    half = keep_ref.shape[1]
    for slot in range(4):
        rows = slice(slot * 256, slot * 256 + 256)
        hidden = jnp.dot(normed_ref[rows, :], up_ref[...], preferred_element_type=F32) + bias
        phi, e = phi_pair(hidden)
        act_ref[rows, :] = (hidden * phi).astype(BF16)
        pre_ref[rows, :] = (in_ref[rows, :] * (phi + hidden * (e * DENSITY))).astype(BF16)
    for at, left, right in ((0, grad_turned_ref, act_ref), (1, turned_ref, pre_ref)):
        grad = jnp.dot(left[...], right[...], preferred_element_type=F32).astype(BF16)
        keep_ref[at] = grad[:half]
        send_ref[at] = grad[half:]


def split(second, value):
    half = value.shape[1] // 2
    s = second.astype(F32)
    low, high = value[:, :half], value[:, half:]
    return low * (1.0 - s) + high * s, low * s + high * (1.0 - s)


def turned_dot(values, w_ref):
    total = None
    for at, ref in enumerate(values):
        width = ref.shape[1]
        term = lax.dot_general(
            ref[...], w_ref[:, at * width : (at + 1) * width], (((1,), (1,)), ((), ())), preferred_element_type=F32
        )
        total = term if total is None else total + term
    return total


def back_body(own_ref, other_ref, stats_ref, gain_ref, up_ref, *rest):
    pres, (keep_ref, send_ref, more_ref, sums_ref) = rest[:CHUNKS], rest[CHUNKS:]
    second = lax.axis_index("tensor") == 1
    back = turned_dot(pres, up_ref)
    rows = pick(second, own_ref[...], other_ref[...])
    stats = stats_ref[...]
    normalized = (rows - stats[:, 0:1]) * stats[:, 1:2]
    scaled = back * gain_ref[...].reshape(1, -1)
    both = (jnp.sum(scaled, axis=1, keepdims=True), jnp.sum(scaled * normalized, axis=1, keepdims=True))
    sums_ref[...] = in_lanes(both, LANES)
    pieces = []
    for value in both:
        for _ in range(3):
            piece = value.astype(BF16).astype(F32)
            pieces.append(piece)
            value = value - piece
    half = keep_ref.shape[1]
    keep, send = split(second, back)
    keep_ref[...] = keep
    cut = send_ref.shape[1]
    send_ref[...] = send[:, :cut].astype(BF16)
    more_ref[:, : half - cut] = send[:, cut:].astype(BF16)
    more_ref[:, half - cut :] = in_lanes(pieces, LANES).astype(BF16)


def branch_body(down_ref, *rest):
    acts, (keep_ref, send_ref, more_ref) = rest[:CHUNKS], rest[CHUNKS:]
    keep, send = split(lax.axis_index("tensor") == 1, turned_dot(acts, down_ref))
    keep_ref[...] = keep
    cut = send_ref.shape[1]
    send_ref[...] = send[:, :cut].astype(BF16)
    more_ref[...] = send[:, cut:].astype(BF16)


def first_body(keep_ref, got_ref, keep_out, send_out):
    bit = (lax.axis_index("space") // 2) % 2
    for half in range(2):
        for out_ref, at in ((keep_out, 2 * half + bit), (send_out, 2 * half + 1 - bit)):
            value = keep_ref[:, at].astype(F32) + got_ref[:, at].astype(F32)
            out_ref[:, half] = value.astype(out_ref.dtype)


def second_body(keep_ref, got_ref, keep_out, send_out):
    bit = lax.axis_index("space") // 4
    keep_out[...] = keep_ref[:, bit] + got_ref[:, bit].astype(F32)
    send_out[...] = (keep_ref[:, 1 - bit] + got_ref[:, 1 - bit].astype(F32)).astype(BF16)


def third_body(keep_ref, got_ref, out_ref):
    out_ref[...] = keep_ref[...] + got_ref[...].astype(F32)


def put_taps(value, send_ref, at):
    high = value.astype(BF16)
    low = (value - high.astype(F32)).astype(BF16)
    rows = value.shape[0]
    for lanes in range(value.shape[1] // LANES):
        cols = slice(lanes * LANES, (lanes + 1) * LANES)
        send_ref[at : at + rows, :] = high[:, cols]
        send_ref[at + rows : at + 2 * rows, :] = low[:, cols]
        at += 2 * rows
    return high.astype(F32) + low.astype(F32)


def got_taps(got_ref, at, shape):
    rows, width = shape
    parts = []
    for lanes in range(width // LANES):
        parts.append(got_ref[at : at + rows, :].astype(F32) + got_ref[at + rows : at + 2 * rows, :].astype(F32))
        at += 2 * rows
    return jnp.concatenate(parts, axis=1)


def first_taps_body(keep_ref, got_ref, taps_ref, taps_got_ref, keep_out, send_out, taps_out):
    bit = (lax.axis_index("space") // 2) % 2
    per, width = keep_ref.shape[2:]
    blocks = width // LANES
    for half in range(2):
        at = 2 * half + bit
        keep_out[:, half] = keep_ref[:, at].astype(F32) + got_ref[:, at].astype(F32)
        at = 2 * half + 1 - bit
        value = (keep_ref[:, at].astype(F32) + got_ref[:, at].astype(F32)).astype(BF16)
        for g in range(2):
            for lanes in range(blocks):
                row = ((g * 2 + half) * blocks + lanes) * per
                send_out[row : row + per, :] = value[g, :, lanes * LANES : (lanes + 1) * LANES]
    taps_out[...] = put_taps(taps_ref[...] + taps_got_ref[...], send_out, 4 * blocks * per)


def second_taps_body(keep_ref, got_ref, taps_ref, keep_out, send_out, taps_out):
    bit = lax.axis_index("space") // 4
    per, width = keep_ref.shape[2:]
    blocks = width // LANES
    for g in range(2):
        for lanes in range(blocks):
            cols = slice(lanes * LANES, (lanes + 1) * LANES)

            def got(half):
                row = pl.multiple_of(((g * 2 + half) * blocks + lanes) * per, 16)
                return got_ref[pl.ds(row, per), :].astype(F32)

            keep_out[g, :, cols] = keep_ref[g, bit, :, cols] + got(bit)
            row = (g * blocks + lanes) * per
            send_out[row : row + per, :] = (keep_ref[g, 1 - bit, :, cols] + got(1 - bit)).astype(BF16)
    total = taps_ref[...] + got_taps(got_ref, 4 * blocks * per, taps_ref.shape)
    taps_out[...] = put_taps(total, send_out, 2 * blocks * per)


def last_body(tissue_ref, *refs):
    *sums, keep_ref, got_ref, taps_ref, down_ref, up_ref, kernel_ref = refs
    tiles = tissue_ref[0]
    for at in range(1, tissue_ref.shape[0]):
        tiles = tiles + tissue_ref[at]
    scale = lax.rsqrt(jnp.full((8, LANES), 256.0, F32) * tiles.astype(F32))[0:1, 0:1]
    per, width = keep_ref.shape[1:]
    blocks = width // LANES
    for at, out_ref in enumerate((down_ref, up_ref)):
        for k, ref in enumerate(sums):
            out_ref[:, k * width : (k + 1) * width] = ref[at] * scale
        for lanes in range(blocks):
            cols = slice(lanes * LANES, (lanes + 1) * LANES)
            row = (at * blocks + lanes) * per
            value = keep_ref[at, :, cols] + got_ref[row : row + per, :].astype(F32)
            start = len(sums) * width + lanes * LANES
            out_ref[:, start : start + LANES] = value * scale
    total = taps_ref[...] + got_taps(got_ref, 2 * blocks * per, taps_ref.shape)
    kernel_ref[...] = (total * scale)[: kernel_ref.shape[0]]


def block_out_body(tissue_ref, x_ref, keep_ref, got_ref, more_ref, scale_ref, bias_ref, out_ref):
    count = tissue_ref[lax.axis_index("space")]
    ok = (pl.program_id(0) < count).astype(F32)
    got = jnp.concatenate([got_ref[...], more_ref[...]], axis=1).astype(F32)
    branch = keep_ref[...] + got + bias_ref[...].reshape(1, -1)
    value = (x_ref[...].astype(F32) + scale_ref[...].reshape(1, -1) * branch) * ok
    out_ref[...] = value.astype(BF16)


def norm_back_body(cols, tissue_ref, own_ref, stats_ref, keep_ref, got_ref, more_ref, sums_ref, gain_ref, out_ref, near_ref, far_ref):
    half = own_ref.shape[1]
    stats = stats_ref[...]
    inverse = stats[:, 1:2]
    normalized = (own_ref[...].astype(F32) - stats[:, 0:1]) * inverse
    got = jnp.concatenate([got_ref[...], more_ref[...]], axis=1).astype(F32)
    scaled = (keep_ref[...] + got[:, :half]) * gain_ref[...]
    sums = sums_ref[...]
    first = (sums[:, 0:1] + (got[:, half : half + 1] + got[:, half + 1 : half + 2] + got[:, half + 2 : half + 3])) / (2.0 * half)
    other = (sums[:, 1:2] + (got[:, half + 3 : half + 4] + got[:, half + 4 : half + 5] + got[:, half + 5 : half + 6])) / (2.0 * half)
    grad = inverse * (scaled - first - normalized * other)
    out_ref[...] = grad.astype(BF16)
    tile = grad.reshape(16, 16, grad.shape[1])
    odd_row, _, _ = place(cols, tissue_ref)
    slot = pl.program_id(0)
    for side in range(2):
        span = slice(side * 16, side * 16 + 16)

        @pl.when(slot == side)
        def _():
            top = tile[0:3].astype(BF16)

            @pl.when(odd_row == 0)
            def _():
                far_ref[:, span, :] = top

            @pl.when(odd_row == 1)
            def _():
                near_ref[:, span, :] = top

        @pl.when(slot == side + 2)
        def _():
            bottom = tile[13:16].astype(BF16)

            @pl.when(odd_row == 0)
            def _():
                near_ref[:, span, :] = bottom

            @pl.when(odd_row == 1)
            def _():
                far_ref[:, span, :] = bottom


def on_device(
    features, dw_kernel, dw_bias, ln_gain, ln_bias, w_up, up_bias, w_down, down_bias, layer_scale,
    cotangent, neighbors, tissue_count,
):
    tiles_dev, side, _, chans = features.shape
    units = w_up.shape[1]
    cells = tiles_dev * side * side
    devices = lax.axis_size("space")
    me = lax.axis_index("space")
    tensor_index = lax.axis_index("tensor")
    block_rows = max(d for d in range(1, math.isqrt(devices) + 1) if devices % d == 0)
    block_cols = devices // block_rows
    blocks = chans // LANES

    call = Chain()

    def sds(shape, dtype):
        return jax.ShapeDtypeStruct(shape, dtype)

    hbm = pltpu.HBM

    def pin(value):
        return pltpu.with_memory_space_constraint(value, pltpu.HBM)

    def across(value):
        return lax.ppermute(value, "tensor", [(0, 1), (1, 0)])

    def exchanged(value, bit):
        return lax.ppermute(value, "space", [(d, d ^ bit) for d in range(devices)])

    def paired(value, along_rows, round_at):
        size = block_rows if along_rows else block_cols
        pairs = []
        for d in range(devices):
            place = d // block_cols if along_rows else d % block_cols
            other = place + 1 if place % 2 == round_at else place - 1
            if 0 <= other < size:
                pairs.append((d, d + (other - place) * (block_cols if along_rows else 1)))
        if not pairs:
            return jnp.zeros_like(value)
        return lax.ppermute(value, "space", pairs)

    rim_shape = (RIM, 2 * side, chans)
    pack_shape = (160, chans)

    def sides(x, near, far, masked):
        return call(
            functools.partial(side_body, masked, block_cols),
            (1,),
            [smem(), whole(features.shape), whole(rim_shape), whole(rim_shape)],
            [whole(pack_shape)] * 2,
            [sds(pack_shape, BF16)] * 2,
            [pltpu.VMEM((40, 8, chans), F32), pltpu.VMEM((40, 8, chans), F32), pltpu.VMEM((20, 8, chans), F32)],
            (tissue, x, near, far),
        )

    split_shape = (4, 8, 2, side, chans)
    split_spec = pl.BlockSpec((4, 8, 2, side, LANES), lambda c: (0, 0, 0, 0, c))

    left_shape = (blocks, 608, 1792)

    def conv(x, near, far, one, two, last, backward):
        outs = [whole(split_shape)]
        shapes = [sds(split_shape, BF16)]
        scratch = [pltpu.VMEM((40, 48, LANES), F32)]
        if backward:
            scratch += [pltpu.VMEM((1,) + left_shape[1:], BF16)] * 2
        else:
            outs.append(whole(left_shape))
            shapes.append(hbm(left_shape, BF16))
        scratch += [pltpu.VMEM((4 * 1792, 256), BF16)] * 2
        return call(
            functools.partial(conv_body, backward, block_cols),
            (1,),
            [
                smem(), whole(features.shape), whole(rim_shape), whole(rim_shape), whole(pack_shape), whole(pack_shape),
                whole((KERNEL * KERNEL, chans)), whole(last.shape),
            ],
            outs, shapes, scratch,
            (tissue, x, near, far, one, two, dw_kernel, last), CONV_BYTES, 100000000 if backward else 1000,
        )

    total = 2 * chans
    width = units // CHUNKS

    def at_chunk(shape, k):
        return pl.BlockSpec(shape, lambda *_: (0, k))

    tissue = pin(tissue_count)
    near_send, far_send, branch_grad = call(
        functools.partial(rims_body, block_cols),
        (1,),
        [smem(), whole(features.shape), whole((cells, chans)), whole((chans,))],
        [whole(rim_shape), whole(rim_shape), whole((cells, chans))],
        [sds(rim_shape, BF16), sds(rim_shape, BF16), sds((cells, chans), BF16)],
        [], (tissue, pin(features), pin(cotangent.reshape(cells, chans)), layer_scale),
    )
    near = paired(near_send, True, 0)
    far = paired(far_send, True, 1)
    other_grad = across(branch_grad)
    act_grads = [None] * CHUNKS
    act_grads[0], grad_turned, grad_full = call(
        functools.partial(grad_in_body, devices),
        (1,),
        [whole((cells, chans)), whole((cells, chans)), at_chunk((total, width), 0)],
        [whole((cells, width)), whole((total, cells)), whole((cells, total))],
        [sds((cells, width), F32), sds((total, cells), BF16), sds((cells, total), BF16)],
        [], (branch_grad, other_grad, w_down),
    )
    one_send, two_send = sides(features, near, far, True)
    one = paired(one_send, False, 0)
    two = paired(two_send, False, 1)

    def more(k):
        (act_grads[k],) = call(
            grad_more_body,
            (1,),
            [whole((cells, total)), at_chunk((total, width), k)],
            [whole((cells, width))],
            [sds((cells, width), F32)],
            [], (grad_full, w_down),
        )

    for k in range(1, CHUNKS - 1):
        more(k)
    conv_out, left = conv(features, near, far, one, two, dw_bias.reshape(1, chans), False)
    conv_own = conv_out.reshape(cells, chans)
    conv_other = across(conv_own)
    more(CHUNKS - 1)
    normed, normed_turned, stats = call(
        functools.partial(norm_body, devices),
        (1,),
        [whole((cells, chans)), whole((cells, chans)), whole((total,)), whole((total,))],
        [whole((cells, total)), whole((total, cells)), whole((cells, LANES))],
        [sds((cells, total), BF16), sds((total, cells), BF16), sds((cells, LANES), F32)],
        [], (conv_own, conv_other, ln_gain, ln_bias),
    )

    grad_scale = lax.rsqrt(F32(side * side) * jnp.sum(tissue_count).astype(F32))
    stepped = devices == 8
    per = total // devices
    acts, pres, kept, got = [], [], [], []
    for k in range(CHUNKS):
        act, pre, keep, send = call(
            chunk_body,
            (1,),
            [
                whole((cells, total)), at_chunk((total, width), k), at_chunk((1, width), k), whole((cells, width)),
                whole((total, cells)), whole((total, cells)),
            ],
            [whole((cells, width)), whole((cells, width)), whole((2, chans, width)), whole((2, chans, width))],
            [hbm((cells, width), BF16), sds((cells, width), BF16), sds((2, chans, width), BF16), hbm((2, chans, width), BF16)],
            [],
            (normed, w_up, up_bias.reshape(1, units), act_grads[k], grad_turned, normed_turned),
        )
        acts.append(act)
        pres.append(pre)
        kept.append(keep)
        got.append(exchanged(send, 1) if stepped else send)

    def first(k):
        if stepped:
            shape = (2, 4, per, width)
            out = (2, 2, per, width)
            keep, send = call(
                first_body, (1,), [whole(shape)] * 2, [whole(out)] * 2, [hbm(out, F32), sds(out, BF16)], [],
                (kept[k].reshape(shape), got[k].reshape(shape)),
            )
            kept[k], got[k] = keep, exchanged(send, 2)

    def second(k):
        if stepped:
            out = (2, per, width)
            keep, send = call(
                second_body, (1,), [whole((2, 2, per, width))] * 2, [whole(out)] * 2, [sds(out, F32), sds(out, BF16)], [],
                (pin(kept[k]), got[k]),
            )
            kept[k], got[k] = keep, exchanged(send, 4)

    def third(k):
        if stepped:
            out = (2, per, width)
            (kept[k],) = call(
                third_body, (1,), [whole(out)] * 2, [whole(out)], [sds(out, F32)], [], (kept[k], got[k])
            )

    def scattered(k):
        value = jnp.concatenate([kept[k], got[k]], axis=1)
        if devices & (devices - 1):
            return lax.psum_scatter(value.astype(F32), "space", scatter_dimension=1, tiled=True) * grad_scale
        value = value.reshape(2, devices, -1, width)
        bit = 1
        while bit < devices:
            halves = value.reshape(2, -1, 2, *value.shape[2:])
            high = (me // bit) % 2 == 1
            send = jnp.where(high, halves[:, :, 0], halves[:, :, 1])
            keep = jnp.where(high, halves[:, :, 1], halves[:, :, 0])
            value = keep.astype(F32) + exchanged(send, bit).astype(F32)
            bit *= 2
            if bit < devices:
                value = value.astype(BF16)
        return value.reshape(2, -1, width) * grad_scale

    row_block = pl.BlockSpec((256, chans), lambda i: (i, 0))
    sums_spec = pl.BlockSpec((256, LANES), lambda i: (i, 0))
    wide = (chans + LANES) // 2
    wide_block = pl.BlockSpec((256, wide), lambda i: (i, 0))
    chunk_rows = [pl.BlockSpec((256, width), lambda i: (i, 0))] * CHUNKS
    back_keep, back_send, back_more, sums = call(
        back_body,
        (tiles_dev,),
        [row_block, row_block, sums_spec, whole((total,)), whole((total, units))] + chunk_rows,
        [row_block, wide_block, wide_block, sums_spec],
        [hbm((cells, chans), F32), hbm((cells, wide), BF16), hbm((cells, wide), BF16), hbm((cells, LANES), F32)],
        [], (conv_own, conv_other, stats, ln_gain, w_up, *pres),
    )
    back_got = across(back_send), across(back_more)
    def first_taps(k):
        out = (2, 2, per, width)
        rows = 4 * per * width // LANES + 2 * taps.shape[0] * blocks
        shape = (2, 4, per, width)
        keep, send, value = call(
            first_taps_body, (1,), [whole(shape)] * 2 + [whole(taps.shape)] * 2,
            [whole(out), whole((rows, LANES)), whole(taps.shape)],
            [sds(out, F32), sds((rows, LANES), BF16), sds(taps.shape, F32)], [],
            (kept[k].reshape(shape), got[k].reshape(shape), taps, taps_got),
        )
        kept[k], got[k] = keep, exchanged(send, 2)
        return value

    def second_taps(k):
        out = (2, per, width)
        was = got[k].shape
        rows = 2 * per * width // LANES + 2 * taps.shape[0] * blocks
        keep, send, value = call(
            second_taps_body, (1,), [whole((2, 2, per, width)), whole(was), whole(taps.shape)],
            [whole(out), whole((rows, LANES)), whole(taps.shape)],
            [sds(out, F32), sds((rows, LANES), BF16), sds(taps.shape, F32)], [], (kept[k], got[k], taps),
        )
        kept[k], got[k] = keep, exchanged(send, 4)
        return value

    first(0)
    my_gain = lax.dynamic_slice_in_dim(ln_gain.reshape(1, total), lax.axis_index("tensor") * chans, chans, 1)
    conv_grad, near_send, far_send = call(
        functools.partial(norm_back_body, block_cols),
        (tiles_dev,),
        [smem(), row_block, sums_spec, row_block, wide_block, wide_block, sums_spec, whole((1, chans))],
        [row_block, whole(rim_shape), whole(rim_shape)],
        [sds((cells, chans), BF16), sds(rim_shape, BF16), sds(rim_shape, BF16)],
        [],
        (tissue, pin(conv_own), pin(stats), pin(back_keep), *back_got, pin(sums), my_gain),
    )
    near = paired(near_send, True, 0)
    far = paired(far_send, True, 1)
    branch_keep, branch_send, branch_more = call(
        branch_body,
        (tiles_dev,),
        [whole((total, units))] + chunk_rows,
        [row_block, pl.BlockSpec((256, 2 * LANES), lambda i: (i, 0)), sums_spec],
        [sds((cells, chans), F32), sds((cells, 2 * LANES), BF16), sds((cells, LANES), BF16)],
        [], (w_down, *acts),
    )
    branch_got = across(branch_send), across(branch_more)
    second(0)
    conv_grad_tiles = conv_grad.reshape(features.shape)
    one_send, two_send = sides(conv_grad_tiles, near, far, False)
    one = paired(one_send, False, 0)
    two = paired(two_send, False, 1)
    first(1)
    (taps,) = call(
        taps_body,
        (blocks,),
        [split_spec, pl.BlockSpec((1, 608, 1792), lambda c: (c, 0, 0))],
        [pl.BlockSpec((64, LANES), lambda c: (0, c))],
        [sds((64, chans), F32)],
        [pltpu.VMEM((16, 32, 256), F32), pltpu.VMEM((KERNEL * KERNEL, 8, LANES), F32)],
        (conv_grad.reshape(split_shape), pin(left)),
    )
    taps_got = exchanged(taps, 1) if stepped else None
    third(0)
    (block_out,) = call(
        block_out_body,
        (tiles_dev,),
        [smem(), row_block, row_block, pl.BlockSpec((256, 2 * LANES), lambda i: (i, 0)), sums_spec, whole((chans,)), whole((chans,))],
        [row_block],
        [sds((cells, chans), BF16)],
        [], (tissue, features.reshape(cells, chans), branch_keep, *branch_got, layer_scale, down_bias),
    )
    block_out = block_out.reshape(features.shape)
    second(1)
    if stepped:
        taps = first_taps(2)
    third(1)
    (grad_features,) = conv(
        conv_grad_tiles, near, far, one, two, cotangent.reshape(split_shape), True
    )
    grad_features = grad_features.reshape(features.shape)
    if stepped:
        taps = second_taps(2)
    if stepped:
        kernel_shape = (KERNEL * KERNEL, chans)
        grad_down, grad_up, grad_kernel = call(
            last_body,
            (1,),
            [smem()] + [whole((2, per, width))] * CHUNKS + [whole(got[CHUNKS - 1].shape), whole(taps.shape)],
            [whole((per, units))] * 2 + [whole(kernel_shape)],
            [sds((per, units), F32)] * 2 + [sds(kernel_shape, F32)],
            [], (tissue, *kept, got[CHUNKS - 1], taps),
        )
    else:
        grad_kernel = lax.psum(taps, "space")[: KERNEL * KERNEL] * grad_scale
        grads = [scattered(k) for k in range(CHUNKS)]
        grad_down = jnp.concatenate([g[0] for g in grads], axis=1).reshape(-1, units)
        grad_up = jnp.concatenate([g[1] for g in grads], axis=1).reshape(-1, units)
    return (block_out, grad_features, grad_up, grad_down, grad_kernel)


def solution(mesh):
    return jax.shard_map(
        on_device,
        mesh=mesh,
        in_specs=(
            P(("slide", "space"), None, None, "tensor"),
            P(None, "tensor"),
            P("tensor"),
            P(),
            P(),
            P(None, "tensor"),
            P("tensor"),
            P(None, "tensor"),
            P("tensor"),
            P("tensor"),
            P(("slide", "space"), None, None, "tensor"),
            P("slide", None),
            P("slide"),
        ),
        out_specs=(
            P(("slide", "space"), None, None, "tensor"),
            P(("slide", "space"), None, None, "tensor"),
            P(("slide", "space"), "tensor"),
            P(("slide", "space"), "tensor"),
            P("slide", "tensor"),
        ),
        check_vma=False,
    )
```

time: 202 us -> 142 us (0.70)
  waiting for transfers between devices: 62.2 us -> 25.4 us
  other arithmetic: 16.5 us -> 0 us
  local copies, waits for them, and re-layouts: 10.4 us -> 2.52 us
    ppermute x9 -> x10, waiting for transfers between devices: 39.4 us -> 17.5 us  [exchanged(): return lax.ppermute(value, 'space', [(d, d ^ bit) for d in range(devices)])]
    ppermute x6, waiting for transfers between devices: 22.8 us -> 6.63 us  [paired(): return lax.ppermute(value, 'space', pairs)]
    convert_element_type x4 -> x0, other arithmetic: 7.44 us -> none  [the longest x2 4.13 us: scattered(): value = value.astype(BF16)]
    select_n x6 -> x0, other arithmetic: 4.17 us -> none  [scattered(): send = jnp.where(high, halves[:, 0], halves[:, 1])]
    ppermute x9 -> x10, starting transfers between devices: 17.8 us -> 21.5 us  [exchanged(): return lax.ppermute(value, 'space', [(d, d ^ bit) for d in range(devices)])]
    ppermute x6, starting transfers between devices: 14.6 us -> 11.7 us  [paired(): return lax.ppermute(value, 'space', pairs)]
    mul x3 -> x0, other arithmetic: 2.51 us -> none  [the longest x2 1.86 us: scattered(): return value.reshape(-1, units) * grad_scale]
    unnamed x36 -> x44, local copies, waits for them, and re-layouts: 4.25 us -> 2.43 us
  transfers between devices with their start and end apart: 20 -> 22, of which waited for: 8 -> 8; matrix products, arithmetic and copies ran while one was open for 9% -> 0% of each run, Pallas kernels for 27% -> 39%
where the time goes in v2:
time: 142 us; the launch traced here: 141 us
  Pallas kernels  78 us (55%)
  starting transfers between devices  34.3 us (24%)
  waiting for transfers between devices  25.4 us (18%)
  local copies, waits for them, and re-layouts  2.52 us (2%)
    pallas_call x26, Pallas kernels, __call__(): pl.pallas_call(run, grid=grid, in_specs=[pl.BlockSpec(memory_space=pl.ANY...  78 us
    ppermute x10, starting transfers between devices, exchanged(): return lax.ppermute(value, 'space', [(d, d ^ bit) for d in range(devices)])  21.5 us
    ppermute x10, waiting for transfers between devices, exchanged(): return lax.ppermute(value, 'space', [(d, d ^ bit) for d in range(devices)])  17.5 us
    ppermute x6, starting transfers between devices, paired(): return lax.ppermute(value, 'space', pairs)  11.7 us
    ppermute x6, waiting for transfers between devices, paired(): return lax.ppermute(value, 'space', pairs)  6.63 us
  transfers between devices with their start and end apart: 22, of which 8 were waited for; matrix products, arithmetic and copies ran while one was open for 0% of the time, Pallas kernels for 39%

profile of v2, /device:TPU:0, one launch (start us, length us, event | category | flops | bytes accessed | tf_op | source)
XLA Modules:
  0.0 141.2 jit_solution(14809799524672519065)
XLA Ops:
  1.3 2.1 %rims.1 = (bf16[3,32,384]{2,1,0:T(8,128)(2,1)S(1)}, bf16[3,32,384]{2,1,0:T(8,128)(2,1)}, bf16[1024,384]{1,0:T(8,128)(2,1)S(1)}, f32[8,128]{1,0:T(8,128)S(1)}) custom-call(s32[8]{0:T(128)} %refs_1_.17, bf16[4,16,16,384]{3,2,1,0:T(8,128)(2,1)} %refs_2_.9, bf16[1024,384]{1,0:T(8,128)(2,1)} %bitcast.23, f32[384]{0:T(512)S(1)} %copy-done.16), custom_call_target="tpu_custom_call" | custom-call | flops 100000 | bytes 1000 | tf_op jit(solution)/shard_map/rims/pallas_call | solution.py:54
  3.9 3.6 %collective-permute-start.1 = (bf16[3,32,384]{2,1,0:T(8,128)(2,1)S(1)}, bf16[3,32,384]{2,1,0:T(8,128)(2,1)S(1)}, u32[]{:S(2)}, u32[]{:S(2)}) collective-permute-start(bf16[3,32,384]{2,1,0:T(8,128)(2,1)S(1)} %get-tuple-element.92), channel_id=1, source_target_pairs={{0,8},{2,10},{4,12},{6,14},{8,0},{10,2},{12,4},{14,6},{1,9},{3,11}... | collective-permute-start | bytes 221192 | tf_op jit(solution)/shard_map/ppermute | solution.py:612
  7.5 1.7 %copy-done = bf16[768,1536]{1,0:T(8,128)(2,1)S(1)} copy-done((bf16[768,1536]{1,0:T(8,128)(2,1)S(1)}, bf16[768,1536]{1,0:T(8,128)(2,1)}, u32[]{:S(2)}) %copy-start) | copy-done | bytes 2359320
  10.4 1.6 %collective-permute-done.1.refs_3_ = bf16[3,32,384]{2,1,0:T(8,128)(2,1)S(1)} collective-permute-done((bf16[3,32,384]{2,1,0:T(8,128)(2,1)S(1)}, bf16[3,32,384]{2,1,0:T(8,128)(2,1)S(1)}, u32[]{:S(2)}, u32[]{:S(2)}) %collective-permute-start.1) | collective-permute-done | bytes 73760 | tf_op jit(solution)/shard_map/ppermute | solution.py:612
  12.9 1.6 %collective-permute-start.2 = (bf16[160,384]{1,0:T(8,128)(2,1)S(1)}, bf16[160,384]{1,0:T(8,128)(2,1)S(1)}, u32[]{:S(2)}, u32[]{:S(2)}) collective-permute-start(bf16[160,384]{1,0:T(8,128)(2,1)S(1)} %get-tuple-element.96), channel_id=1, source_target_pairs={{0,2},{2,0},{4,6},{6,4},{8,10},{10,8},{12,14},{14,12},{1,3},{3,1},... | collective-permute-start | bytes 368648 | tf_op jit(solution)/shard_map/ppermute | solution.py:612
  16.3 1.9 %collective-permute-done.2.refs_5_ = bf16[160,384]{1,0:T(8,128)(2,1)S(1)} collective-permute-done((bf16[160,384]{1,0:T(8,128)(2,1)S(1)}, bf16[160,384]{1,0:T(8,128)(2,1)S(1)}, u32[]{:S(2)}, u32[]{:S(2)}) %collective-permute-start.2) | collective-permute-done | bytes 122912 | tf_op jit(solution)/shard_map/ppermute | solution.py:612
  18.2 10.3 %conv.2 = (bf16[4,8,2,16,384]{4,3,2,1,0:T(8,128)(2,1)S(1)}, bf16[3,608,1792]{2,1,0:T(8,128)(2,1)}, f32[8,128]{1,0:T(8,128)S(1)}) custom-call(f32[8,128]{1,0:T(8,128)S(1)} %get-tuple-element.95.refs_0_, s32[8]{0:T(128)} %refs_1_.17, bf16[4,16,16,384]{3,2,1,0:T(8,128)(2,1)S(1)} %copy-done.3, bf16[3,32,384]{2,1,0:T(8,128)(2,1)S(1)} %collective-permute-done.1.refs_3_, ...), custom_call_target="tpu_custom_call" | custom-call | flops 100000 | bytes 1000 | tf_op jit(solution)/shard_map/conv/pallas_call | solution.py:54
  30.7 1.6 %norm.1 = (bf16[1024,768]{1,0:T(8,128)(2,1)S(1)}, bf16[768,1024]{1,0:T(8,128)(2,1)S(1)}, f32[1024,128]{1,0:T(8,128)S(1)}, f32[8,128]{1,0:T(8,128)S(1)}) custom-call(f32[8,128]{1,0:T(8,128)S(1)} %get-tuple-element.99.refs_0_, bf16[1024,384]{1,0:T(8,128)(2,1)S(1)} %bitcast.16, bf16[1024,384]{1,0:T(8,128)(2,1)S(1)} %collective-permute-done.4.refs_2_, ...), custom_call_target="tpu_custom_call" | custom-call | flops 100000 | bytes 1000 | tf_op jit(solution)/shard_map/norm/pallas_call | solution.py:54
  32.4 5.7 %chunk.3 = (bf16[1024,512]{1,0:T(8,128)(2,1)}, bf16[1024,512]{1,0:T(8,128)(2,1)S(1)}, bf16[2,384,512]{2,1,0:T(8,128)(2,1)S(1)}, bf16[2,384,512]{2,1,0:T(8,128)(2,1)}, f32[8,128]{1,0:T(8,128)S(1)}) custom-call(f32[8,128]{1,0:T(8,128)S(1)} %get-tuple-element.101.refs_0_, bf16[1024,768]{1,0:T(8,128)(2,1)S(1)} %get-tuple-element.102.refs_1_, ...), custom_call_target="tpu_custom_call" | custom-call | flops 100000 | bytes 1000 | tf_op jit(solution)/shard_map/chunk/pallas_call | solution.py:54
  38.1 4.5 %collective-permute-start.5 = (bf16[2,384,512]{2,1,0:T(8,128)(2,1)}, bf16[2,384,512]{2,1,0:T(8,128)(2,1)S(1)}, u32[]{:S(2)}, u32[]{:S(2)}) collective-permute-start(bf16[2,384,512]{2,1,0:T(8,128)(2,1)} %get-tuple-element.117), channel_id=1, source_target_pairs={{0,2},{2,0},{4,6},{6,4},{8,10},{10,8},{12,14},{14,12},{1,3},{3,1},... | collective-permute-start | bytes 2359304 | tf_op jit(solution)/shard_map/ppermute | solution.py:600
  42.6 5.6 %chunk.4 = (bf16[1024,512]{1,0:T(8,128)(2,1)}, bf16[1024,512]{1,0:T(8,128)(2,1)S(1)}, bf16[2,384,512]{2,1,0:T(8,128)(2,1)S(1)}, bf16[2,384,512]{2,1,0:T(8,128)(2,1)}, f32[8,128]{1,0:T(8,128)S(1)}) custom-call(f32[8,128]{1,0:T(8,128)S(1)} %get-tuple-element.106.refs_0_, bf16[1024,768]{1,0:T(8,128)(2,1)S(1)} %get-tuple-element.102.refs_1_, ...), custom_call_target="tpu_custom_call" | custom-call | flops 100000 | bytes 1000 | tf_op jit(solution)/shard_map/chunk/pallas_call | solution.py:54
  48.2 5.6 %chunk.5 = (bf16[1024,512]{1,0:T(8,128)(2,1)}, bf16[1024,512]{1,0:T(8,128)(2,1)S(1)}, bf16[2,384,512]{2,1,0:T(8,128)(2,1)S(1)}, bf16[2,384,512]{2,1,0:T(8,128)(2,1)}, f32[8,128]{1,0:T(8,128)S(1)}) custom-call(f32[8,128]{1,0:T(8,128)S(1)} %get-tuple-element.108.refs_0_, bf16[1024,768]{1,0:T(8,128)(2,1)S(1)} %get-tuple-element.102.refs_1_, ...), custom_call_target="tpu_custom_call" | custom-call | flops 100000 | bytes 1000 | tf_op jit(solution)/shard_map/chunk/pallas_call | solution.py:54
  53.9 5.2 %back.1 = (f32[1024,384]{1,0:T(8,128)}, bf16[1024,256]{1,0:T(8,128)(2,1)}, bf16[1024,256]{1,0:T(8,128)(2,1)}, f32[1024,128]{1,0:T(8,128)}, f32[8,128]{1,0:T(8,128)S(1)}) custom-call(f32[8,128]{1,0:T(8,128)S(1)} %get-tuple-element.110.refs_0_, bf16[1024,384]{1,0:T(8,128)(2,1)S(1)} %bitcast.17, bf16[1024,384]{1,0:T(8,128)(2,1)S(1)} %collective-permute-done.4.refs_2_, ...), custom_call_target="tpu_custom_call" | custom-call | flops 100000 | bytes 1000 | tf_op jit(solution)/shard_map/back/pallas_call | solution.py:54
  59.6 1.5 %collective-permute-done.5 = bf16[2,384,512]{2,1,0:T(8,128)(2,1)S(1)} collective-permute-done((bf16[2,384,512]{2,1,0:T(8,128)(2,1)}, bf16[2,384,512]{2,1,0:T(8,128)(2,1)S(1)}, u32[]{:S(2)}, u32[]{:S(2)}) %collective-permute-start.5) | collective-permute-done | bytes 786464 | tf_op jit(solution)/shard_map/ppermute | solution.py:600
  62.3 2.4 %collective-permute-start.8 = (bf16[2,2,96,512]{3,2,1,0:T(8,128)(2,1)}, bf16[2,2,96,512]{3,2,1,0:T(8,128)(2,1)}, u32[]{:S(2)}, u32[]{:S(2)}) collective-permute-start(bf16[2,2,96,512]{3,2,1,0:T(8,128)(2,1)} %get-tuple-element.129), channel_id=1, source_target_pairs={{0,4},{2,6},{4,0},{6,2},{8,12},{10,14},{12,8},{14,10},{1,5},{3,7},... | collective-permute-start | bytes 1179656 | tf_op jit(solution)/shard_map/ppermute | solution.py:600
  64.9 4.7 %norm_back.1 = (bf16[1024,384]{1,0:T(8,128)(2,1)S(1)}, bf16[3,32,384]{2,1,0:T(8,128)(2,1)S(1)}, bf16[3,32,384]{2,1,0:T(8,128)(2,1)}, f32[8,128]{1,0:T(8,128)S(1)}) custom-call(f32[8,128]{1,0:T(8,128)S(1)} %get-tuple-element.118.refs_0_, s32[8]{0:T(128)} %refs_1_.17, bf16[1024,384]{1,0:T(8,128)(2,1)} %bitcast.18, f32[1024,128]{1,0:T(8,128)} %copy-done.5, ...), custom_call_target="tpu_custom_call" | custom-call | flops 100000 | bytes 1000 | tf_op jit(solution)/shard_map/norm_back/pallas_call | solution.py:54
  69.6 3.4 %branch.1 = (f32[1024,384]{1,0:T(8,128)S(1)}, bf16[1024,256]{1,0:T(8,128)(2,1)S(1)}, bf16[1024,128]{1,0:T(8,128)(2,1)S(1)}, f32[8,128]{1,0:T(8,128)S(1)}) custom-call(f32[8,128]{1,0:T(8,128)S(1)} %get-tuple-element.123.refs_0_, bf16[768,1536]{1,0:T(8,128)(2,1)S(1)} %copy-done.1, bf16[1024,512]{1,0:T(8,128)(2,1)S(1)} %copy-done.6, ...), custom_call_target="tpu_custom_call" | custom-call | flops 100000 | bytes 1000 | tf_op jit(solution)/shard_map/branch/pallas_call | solution.py:54
  73.0 3.5 %collective-permute-start.9 = (bf16[3,32,384]{2,1,0:T(8,128)(2,1)S(1)}, bf16[3,32,384]{2,1,0:T(8,128)(2,1)S(1)}, u32[]{:S(2)}, u32[]{:S(2)}) collective-permute-start(bf16[3,32,384]{2,1,0:T(8,128)(2,1)S(1)} %get-tuple-element.132), channel_id=1, source_target_pairs={{0,8},{2,10},{4,12},{6,14},{8,0},{10,2},{12,4},{14,6},{1,9},{3,11}... | collective-permute-start | bytes 221192 | tf_op jit(solution)/shard_map/ppermute | solution.py:612
  77.8 3.1 %collective-permute-done.9.refs_3_ = bf16[3,32,384]{2,1,0:T(8,128)(2,1)S(1)} collective-permute-done((bf16[3,32,384]{2,1,0:T(8,128)(2,1)S(1)}, bf16[3,32,384]{2,1,0:T(8,128)(2,1)S(1)}, u32[]{:S(2)}, u32[]{:S(2)}) %collective-permute-start.9) | collective-permute-done | bytes 73760 | tf_op jit(solution)/shard_map/ppermute | solution.py:612
  82.0 2.1 %first.3 = (f32[2,2,96,512]{3,2,1,0:T(8,128)}, bf16[2,2,96,512]{3,2,1,0:T(8,128)(2,1)S(1)}, f32[8,128]{1,0:T(8,128)S(1)}) custom-call(f32[8,128]{1,0:T(8,128)S(1)} %get-tuple-element.133.refs_0_, bf16[2,4,96,512]{3,2,1,0:T(8,128)(2,1)S(1)} %bitcast.25, bf16[2,4,96,512]{3,2,1,0:T(8,128)(2,1)} %bitcast.6.refs_2_), custom_call_target="tpu_custom_call" | custom-call | flops 100000 | bytes 1000 | tf_op jit(solution)/shard_map/first/pallas_call | solution.py:54
  84.3 3.4 %collective-permute-start.11 = (bf16[2,96,512]{2,1,0:T(8,128)(2,1)S(1)}, bf16[2,96,512]{2,1,0:T(8,128)(2,1)S(1)}, u32[]{:S(2)}, u32[]{:S(2)}) collective-permute-start(bf16[2,96,512]{2,1,0:T(8,128)(2,1)S(1)} %get-tuple-element.140), channel_id=1, source_target_pairs={{0,8},{2,10},{4,12},{6,14},{8,0},{10,2},{12,4},{14,6},{1,9},{3,11}... | collective-permute-start | bytes 589832 | tf_op jit(solution)/shard_map/ppermute | solution.py:600
  87.6 8.2 %taps.1 = (f32[64,384]{1,0:T(8,128)S(1)}, f32[8,128]{1,0:T(8,128)S(1)}) custom-call(f32[8,128]{1,0:T(8,128)S(1)} %get-tuple-element.136.refs_0_, bf16[4,8,2,16,384]{4,3,2,1,0:T(8,128)(2,1)S(1)} %bitcast.20, bf16[3,608,1792]{2,1,0:T(8,128)(2,1)} %get-tuple-element.137.refs_2_), custom_call_target="tpu_custom_call" | custom-call | flops 100000 | bytes 1000 | tf_op jit(solution)/shard_map/taps/pallas_call | solution.py:54
  97.1 2.5 %block_out.1 = (bf16[1024,384]{1,0:T(8,128)(2,1)}, f32[8,128]{1,0:T(8,128)S(1)}) custom-call(f32[8,128]{1,0:T(8,128)S(1)} %get-tuple-element.141.refs_0_, s32[8]{0:T(128)} %refs_1_.17, bf16[1024,384]{1,0:T(8,128)(2,1)S(1)} %bitcast.14, f32[1024,384]{1,0:T(8,128)S(1)} %get-tuple-element.142.refs_3_, bf16[1024,256]{1,0:T(8,128)(2,1)S(1)} %collective-permute-done.12.refs_4_, ...), custom_call_target="tpu_custom_call" | custom-call | flops 100000 | bytes 1000 | tf_op jit(solution)/shard_map/block_out/pallas_call | solution.py:54
  100.9 3.4 %collective-permute-start.17 = (bf16[2,96,512]{2,1,0:T(8,128)(2,1)S(1)}, bf16[2,96,512]{2,1,0:T(8,128)(2,1)S(1)}, u32[]{:S(2)}, u32[]{:S(2)}) collective-permute-start(bf16[2,96,512]{2,1,0:T(8,128)(2,1)S(1)} %get-tuple-element.155), channel_id=1, source_target_pairs={{0,8},{2,10},{4,12},{6,14},{8,0},{10,2},{12,4},{14,6},{1,9},{3,11}... | collective-permute-start | bytes 589832 | tf_op jit(solution)/shard_map/ppermute | solution.py:600
  104.4 1.7 %collective-permute-start.18 = (bf16[160,384]{1,0:T(8,128)(2,1)S(1)}, bf16[160,384]{1,0:T(8,128)(2,1)S(1)}, u32[]{:S(2)}, u32[]{:S(2)}) collective-permute-start(bf16[160,384]{1,0:T(8,128)(2,1)S(1)} %get-tuple-element.157), channel_id=1, source_target_pairs={{0,2},{2,0},{4,6},{6,4},{8,10},{10,8},{12,14},{14,12},{1,3},{3,1},... | collective-permute-start | bytes 368648 | tf_op jit(solution)/shard_map/ppermute | solution.py:612
  106.8 2.9 %collective-permute-start.16 = (f32[64,384]{1,0:T(8,128)S(1)}, f32[64,384]{1,0:T(8,128)S(1)}, u32[]{:S(2)}, u32[]{:S(2)}) collective-permute-start(f32[64,384]{1,0:T(8,128)S(1)} %get-tuple-element.152.refs_3_), channel_id=1, source_target_pairs={{0,2},{2,0},{4,6},{6,4},{8,10},{10,8},{12,14},{14,12},{1,3},{3,1},... | collective-permute-start | bytes 294920 | tf_op jit(solution)/shard_map/ppermute | solution.py:600
  109.7 3.6 %collective-permute-done.16.refs_4_ = f32[64,384]{1,0:T(8,128)S(1)} collective-permute-done((f32[64,384]{1,0:T(8,128)S(1)}, f32[64,384]{1,0:T(8,128)S(1)}, u32[]{:S(2)}, u32[]{:S(2)}) %collective-permute-start.16) | collective-permute-done | bytes 98336 | tf_op jit(solution)/shard_map/ppermute | solution.py:600
  114.6 2.4 %collective-permute-start.20 = (bf16[1920,128]{1,0:T(8,128)(2,1)S(1)}, bf16[1920,128]{1,0:T(8,128)(2,1)S(1)}, u32[]{:S(2)}, u32[]{:S(2)}) collective-permute-start(bf16[1920,128]{1,0:T(8,128)(2,1)S(1)} %get-tuple-element.162), channel_id=1, source_target_pairs={{0,4},{2,6},{4,0},{6,2},{8,12},{10,14},{12,8},{14,10},{1,5},{3,7},... | collective-permute-start | bytes 1474568 | tf_op jit(solution)/shard_map/ppermute | solution.py:600
  117.1 8.8 %conv.3 = (bf16[4,8,2,16,384]{4,3,2,1,0:T(8,128)(2,1)}, f32[8,128]{1,0:T(8,128)S(1)}) custom-call(f32[8,128]{1,0:T(8,128)S(1)} %get-tuple-element.156.refs_0_, s32[8]{0:T(128)} %refs_1_.17, bf16[4,16,16,384]{3,2,1,0:T(8,128)(2,1)S(1)} %bitcast.21, bf16[3,32,384]{2,1,0:T(8,128)(2,1)S(1)} %collective-permute-done.9.refs_3_, ...), custom_call_target="tpu_custom_call" | custom-call | flops 10000000000 | bytes 100000000 | tf_op jit(solution)/shard_map/conv/pallas_call | solution.py:54
  126.1 2.2 %collective-permute-start.21 = (bf16[1152,128]{1,0:T(8,128)(2,1)S(1)}, bf16[1152,128]{1,0:T(8,128)(2,1)S(1)}, u32[]{:S(2)}, u32[]{:S(2)}) collective-permute-start(bf16[1152,128]{1,0:T(8,128)(2,1)S(1)} %get-tuple-element.168), channel_id=1, source_target_pairs={{0,8},{2,10},{4,12},{6,14},{8,0},{10,2},{12,4},{14,6},{1,9},{3,11}... | collective-permute-start | bytes 884744 | tf_op jit(solution)/shard_map/ppermute | solution.py:600
  128.3 11.1 %collective-permute-done.21.refs_5_ = bf16[1152,128]{1,0:T(8,128)(2,1)S(1)} collective-permute-done((bf16[1152,128]{1,0:T(8,128)(2,1)S(1)}, bf16[1152,128]{1,0:T(8,128)(2,1)S(1)}, u32[]{:S(2)}, u32[]{:S(2)}) %collective-permute-start.21) | collective-permute-done | bytes 294944 | tf_op jit(solution)/shard_map/ppermute | solution.py:600
  139.4 1.8 %last.1 = (f32[96,1536]{1,0:T(8,128)}, f32[96,1536]{1,0:T(8,128)}, f32[49,384]{1,0:T(8,128)}, f32[8,128]{1,0:T(8,128)}) custom-call(f32[8,128]{1,0:T(8,128)S(1)} %get-tuple-element.164.refs_0_, s32[8]{0:T(128)} %refs_1_.17, f32[2,96,512]{2,1,0:T(8,128)S(1)} %get-tuple-element.165.refs_2_, f32[2,96,512]{2,1,0:T(8,128)S(1)} %get-tuple-element.166.refs_3_, ...), custom_call_target="tpu_custom_call" | custom-call | flops 100000 | bytes 1000 | tf_op jit(solution)/shard_map/last/pallas_call | solution.py:54
  (87 shorter events, 16.3 us)
Async XLA Ops:
  1.3 10.7 %copy-start.3 = (bf16[4,16,16,384]{3,2,1,0:T(8,128)(2,1)S(1)}, bf16[4,16,16,384]{3,2,1,0:T(8,128)(2,1)}, u32[]{:S(2)}) copy-start(bf16[4,16,16,384]{3,2,1,0:T(8,128)(2,1)} %refs_2_.9) | copy-start | bytes 2359300
  3.5 4.0 %collective-permute-start = (bf16[1024,384]{1,0:T(8,128)(2,1)S(1)}, bf16[1024,384]{1,0:T(8,128)(2,1)S(1)}, u32[]{:S(2)}, u32[]{:S(2)}) collective-permute-start(bf16[1024,384]{1,0:T(8,128)(2,1)S(1)} %get-tuple-element.90.refs_1_), channel_id=1, source_target_pairs={{0,1},{1,0},{2,3},{3,2},{4,5},{5,4},{6,7},{7,6},{8,9},{9,8},{10,11... | collective-permute-start | bytes 2359304 | tf_op jit(solution)/shard_map/ppermute | solution.py:597
  3.9 8.1 %collective-permute-start.1 = (bf16[3,32,384]{2,1,0:T(8,128)(2,1)S(1)}, bf16[3,32,384]{2,1,0:T(8,128)(2,1)S(1)}, u32[]{:S(2)}, u32[]{:S(2)}) collective-permute-start(bf16[3,32,384]{2,1,0:T(8,128)(2,1)S(1)} %get-tuple-element.92), channel_id=1, source_target_pairs={{0,8},{2,10},{4,12},{6,14},{8,0},{10,2},{12,4},{14,6},{1,9},{3,11}... | collective-permute-start | bytes 221192 | tf_op jit(solution)/shard_map/ppermute | solution.py:612
  9.2 6.1 %copy-start.1 = (bf16[768,1536]{1,0:T(8,128)(2,1)S(1)}, bf16[768,1536]{1,0:T(8,128)(2,1)}, u32[]{:S(2)}) copy-start(bf16[768,1536]{1,0:T(8,128)(2,1)} %refs_1_.13) | copy-start | bytes 7077892
  12.9 5.2 %collective-permute-start.2 = (bf16[160,384]{1,0:T(8,128)(2,1)S(1)}, bf16[160,384]{1,0:T(8,128)(2,1)S(1)}, u32[]{:S(2)}, u32[]{:S(2)}) collective-permute-start(bf16[160,384]{1,0:T(8,128)(2,1)S(1)} %get-tuple-element.96), channel_id=1, source_target_pairs={{0,2},{2,0},{4,6},{6,4},{8,10},{10,8},{12,14},{14,12},{1,3},{3,1},... | collective-permute-start | bytes 368648 | tf_op jit(solution)/shard_map/ppermute | solution.py:612
  14.6 3.6 %collective-permute-start.3 = (bf16[160,384]{1,0:T(8,128)(2,1)S(1)}, bf16[160,384]{1,0:T(8,128)(2,1)S(1)}, u32[]{:S(2)}, u32[]{:S(2)}) collective-permute-start(bf16[160,384]{1,0:T(8,128)(2,1)S(1)} %get-tuple-element.97), channel_id=1, source_target_pairs={{2,4},{4,2},{10,12},{12,10},{3,5},{5,3},{11,13},{13,11},{18,20},{2... | collective-permute-start | bytes 368648 | tf_op jit(solution)/shard_map/ppermute | solution.py:612
  15.3 13.2 %copy-start.20 = (f32[1536]{0:T(1024)S(1)}, f32[1536]{0:T(1024)}, u32[]{:S(2)}) copy-start(f32[1536]{0:T(1024)} %param.19) | copy-start | bytes 18436
  28.4 25.5 %copy-start.4 = (bf16[4,8,2,16,384]{4,3,2,1,0:T(8,128)(2,1)}, bf16[4,8,2,16,384]{4,3,2,1,0:T(8,128)(2,1)S(1)}, u32[]{:S(2)}) copy-start(bf16[4,8,2,16,384]{4,3,2,1,0:T(8,128)(2,1)S(1)} %get-tuple-element.100) | copy-start | bytes 2359300
  28.4 2.3 %collective-permute-start.4 = (bf16[1024,384]{1,0:T(8,128)(2,1)S(1)}, bf16[1024,384]{1,0:T(8,128)(2,1)S(1)}, u32[]{:S(2)}, u32[]{:S(2)}) collective-permute-start(bf16[1024,384]{1,0:T(8,128)(2,1)S(1)} %bitcast.15), channel_id=1, source_target_pairs={{0,1},{1,0},{2,3},{3,2},{4,5},{5,4},{6,7},{7,6},{8,9},{9,8},{10,11... | collective-permute-start | bytes 2359304 | tf_op jit(solution)/shard_map/ppermute | solution.py:597
  32.4 21.5 %copy-start.5 = (f32[1024,128]{1,0:T(8,128)}, f32[1024,128]{1,0:T(8,128)S(1)}, u32[]{:S(2)}) copy-start(f32[1024,128]{1,0:T(8,128)S(1)} %get-tuple-element.111.refs_3_) | copy-start | bytes 1572868
  38.1 23.1 %collective-permute-start.5 = (bf16[2,384,512]{2,1,0:T(8,128)(2,1)}, bf16[2,384,512]{2,1,0:T(8,128)(2,1)S(1)}, u32[]{:S(2)}, u32[]{:S(2)}) collective-permute-start(bf16[2,384,512]{2,1,0:T(8,128)(2,1)} %get-tuple-element.117), channel_id=1, source_target_pairs={{0,2},{2,0},{4,6},{6,4},{8,10},{10,8},{12,14},{14,12},{1,3},{3,1},... | collective-permute-start | bytes 2359304 | tf_op jit(solution)/shard_map/ppermute | solution.py:600
  48.2 33.8 %collective-permute-start.10 = (bf16[2,384,512]{2,1,0:T(8,128)(2,1)}, bf16[2,384,512]{2,1,0:T(8,128)(2,1)}, u32[]{:S(2)}, u32[]{:S(2)}) collective-permute-start(bf16[2,384,512]{2,1,0:T(8,128)(2,1)} %get-tuple-element.135), channel_id=1, source_target_pairs={{0,2},{2,0},{4,6},{6,4},{8,10},{10,8},{12,14},{14,12},{1,3},{3,1},... | collective-permute-start | bytes 2359304 | tf_op jit(solution)/shard_map/ppermute | solution.py:600
  59.1 5.8 %collective-permute-start.6 = (bf16[1024,256]{1,0:T(8,128)(2,1)}, bf16[1024,256]{1,0:T(8,128)(2,1)}, u32[]{:S(2)}, u32[]{:S(2)}) collective-permute-start(bf16[1024,256]{1,0:T(8,128)(2,1)} %get-tuple-element.120), channel_id=1, source_target_pairs={{0,1},{1,0},{2,3},{3,2},{4,5},{5,4},{6,7},{7,6},{8,9},{9,8},{10,11... | collective-permute-start | bytes 1572872 | tf_op jit(solution)/shard_map/ppermute | solution.py:597
  59.1 5.7 %collective-permute-start.7 = (bf16[1024,256]{1,0:T(8,128)(2,1)}, bf16[1024,256]{1,0:T(8,128)(2,1)}, u32[]{:S(2)}, u32[]{:S(2)}) collective-permute-start(bf16[1024,256]{1,0:T(8,128)(2,1)} %get-tuple-element.121), channel_id=1, source_target_pairs={{0,1},{1,0},{2,3},{3,2},{4,5},{5,4},{6,7},{7,6},{8,9},{9,8},{10,11... | collective-permute-start | bytes 1572872 | tf_op jit(solution)/shard_map/ppermute | solution.py:597
  62.3 14.2 %collective-permute-start.8 = (bf16[2,2,96,512]{3,2,1,0:T(8,128)(2,1)}, bf16[2,2,96,512]{3,2,1,0:T(8,128)(2,1)}, u32[]{:S(2)}, u32[]{:S(2)}) collective-permute-start(bf16[2,2,96,512]{3,2,1,0:T(8,128)(2,1)} %get-tuple-element.129), channel_id=1, source_target_pairs={{0,4},{2,6},{4,0},{6,2},{8,12},{10,14},{12,8},{14,10},{1,5},{3,7},... | collective-permute-start | bytes 1179656 | tf_op jit(solution)/shard_map/ppermute | solution.py:600
  64.7 44.9 %collective-permute-start.15 = (bf16[2,384,512]{2,1,0:T(8,128)(2,1)}, bf16[2,384,512]{2,1,0:T(8,128)(2,1)}, u32[]{:S(2)}, u32[]{:S(2)}) collective-permute-start(bf16[2,384,512]{2,1,0:T(8,128)(2,1)} %get-tuple-element.151), channel_id=1, source_target_pairs={{0,2},{2,0},{4,6},{6,4},{8,10},{10,8},{12,14},{14,12},{1,3},{3,1},... | collective-permute-start | bytes 2359304 | tf_op jit(solution)/shard_map/ppermute | solution.py:600
  72.9 9.1 %copy-start.13 = (bf16[2,384,512]{2,1,0:T(8,128)(2,1)S(1)}, bf16[2,384,512]{2,1,0:T(8,128)(2,1)}, u32[]{:S(2)}) copy-start(bf16[2,384,512]{2,1,0:T(8,128)(2,1)} %copy-done.12) | copy-start | bytes 2359300
  72.9 24.1 %collective-permute-start.12 = (bf16[1024,256]{1,0:T(8,128)(2,1)S(1)}, bf16[1024,256]{1,0:T(8,128)(2,1)S(1)}, u32[]{:S(2)}, u32[]{:S(2)}) collective-permute-start(bf16[1024,256]{1,0:T(8,128)(2,1)S(1)} %get-tuple-element.143), channel_id=1, source_target_pairs={{0,1},{1,0},{2,3},{3,2},{4,5},{5,4},{6,7},{7,6},{8,9},{9,8},{10,11... | collective-permute-start | bytes 1572872 | tf_op jit(solution)/shard_map/ppermute | solution.py:597
  73.0 7.9 %collective-permute-start.9 = (bf16[3,32,384]{2,1,0:T(8,128)(2,1)S(1)}, bf16[3,32,384]{2,1,0:T(8,128)(2,1)S(1)}, u32[]{:S(2)}, u32[]{:S(2)}) collective-permute-start(bf16[3,32,384]{2,1,0:T(8,128)(2,1)S(1)} %get-tuple-element.132), channel_id=1, source_target_pairs={{0,8},{2,10},{4,12},{6,14},{8,0},{10,2},{12,4},{14,6},{1,9},{3,11}... | collective-permute-start | bytes 221192 | tf_op jit(solution)/shard_map/ppermute | solution.py:612
  84.1 15.5 %collective-permute-start.14 = (bf16[2,2,96,512]{3,2,1,0:T(8,128)(2,1)S(1)}, bf16[2,2,96,512]{3,2,1,0:T(8,128)(2,1)S(1)}, u32[]{:S(2)}, u32[]{:S(2)}) collective-permute-start(bf16[2,2,96,512]{3,2,1,0:T(8,128)(2,1)S(1)} %get-tuple-element.148), channel_id=1, source_target_pairs={{0,4},{2,6},{4,0},{6,2},{8,12},{10,14},{12,8},{14,10},{1,5},{3,7},... | collective-permute-start | bytes 1179656 | tf_op jit(solution)/shard_map/ppermute | solution.py:600
  84.3 12.8 %collective-permute-start.13 = (bf16[1024,128]{1,0:T(8,128)(2,1)S(1)}, bf16[1024,128]{1,0:T(8,128)(2,1)S(1)}, u32[]{:S(2)}, u32[]{:S(2)}) collective-permute-start(bf16[1024,128]{1,0:T(8,128)(2,1)S(1)} %get-tuple-element.144), channel_id=1, source_target_pairs={{0,1},{1,0},{2,3},{3,2},{4,5},{5,4},{6,7},{7,6},{8,9},{9,8},{10,11... | collective-permute-start | bytes 786440 | tf_op jit(solution)/shard_map/ppermute | solution.py:597
  84.3 12.8 %collective-permute-start.11 = (bf16[2,96,512]{2,1,0:T(8,128)(2,1)S(1)}, bf16[2,96,512]{2,1,0:T(8,128)(2,1)S(1)}, u32[]{:S(2)}, u32[]{:S(2)}) collective-permute-start(bf16[2,96,512]{2,1,0:T(8,128)(2,1)S(1)} %get-tuple-element.140), channel_id=1, source_target_pairs={{0,8},{2,10},{4,12},{6,14},{8,0},{10,2},{12,4},{14,6},{1,9},{3,11}... | collective-permute-start | bytes 589832 | tf_op jit(solution)/shard_map/ppermute | solution.py:600
  87.6 9.4 %copy-start.17 = (f32[384]{0:T(512)S(1)}, f32[384]{0:T(512)}, u32[]{:S(2)}) copy-start(f32[384]{0:T(512)} %refs_6_.1) | copy-start | bytes 4612
  87.6 9.5 %copy-start.19 = (f32[384]{0:T(512)S(1)}, f32[384]{0:T(512)}, u32[]{:S(2)}) copy-start(f32[384]{0:T(512)} %refs_7_.4) | copy-start | bytes 4612
  97.1 16.2 %copy-start.10 = (bf16[2,384,512]{2,1,0:T(8,128)(2,1)S(1)}, bf16[2,384,512]{2,1,0:T(8,128)(2,1)}, u32[]{:S(2)}) copy-start(bf16[2,384,512]{2,1,0:T(8,128)(2,1)} %copy-done.9) | copy-start | bytes 2359300
  99.6 17.5 %copy-start.11 = (bf16[4,16,16,384]{3,2,1,0:T(8,128)(2,1)S(1)}, bf16[4,16,16,384]{3,2,1,0:T(8,128)(2,1)}, u32[]{:S(2)}) copy-start(bf16[4,16,16,384]{3,2,1,0:T(8,128)(2,1)} %param.23) | copy-start | bytes 2359300
  100.9 16.1 %collective-permute-start.17 = (bf16[2,96,512]{2,1,0:T(8,128)(2,1)S(1)}, bf16[2,96,512]{2,1,0:T(8,128)(2,1)S(1)}, u32[]{:S(2)}, u32[]{:S(2)}) collective-permute-start(bf16[2,96,512]{2,1,0:T(8,128)(2,1)S(1)} %get-tuple-element.155), channel_id=1, source_target_pairs={{0,8},{2,10},{4,12},{6,14},{8,0},{10,2},{12,4},{14,6},{1,9},{3,11}... | collective-permute-start | bytes 589832 | tf_op jit(solution)/shard_map/ppermute | solution.py:600
  104.4 12.7 %collective-permute-start.18 = (bf16[160,384]{1,0:T(8,128)(2,1)S(1)}, bf16[160,384]{1,0:T(8,128)(2,1)S(1)}, u32[]{:S(2)}, u32[]{:S(2)}) collective-permute-start(bf16[160,384]{1,0:T(8,128)(2,1)S(1)} %get-tuple-element.157), channel_id=1, source_target_pairs={{0,2},{2,0},{4,6},{6,4},{8,10},{10,8},{12,14},{14,12},{1,3},{3,1},... | collective-permute-start | bytes 368648 | tf_op jit(solution)/shard_map/ppermute | solution.py:612
  106.1 11.0 %collective-permute-start.19 = (bf16[160,384]{1,0:T(8,128)(2,1)S(1)}, bf16[160,384]{1,0:T(8,128)(2,1)S(1)}, u32[]{:S(2)}, u32[]{:S(2)}) collective-permute-start(bf16[160,384]{1,0:T(8,128)(2,1)S(1)} %get-tuple-element.158), channel_id=1, source_target_pairs={{2,4},{4,2},{10,12},{12,10},{3,5},{5,3},{11,13},{13,11},{18,20},{2... | collective-permute-start | bytes 368648 | tf_op jit(solution)/shard_map/ppermute | solution.py:612
  106.8 6.5 %collective-permute-start.16 = (f32[64,384]{1,0:T(8,128)S(1)}, f32[64,384]{1,0:T(8,128)S(1)}, u32[]{:S(2)}, u32[]{:S(2)}) collective-permute-start(f32[64,384]{1,0:T(8,128)S(1)} %get-tuple-element.152.refs_3_), channel_id=1, source_target_pairs={{0,2},{2,0},{4,6},{6,4},{8,10},{10,8},{12,14},{14,12},{1,3},{3,1},... | collective-permute-start | bytes 294920 | tf_op jit(solution)/shard_map/ppermute | solution.py:600
  114.6 11.3 %collective-permute-start.20 = (bf16[1920,128]{1,0:T(8,128)(2,1)S(1)}, bf16[1920,128]{1,0:T(8,128)(2,1)S(1)}, u32[]{:S(2)}, u32[]{:S(2)}) collective-permute-start(bf16[1920,128]{1,0:T(8,128)(2,1)S(1)} %get-tuple-element.162), channel_id=1, source_target_pairs={{0,4},{2,6},{4,0},{6,2},{8,12},{10,14},{12,8},{14,10},{1,5},{3,7},... | collective-permute-start | bytes 1474568 | tf_op jit(solution)/shard_map/ppermute | solution.py:600
  126.1 13.3 %collective-permute-start.21 = (bf16[1152,128]{1,0:T(8,128)(2,1)S(1)}, bf16[1152,128]{1,0:T(8,128)(2,1)S(1)}, u32[]{:S(2)}, u32[]{:S(2)}) collective-permute-start(bf16[1152,128]{1,0:T(8,128)(2,1)S(1)} %get-tuple-element.168), channel_id=1, source_target_pairs={{0,8},{2,10},{4,12},{6,14},{8,0},{10,2},{12,4},{14,6},{1,9},{3,11}... | collective-permute-start | bytes 884744 | tf_op jit(solution)/shard_map/ppermute | solution.py:600
  (12 other events, 47.2 us)

commit v3 on v2

--- a/solution.py
+++ b/solution.py
@@ -164,8 +164,9 @@
         lefts = [lefts[c % 2] for c in range(blocks)]
         scratch = scratch[2:]
     else:
-        left_ref, image, *scratch = rest
-        lefts = [left_ref.at[c] for c in range(blocks)]
+        left_ref, image, windows_ref, sems, *scratch = rest
+        lefts = [windows_ref.at[c] for c in range(blocks)]
+        copies = [pltpu.make_async_copy(lefts[c], left_ref.at[c], sems.at[c]) for c in range(blocks)]
     weights = [scratch[c % 2] for c in range(blocks)]
     odd_row, odd_col, count = place(cols, tissue_ref)
     row_odd = (odd_row == 1).astype(F32)
@@ -250,8 +251,13 @@
                 for b in range(2 * q, min(2 * q + 2, KERNEL)):
                     windows(c, b)
                     diagonals(c, b)
+        if c < blocks and not backward:
+            copies[c].start()
         if c:
             finish(c - 1, acc)
+    if not backward:
+        for copy in copies:
+            copy.wait()
 
 
 def taps_body(g_ref, left_ref, out_ref, paired, sums):
@@ -414,26 +420,35 @@
 
 
 def branch_body(down_ref, *rest):
-    acts, (keep_ref, send_ref, more_ref) = rest[:CHUNKS], rest[CHUNKS:]
+    acts, (keep_ref, send_ref) = rest[:CHUNKS], rest[CHUNKS:]
     keep, send = split(lax.axis_index("tensor") == 1, turned_dot(acts, down_ref))
     keep_ref[...] = keep
-    cut = send_ref.shape[1]
-    send_ref[...] = send[:, :cut].astype(BF16)
-    more_ref[...] = send[:, cut:].astype(BF16)
+    send_ref[...] = send.astype(BF16)
 
 
 def first_body(keep_ref, got_ref, keep_out, send_out):
+    bit = lax.axis_index("space") // 4
+    for half in range(2):
+        for out_ref, at in ((keep_out, 2 * bit + half), (send_out, 2 * (1 - bit) + half)):
+            value = keep_ref[:, at].astype(F32) + got_ref[:, at].astype(F32)
+            out_ref[:, half] = value.astype(out_ref.dtype)
+
+
+def middle_body(keep_ref, got_ref, old_ref, old_got_ref, keep_out, send_out, old_out):
     bit = (lax.axis_index("space") // 2) % 2
     for half in range(2):
         for out_ref, at in ((keep_out, 2 * half + bit), (send_out, 2 * half + 1 - bit)):
             value = keep_ref[:, at].astype(F32) + got_ref[:, at].astype(F32)
             out_ref[:, half] = value.astype(out_ref.dtype)
-
-
-def second_body(keep_ref, got_ref, keep_out, send_out):
+    old_out[...] = old_ref[:, bit] + old_got_ref[:, bit].astype(F32)
+    send_out[:, 2] = (old_ref[:, 1 - bit] + old_got_ref[:, 1 - bit].astype(F32)).astype(BF16)
+
+
+def second_body(keep_ref, got_ref, old_ref, keep_out, send_out, old_out):
     bit = lax.axis_index("space") // 4
     keep_out[...] = keep_ref[:, bit] + got_ref[:, bit].astype(F32)
     send_out[...] = (keep_ref[:, 1 - bit] + got_ref[:, 1 - bit].astype(F32)).astype(BF16)
+    old_out[...] = old_ref[...] + got_ref[:, 2].astype(F32)
 
 
 def third_body(keep_ref, got_ref, out_ref):
@@ -441,24 +456,18 @@
 
 
 def put_taps(value, send_ref, at):
-    high = value.astype(BF16)
-    low = (value - high.astype(F32)).astype(BF16)
+    value = value.astype(BF16)
     rows = value.shape[0]
     for lanes in range(value.shape[1] // LANES):
-        cols = slice(lanes * LANES, (lanes + 1) * LANES)
-        send_ref[at : at + rows, :] = high[:, cols]
-        send_ref[at + rows : at + 2 * rows, :] = low[:, cols]
-        at += 2 * rows
-    return high.astype(F32) + low.astype(F32)
+        send_ref[at : at + rows, :] = value[:, lanes * LANES : (lanes + 1) * LANES]
+        at += rows
+    return value.astype(F32)
 
 
 def got_taps(got_ref, at, shape):
     rows, width = shape
-    parts = []
-    for lanes in range(width // LANES):
-        parts.append(got_ref[at : at + rows, :].astype(F32) + got_ref[at + rows : at + 2 * rows, :].astype(F32))
-        at += 2 * rows
-    return jnp.concatenate(parts, axis=1)
+    parts = [got_ref[at + k * rows : at + (k + 1) * rows, :] for k in range(width // LANES)]
+    return jnp.concatenate(parts, axis=1).astype(F32)
 
 
 def first_taps_body(keep_ref, got_ref, taps_ref, taps_got_ref, keep_out, send_out, taps_out):
@@ -517,11 +526,10 @@
     kernel_ref[...] = (total * scale)[: kernel_ref.shape[0]]
 
 
-def block_out_body(tissue_ref, x_ref, keep_ref, got_ref, more_ref, scale_ref, bias_ref, out_ref):
+def block_out_body(tissue_ref, x_ref, keep_ref, got_ref, scale_ref, bias_ref, out_ref):
     count = tissue_ref[lax.axis_index("space")]
     ok = (pl.program_id(0) < count).astype(F32)
-    got = jnp.concatenate([got_ref[...], more_ref[...]], axis=1).astype(F32)
-    branch = keep_ref[...] + got + bias_ref[...].reshape(1, -1)
+    branch = keep_ref[...] + got_ref[...].astype(F32) + bias_ref[...].reshape(1, -1)
     value = (x_ref[...].astype(F32) + scale_ref[...].reshape(1, -1) * branch) * ok
     out_ref[...] = value.astype(BF16)
 
@@ -637,7 +645,8 @@
         if backward:
             scratch += [pltpu.VMEM((1,) + left_shape[1:], BF16)] * 2
         else:
-            outs.append(whole(left_shape))
+            outs.append(pl.BlockSpec(memory_space=pltpu.HBM))
+            scratch += [pltpu.VMEM(left_shape, BF16), pltpu.SemaphoreType.DMA((blocks,))]
             shapes.append(hbm(left_shape, BF16))
         scratch += [pltpu.VMEM((4 * 1792, 256), BF16)] * 2
         return call(
@@ -664,7 +673,7 @@
         [smem(), whole(features.shape), whole((cells, chans)), whole((chans,))],
         [whole(rim_shape), whole(rim_shape), whole((cells, chans))],
         [sds(rim_shape, BF16), sds(rim_shape, BF16), sds((cells, chans), BF16)],
-        [], (tissue, pin(features), pin(cotangent.reshape(cells, chans)), layer_scale),
+        [], (tissue, pin(features), pin(cotangent.reshape(cells, chans)), pin(layer_scale)),
     )
     near = paired(near_send, True, 0)
     far = paired(far_send, True, 1)
@@ -676,7 +685,7 @@
         [whole((cells, chans)), whole((cells, chans)), at_chunk((total, width), 0)],
         [whole((cells, width)), whole((total, cells)), whole((cells, total))],
         [sds((cells, width), F32), sds((total, cells), BF16), sds((cells, total), BF16)],
-        [], (branch_grad, other_grad, w_down),
+        [], (branch_grad, other_grad, pin(w_down)),
     )
     one_send, two_send = sides(features, near, far, True)
     one = paired(one_send, False, 0)
@@ -729,22 +738,37 @@
         kept.append(keep)
         got.append(exchanged(send, 1) if stepped else send)
 
+    half_shape = (2, 2, per, width)
+    row_shape = (2, per, width)
+
     def first(k):
         if stepped:
             shape = (2, 4, per, width)
-            out = (2, 2, per, width)
             keep, send = call(
-                first_body, (1,), [whole(shape)] * 2, [whole(out)] * 2, [hbm(out, F32), sds(out, BF16)], [],
+                first_body, (1,), [whole(shape)] * 2, [whole(half_shape)] * 2,
+                [hbm(half_shape, F32), sds(half_shape, BF16)], [],
                 (kept[k].reshape(shape), got[k].reshape(shape)),
             )
+            kept[k], got[k] = keep, exchanged(send, 4)
+
+    def middle(k):
+        if stepped:
+            shape = (2, 4, per, width)
+            out = (2, 3, per, width)
+            keep, send, kept[k - 1] = call(
+                middle_body, (1,), [whole(shape)] * 2 + [whole(half_shape)] * 2,
+                [whole(half_shape), whole(out), whole(row_shape)],
+                [hbm(half_shape, F32), sds(out, BF16), hbm(row_shape, F32)], [],
+                (kept[k].reshape(shape), got[k].reshape(shape), pin(kept[k - 1]), got[k - 1]),
+            )
             kept[k], got[k] = keep, exchanged(send, 2)
 
     def second(k):
         if stepped:
-            out = (2, per, width)
-            keep, send = call(
-                second_body, (1,), [whole((2, 2, per, width))] * 2, [whole(out)] * 2, [sds(out, F32), sds(out, BF16)], [],
-                (pin(kept[k]), got[k]),
+            keep, send, kept[k - 1] = call(
+                second_body, (1,), [whole(half_shape), whole((2, 3, per, width)), whole(row_shape)], [whole(row_shape)] * 3,
+                [sds(row_shape, F32), sds(row_shape, BF16), sds(row_shape, F32)], [],
+                (pin(kept[k]), got[k], pin(kept[k - 1])),
             )
             kept[k], got[k] = keep, exchanged(send, 4)
 
@@ -788,7 +812,7 @@
     back_got = across(back_send), across(back_more)
     def first_taps(k):
         out = (2, 2, per, width)
-        rows = 4 * per * width // LANES + 2 * taps.shape[0] * blocks
+        rows = 4 * per * width // LANES + taps.shape[0] * blocks
         shape = (2, 4, per, width)
         keep, send, value = call(
             first_taps_body, (1,), [whole(shape)] * 2 + [whole(taps.shape)] * 2,
@@ -802,7 +826,7 @@
     def second_taps(k):
         out = (2, per, width)
         was = got[k].shape
-        rows = 2 * per * width // LANES + 2 * taps.shape[0] * blocks
+        rows = 2 * per * width // LANES + taps.shape[0] * blocks
         keep, send, value = call(
             second_taps_body, (1,), [whole((2, 2, per, width)), whole(was), whole(taps.shape)],
             [whole(out), whole((rows, LANES)), whole(taps.shape)],
@@ -824,21 +848,6 @@
     )
     near = paired(near_send, True, 0)
     far = paired(far_send, True, 1)
-    branch_keep, branch_send, branch_more = call(
-        branch_body,
-        (tiles_dev,),
-        [whole((total, units))] + chunk_rows,
-        [row_block, pl.BlockSpec((256, 2 * LANES), lambda i: (i, 0)), sums_spec],
-        [sds((cells, chans), F32), sds((cells, 2 * LANES), BF16), sds((cells, LANES), BF16)],
-        [], (w_down, *acts),
-    )
-    branch_got = across(branch_send), across(branch_more)
-    second(0)
-    conv_grad_tiles = conv_grad.reshape(features.shape)
-    one_send, two_send = sides(conv_grad_tiles, near, far, False)
-    one = paired(one_send, False, 0)
-    two = paired(two_send, False, 1)
-    first(1)
     (taps,) = call(
         taps_body,
         (blocks,),
@@ -849,26 +858,39 @@
         (conv_grad.reshape(split_shape), pin(left)),
     )
     taps_got = exchanged(taps, 1) if stepped else None
-    third(0)
+    conv_grad_tiles = conv_grad.reshape(features.shape)
+    one_send, two_send = sides(conv_grad_tiles, near, far, False)
+    one = paired(one_send, False, 0)
+    two = paired(two_send, False, 1)
+    middle(1)
+    if stepped:
+        taps = first_taps(2)
+    second(1)
+    branch_keep, branch_send = call(
+        branch_body,
+        (tiles_dev,),
+        [whole((total, units))] + chunk_rows,
+        [row_block, row_block],
+        [sds((cells, chans), F32), sds((cells, chans), BF16)],
+        [], (w_down, *acts),
+    )
+    branch_got = across(branch_send)
+    if stepped:
+        taps = second_taps(2)
+    third(1)
+    (grad_features,) = conv(
+        conv_grad_tiles, near, far, one, two, cotangent.reshape(split_shape), True
+    )
+    grad_features = grad_features.reshape(features.shape)
     (block_out,) = call(
         block_out_body,
         (tiles_dev,),
-        [smem(), row_block, row_block, pl.BlockSpec((256, 2 * LANES), lambda i: (i, 0)), sums_spec, whole((chans,)), whole((chans,))],
+        [smem(), row_block, row_block, row_block, whole((chans,)), whole((chans,))],
         [row_block],
         [sds((cells, chans), BF16)],
-        [], (tissue, features.reshape(cells, chans), branch_keep, *branch_got, layer_scale, down_bias),
+        [], (tissue, features.reshape(cells, chans), branch_keep, branch_got, layer_scale, down_bias),
     )
     block_out = block_out.reshape(features.shape)
-    second(1)
-    if stepped:
-        taps = first_taps(2)
-    third(1)
-    (grad_features,) = conv(
-        conv_grad_tiles, near, far, one, two, cotangent.reshape(split_shape), True
-    )
-    grad_features = grad_features.reshape(features.shape)
-    if stepped:
-        taps = second_taps(2)
     if stepped:
         kernel_shape = (KERNEL * KERNEL, chans)
         grad_down, grad_up, grad_kernel = call(

time: 142 us -> 134 us (0.944)
  starting transfers between devices: 34.3 us -> 23.6 us
  waiting for transfers between devices: 25.4 us -> 30.3 us
    ppermute x10 -> x9, starting transfers between devices: 21.5 us -> 15.3 us  [exchanged(): return lax.ppermute(value, 'space', [(d, d ^ bit) for d in range(devices)])]
    ppermute x6, waiting for transfers between devices: 6.63 us -> 11.7 us  [paired(): return lax.ppermute(value, 'space', pairs)]
    ppermute x6, starting transfers between devices: 11.7 us -> 7.19 us  [paired(): return lax.ppermute(value, 'space', pairs)]
    pallas_call x26 -> x24, Pallas kernels: 78 us -> 77.1 us  [__call__(): pl.pallas_call(run, grid=grid, in_specs=[pl.BlockSpec(memory_space=pl.ANY...]
    ppermute x10 -> x9, waiting for transfers between devices: 17.5 us -> 17.3 us  [exchanged(): return lax.ppermute(value, 'space', [(d, d ^ bit) for d in range(devices)])]
  transfers between devices with their start and end apart: 22 -> 20, of which waited for: 8 -> 8; matrix products, arithmetic and copies ran while one was open for 0% -> 0% of each run, Pallas kernels for 39% -> 42%
where the time goes in v3:
time: 134 us; the launch traced here: 133 us
  Pallas kernels  77.1 us (58%)
  waiting for transfers between devices  30.3 us (23%)
  starting transfers between devices  23.6 us (18%)
    pallas_call x24, Pallas kernels, __call__(): pl.pallas_call(run, grid=grid, in_specs=[pl.BlockSpec(memory_space=pl.ANY...  77.1 us
    ppermute x9, waiting for transfers between devices, exchanged(): return lax.ppermute(value, 'space', [(d, d ^ bit) for d in range(devices)])  17.3 us
    ppermute x9, starting transfers between devices, exchanged(): return lax.ppermute(value, 'space', [(d, d ^ bit) for d in range(devices)])  15.3 us
    ppermute x6, waiting for transfers between devices, paired(): return lax.ppermute(value, 'space', pairs)  11.7 us
    ppermute x6, starting transfers between devices, paired(): return lax.ppermute(value, 'space', pairs)  7.19 us
  transfers between devices with their start and end apart: 20, of which 8 were waited for; matrix products, arithmetic and copies ran while one was open for 0% of the time, Pallas kernels for 42%

profile of v3, /device:TPU:0, one launch (start us, length us, event | category | flops | bytes accessed | tf_op | source)
XLA Modules:
  0.0 133.2 jit_solution(10121153604369094326)
XLA Ops:
  0.6 2.1 %rims.1 = (bf16[3,32,384]{2,1,0:T(8,128)(2,1)S(1)}, bf16[3,32,384]{2,1,0:T(8,128)(2,1)}, bf16[1024,384]{1,0:T(8,128)(2,1)S(1)}, f32[8,128]{1,0:T(8,128)S(1)}) custom-call(s32[8]{0:T(128)} %refs_1_.17, bf16[4,16,16,384]{3,2,1,0:T(8,128)(2,1)} %refs_2_.9, bf16[1024,384]{1,0:T(8,128)(2,1)} %bitcast.23, f32[384]{0:T(512)} %refs_5_.3), custom_call_target="tpu_custom_call" | custom-call | flops 100000 | bytes 1000 | tf_op jit(solution)/shard_map/rims/pallas_call | solution.py:54
  3.2 3.6 %collective-permute-start.1 = (bf16[3,32,384]{2,1,0:T(8,128)(2,1)S(1)}, bf16[3,32,384]{2,1,0:T(8,128)(2,1)S(1)}, u32[]{:S(2)}, u32[]{:S(2)}) collective-permute-start(bf16[3,32,384]{2,1,0:T(8,128)(2,1)S(1)} %get-tuple-element.88), channel_id=1, source_target_pairs={{0,8},{2,10},{4,12},{6,14},{8,0},{10,2},{12,4},{14,6},{1,9},{3,11}... | collective-permute-start | bytes 221192 | tf_op jit(solution)/shard_map/ppermute | solution.py:620
  6.8 2.4 %grad_in.1 = (f32[1024,512]{1,0:T(8,128)S(1)}, bf16[768,1024]{1,0:T(8,128)(2,1)S(1)}, bf16[1024,768]{1,0:T(8,128)(2,1)S(1)}, f32[8,128]{1,0:T(8,128)S(1)}) custom-call(f32[8,128]{1,0:T(8,128)S(1)} %get-tuple-element.85.refs_0_, bf16[1024,384]{1,0:T(8,128)(2,1)S(1)} %get-tuple-element.86.refs_1_, bf16[1024,384]{1,0:T(8,128)(2,1)S(1)} %collective-permute-done.refs_2_, ...), custom_call_target="tpu_custom_call" | custom-call | flops 100000 | bytes 1000 | tf_op jit(solution)/shard_map/grad_in/pallas_call | solution.py:54
  9.2 2.1 %collective-permute-done.1.refs_3_ = bf16[3,32,384]{2,1,0:T(8,128)(2,1)S(1)} collective-permute-done((bf16[3,32,384]{2,1,0:T(8,128)(2,1)S(1)}, bf16[3,32,384]{2,1,0:T(8,128)(2,1)S(1)}, u32[]{:S(2)}, u32[]{:S(2)}) %collective-permute-start.1) | collective-permute-done | bytes 73760 | tf_op jit(solution)/shard_map/ppermute | solution.py:620
  12.2 1.6 %collective-permute-start.2 = (bf16[160,384]{1,0:T(8,128)(2,1)S(1)}, bf16[160,384]{1,0:T(8,128)(2,1)S(1)}, u32[]{:S(2)}, u32[]{:S(2)}) collective-permute-start(bf16[160,384]{1,0:T(8,128)(2,1)S(1)} %get-tuple-element.92), channel_id=1, source_target_pairs={{0,2},{2,0},{4,6},{6,4},{8,10},{10,8},{12,14},{14,12},{1,3},{3,1},... | collective-permute-start | bytes 368648 | tf_op jit(solution)/shard_map/ppermute | solution.py:620
  15.5 1.9 %collective-permute-done.2.refs_5_ = bf16[160,384]{1,0:T(8,128)(2,1)S(1)} collective-permute-done((bf16[160,384]{1,0:T(8,128)(2,1)S(1)}, bf16[160,384]{1,0:T(8,128)(2,1)S(1)}, u32[]{:S(2)}, u32[]{:S(2)}) %collective-permute-start.2) | collective-permute-done | bytes 122912 | tf_op jit(solution)/shard_map/ppermute | solution.py:620
  17.4 9.1 %conv.2 = (bf16[4,8,2,16,384]{4,3,2,1,0:T(8,128)(2,1)S(1)}, bf16[3,608,1792]{2,1,0:T(8,128)(2,1)}, f32[8,128]{1,0:T(8,128)S(1)}) custom-call(f32[8,128]{1,0:T(8,128)S(1)} %get-tuple-element.91.refs_0_, s32[8]{0:T(128)} %refs_1_.17, bf16[4,16,16,384]{3,2,1,0:T(8,128)(2,1)S(1)} %copy-done.2, bf16[3,32,384]{2,1,0:T(8,128)(2,1)S(1)} %collective-permute-done.1.refs_3_, ...), custom_call_target="tpu_custom_call" | custom-call | flops 100000 | bytes 1000 | tf_op jit(solution)/shard_map/conv/pallas_call | solution.py:54
  27.7 1.3 collective-permute-done.4.refs_2_
  28.9 1.6 %norm.1 = (bf16[1024,768]{1,0:T(8,128)(2,1)S(1)}, bf16[768,1024]{1,0:T(8,128)(2,1)S(1)}, f32[1024,128]{1,0:T(8,128)S(1)}, f32[8,128]{1,0:T(8,128)S(1)}) custom-call(f32[8,128]{1,0:T(8,128)S(1)} %get-tuple-element.95.refs_0_, bf16[1024,384]{1,0:T(8,128)(2,1)S(1)} %bitcast.16, bf16[1024,384]{1,0:T(8,128)(2,1)S(1)} %collective-permute-done.4.refs_2_, ...), custom_call_target="tpu_custom_call" | custom-call | flops 100000 | bytes 1000 | tf_op jit(solution)/shard_map/norm/pallas_call | solution.py:54
  30.6 5.7 %chunk.3 = (bf16[1024,512]{1,0:T(8,128)(2,1)}, bf16[1024,512]{1,0:T(8,128)(2,1)S(1)}, bf16[2,384,512]{2,1,0:T(8,128)(2,1)S(1)}, bf16[2,384,512]{2,1,0:T(8,128)(2,1)}, f32[8,128]{1,0:T(8,128)S(1)}) custom-call(f32[8,128]{1,0:T(8,128)S(1)} %get-tuple-element.97.refs_0_, bf16[1024,768]{1,0:T(8,128)(2,1)S(1)} %get-tuple-element.98.refs_1_, ...), custom_call_target="tpu_custom_call" | custom-call | flops 100000 | bytes 1000 | tf_op jit(solution)/shard_map/chunk/pallas_call | solution.py:54
  36.3 4.5 %collective-permute-start.5 = (bf16[2,384,512]{2,1,0:T(8,128)(2,1)}, bf16[2,384,512]{2,1,0:T(8,128)(2,1)S(1)}, u32[]{:S(2)}, u32[]{:S(2)}) collective-permute-start(bf16[2,384,512]{2,1,0:T(8,128)(2,1)} %get-tuple-element.113), channel_id=1, source_target_pairs={{0,2},{2,0},{4,6},{6,4},{8,10},{10,8},{12,14},{14,12},{1,3},{3,1},... | collective-permute-start | bytes 2359304 | tf_op jit(solution)/shard_map/ppermute | solution.py:608
  40.9 5.6 %chunk.4 = (bf16[1024,512]{1,0:T(8,128)(2,1)}, bf16[1024,512]{1,0:T(8,128)(2,1)S(1)}, bf16[2,384,512]{2,1,0:T(8,128)(2,1)S(1)}, bf16[2,384,512]{2,1,0:T(8,128)(2,1)}, f32[8,128]{1,0:T(8,128)S(1)}) custom-call(f32[8,128]{1,0:T(8,128)S(1)} %get-tuple-element.102.refs_0_, bf16[1024,768]{1,0:T(8,128)(2,1)S(1)} %get-tuple-element.98.refs_1_, ...), custom_call_target="tpu_custom_call" | custom-call | flops 100000 | bytes 1000 | tf_op jit(solution)/shard_map/chunk/pallas_call | solution.py:54
  47.4 5.6 %chunk.5 = (bf16[1024,512]{1,0:T(8,128)(2,1)}, bf16[1024,512]{1,0:T(8,128)(2,1)S(1)}, bf16[2,384,512]{2,1,0:T(8,128)(2,1)S(1)}, bf16[2,384,512]{2,1,0:T(8,128)(2,1)}, f32[8,128]{1,0:T(8,128)S(1)}) custom-call(f32[8,128]{1,0:T(8,128)S(1)} %get-tuple-element.104.refs_0_, bf16[1024,768]{1,0:T(8,128)(2,1)S(1)} %get-tuple-element.98.refs_1_, ...), custom_call_target="tpu_custom_call" | custom-call | flops 100000 | bytes 1000 | tf_op jit(solution)/shard_map/chunk/pallas_call | solution.py:54
  53.0 5.2 %back.1 = (f32[1024,384]{1,0:T(8,128)}, bf16[1024,256]{1,0:T(8,128)(2,1)}, bf16[1024,256]{1,0:T(8,128)(2,1)}, f32[1024,128]{1,0:T(8,128)}, f32[8,128]{1,0:T(8,128)S(1)}) custom-call(f32[8,128]{1,0:T(8,128)S(1)} %get-tuple-element.106.refs_0_, bf16[1024,384]{1,0:T(8,128)(2,1)S(1)} %bitcast.17, bf16[1024,384]{1,0:T(8,128)(2,1)S(1)} %collective-permute-done.4.refs_2_, ...), custom_call_target="tpu_custom_call" | custom-call | flops 100000 | bytes 1000 | tf_op jit(solution)/shard_map/back/pallas_call | solution.py:54
  58.8 2.0 %collective-permute-start.11 = (bf16[2,384,512]{2,1,0:T(8,128)(2,1)}, bf16[2,384,512]{2,1,0:T(8,128)(2,1)}, u32[]{:S(2)}, u32[]{:S(2)}) collective-permute-start(bf16[2,384,512]{2,1,0:T(8,128)(2,1)} %get-tuple-element.131), channel_id=1, source_target_pairs={{0,2},{2,0},{4,6},{6,4},{8,10},{10,8},{12,14},{14,12},{1,3},{3,1},... | collective-permute-start | bytes 2359304 | tf_op jit(solution)/shard_map/ppermute | solution.py:608
  62.0 2.6 %collective-permute-start.10 = (bf16[2,2,96,512]{3,2,1,0:T(8,128)(2,1)}, bf16[2,2,96,512]{3,2,1,0:T(8,128)(2,1)}, u32[]{:S(2)}, u32[]{:S(2)}) collective-permute-start(bf16[2,2,96,512]{3,2,1,0:T(8,128)(2,1)} %get-tuple-element.128), channel_id=1, source_target_pairs={{0,8},{2,10},{4,12},{6,14},{8,0},{10,2},{12,4},{14,6},{1,9},{3,11}... | collective-permute-start | bytes 1179656 | tf_op jit(solution)/shard_map/ppermute | solution.py:608
  64.6 4.6 %norm_back.1 = (bf16[1024,384]{1,0:T(8,128)(2,1)S(1)}, bf16[3,32,384]{2,1,0:T(8,128)(2,1)S(1)}, bf16[3,32,384]{2,1,0:T(8,128)(2,1)}, f32[8,128]{1,0:T(8,128)S(1)}) custom-call(f32[8,128]{1,0:T(8,128)S(1)} %get-tuple-element.114.refs_0_, s32[8]{0:T(128)} %refs_1_.17, bf16[1024,384]{1,0:T(8,128)(2,1)} %bitcast.18, f32[1024,128]{1,0:T(8,128)} %copy-done.4, ...), custom_call_target="tpu_custom_call" | custom-call | flops 100000 | bytes 1000 | tf_op jit(solution)/shard_map/norm_back/pallas_call | solution.py:54
  69.5 8.2 %taps.1 = (f32[64,384]{1,0:T(8,128)S(1)}, f32[8,128]{1,0:T(8,128)S(1)}) custom-call(f32[8,128]{1,0:T(8,128)S(1)} %get-tuple-element.119.refs_0_, bf16[4,8,2,16,384]{4,3,2,1,0:T(8,128)(2,1)S(1)} %bitcast.19, bf16[3,608,1792]{2,1,0:T(8,128)(2,1)} %get-tuple-element.121.refs_2_), custom_call_target="tpu_custom_call" | custom-call | flops 100000 | bytes 1000 | tf_op jit(solution)/shard_map/taps/pallas_call | solution.py:54
  77.8 7.7 %collective-permute-done.8.refs_3_ = bf16[3,32,384]{2,1,0:T(8,128)(2,1)S(1)} collective-permute-done((bf16[3,32,384]{2,1,0:T(8,128)(2,1)S(1)}, bf16[3,32,384]{2,1,0:T(8,128)(2,1)S(1)}, u32[]{:S(2)}, u32[]{:S(2)}) %collective-permute-start.8) | collective-permute-done | bytes 73760 | tf_op jit(solution)/shard_map/ppermute | solution.py:620
  86.6 2.6 %middle.1 = (f32[2,2,96,512]{3,2,1,0:T(8,128)}, bf16[2,3,96,512]{3,2,1,0:T(8,128)(2,1)S(1)}, f32[2,96,512]{2,1,0:T(8,128)}, f32[8,128]{1,0:T(8,128)S(1)}) custom-call(f32[8,128]{1,0:T(8,128)S(1)} %get-tuple-element.124.refs_0_, bf16[2,4,96,512]{3,2,1,0:T(8,128)(2,1)S(1)} %bitcast.27, bf16[2,4,96,512]{3,2,1,0:T(8,128)(2,1)} %bitcast.7.refs_2_, ...), custom_call_target="tpu_custom_call" | custom-call | flops 100000 | bytes 1000 | tf_op jit(solution)/shard_map/middle/pallas_call | solution.py:54
  90.2 2.9 %collective-permute-done.11 = bf16[2,384,512]{2,1,0:T(8,128)(2,1)} collective-permute-done((bf16[2,384,512]{2,1,0:T(8,128)(2,1)}, bf16[2,384,512]{2,1,0:T(8,128)(2,1)}, u32[]{:S(2)}, u32[]{:S(2)}) %collective-permute-start.11) | collective-permute-done | bytes 786464 | tf_op jit(solution)/shard_map/ppermute | solution.py:608
  93.1 1.7 %collective-permute-done.12.refs_4_ = f32[64,384]{1,0:T(8,128)S(1)} collective-permute-done((f32[64,384]{1,0:T(8,128)S(1)}, f32[64,384]{1,0:T(8,128)S(1)}, u32[]{:S(2)}, u32[]{:S(2)}) %collective-permute-start.12) | collective-permute-done | bytes 98336 | tf_op jit(solution)/shard_map/ppermute | solution.py:608
  94.7 1.3 first_taps.1
  96.0 2.2 %collective-permute-start.14 = (bf16[1728,128]{1,0:T(8,128)(2,1)S(1)}, bf16[1728,128]{1,0:T(8,128)(2,1)S(1)}, u32[]{:S(2)}, u32[]{:S(2)}) collective-permute-start(bf16[1728,128]{1,0:T(8,128)(2,1)S(1)} %get-tuple-element.143), channel_id=1, source_target_pairs={{0,4},{2,6},{4,0},{6,2},{8,12},{10,14},{12,8},{14,10},{1,5},{3,7},... | collective-permute-start | bytes 1327112 | tf_op jit(solution)/shard_map/ppermute | solution.py:608
  98.2 7.3 %collective-permute-done.13.refs_2_ = bf16[2,3,96,512]{3,2,1,0:T(8,128)(2,1)S(1)} collective-permute-done((bf16[2,3,96,512]{3,2,1,0:T(8,128)(2,1)S(1)}, bf16[2,3,96,512]{3,2,1,0:T(8,128)(2,1)S(1)}, u32[]{:S(2)}, u32[]{:S(2)}) %collective-permute-start.13) | collective-permute-done | bytes 589856 | tf_op jit(solution)/shard_map/ppermute | solution.py:608
  105.5 1.4 %second.1 = (f32[2,96,512]{2,1,0:T(8,128)S(1)}, bf16[2,96,512]{2,1,0:T(8,128)(2,1)S(1)}, f32[2,96,512]{2,1,0:T(8,128)S(1)}, f32[8,128]{1,0:T(8,128)S(1)}) custom-call(f32[8,128]{1,0:T(8,128)S(1)} %get-tuple-element.133.refs_0_, f32[2,2,96,512]{3,2,1,0:T(8,128)} %get-tuple-element.134.refs_1_, bf16[2,3,96,512]{3,2,1,0:T(8,128)(2,1)S(1)} %collective-permute-done.13.refs_2_, ...), custom_call_target="tpu_custom_call" | custom-call | flops 100000 | bytes 1000 | tf_op jit(solution)/shard_map/second/pallas_call | solution.py:54
  106.9 2.0 %collective-permute-start.15 = (bf16[2,96,512]{2,1,0:T(8,128)(2,1)S(1)}, bf16[2,96,512]{2,1,0:T(8,128)(2,1)S(1)}, u32[]{:S(2)}, u32[]{:S(2)}) collective-permute-start(bf16[2,96,512]{2,1,0:T(8,128)(2,1)S(1)} %get-tuple-element.147), channel_id=1, source_target_pairs={{0,8},{2,10},{4,12},{6,14},{8,0},{10,2},{12,4},{14,6},{1,9},{3,11}... | collective-permute-start | bytes 589832 | tf_op jit(solution)/shard_map/ppermute | solution.py:608
  109.8 3.4 %branch.1 = (f32[1024,384]{1,0:T(8,128)S(1)}, bf16[1024,384]{1,0:T(8,128)(2,1)S(1)}, f32[8,128]{1,0:T(8,128)S(1)}) custom-call(f32[8,128]{1,0:T(8,128)S(1)} %get-tuple-element.137.refs_0_, bf16[768,1536]{1,0:T(8,128)(2,1)S(1)} %copy-done, bf16[1024,512]{1,0:T(8,128)(2,1)S(1)} %copy-done.5, bf16[1024,512]{1,0:T(8,128)(2,1)S(1)} %copy-done.6, ...), custom_call_target="tpu_custom_call" | custom-call | flops 100000 | bytes 1000 | tf_op jit(solution)/shard_map/branch/pallas_call | solution.py:54
  113.3 5.5 %collective-permute-done.14.refs_2_ = bf16[1728,128]{1,0:T(8,128)(2,1)S(1)} collective-permute-done((bf16[1728,128]{1,0:T(8,128)(2,1)S(1)}, bf16[1728,128]{1,0:T(8,128)(2,1)S(1)}, u32[]{:S(2)}, u32[]{:S(2)}) %collective-permute-start.14) | collective-permute-done | bytes 442400 | tf_op jit(solution)/shard_map/ppermute | solution.py:608
  120.0 8.9 %conv.3 = (bf16[4,8,2,16,384]{4,3,2,1,0:T(8,128)(2,1)}, f32[8,128]{1,0:T(8,128)S(1)}) custom-call(f32[8,128]{1,0:T(8,128)S(1)} %get-tuple-element.148.refs_0_, s32[8]{0:T(128)} %refs_1_.17, bf16[4,16,16,384]{3,2,1,0:T(8,128)(2,1)S(1)} %bitcast.21, bf16[3,32,384]{2,1,0:T(8,128)(2,1)S(1)} %collective-permute-done.8.refs_3_, ...), custom_call_target="tpu_custom_call" | custom-call | flops 10000000000 | bytes 100000000 | tf_op jit(solution)/shard_map/conv/pallas_call | solution.py:54
  129.0 2.4 %block_out.1 = (bf16[1024,384]{1,0:T(8,128)(2,1)}, f32[8,128]{1,0:T(8,128)S(1)}) custom-call(f32[8,128]{1,0:T(8,128)S(1)} %get-tuple-element.151.refs_0_, s32[8]{0:T(128)} %refs_1_.17, bf16[1024,384]{1,0:T(8,128)(2,1)S(1)} %bitcast.14, f32[1024,384]{1,0:T(8,128)S(1)} %get-tuple-element.152.refs_3_, bf16[1024,384]{1,0:T(8,128)(2,1)S(1)} %collective-permute-done.18.refs_4_, ...), custom_call_target="tpu_custom_call" | custom-call | flops 100000 | bytes 1000 | tf_op jit(solution)/shard_map/block_out/pallas_call | solution.py:54
  131.4 1.8 %last.1 = (f32[96,1536]{1,0:T(8,128)}, f32[96,1536]{1,0:T(8,128)}, f32[49,384]{1,0:T(8,128)}, f32[8,128]{1,0:T(8,128)}) custom-call(f32[8,128]{1,0:T(8,128)S(1)} %get-tuple-element.156.refs_0_, s32[8]{0:T(128)} %refs_1_.17, f32[2,96,512]{2,1,0:T(8,128)S(1)} %get-tuple-element.157.refs_2_, f32[2,96,512]{2,1,0:T(8,128)S(1)} %get-tuple-element.158.refs_3_, ...), custom_call_target="tpu_custom_call" | custom-call | flops 100000 | bytes 1000 | tf_op jit(solution)/shard_map/last/pallas_call | solution.py:54
  (77 shorter events, 11.5 us)
Async XLA Ops:
  2.7 8.6 %copy-start.2 = (bf16[4,16,16,384]{3,2,1,0:T(8,128)(2,1)S(1)}, bf16[4,16,16,384]{3,2,1,0:T(8,128)(2,1)}, u32[]{:S(2)}) copy-start(bf16[4,16,16,384]{3,2,1,0:T(8,128)(2,1)} %refs_2_.9) | copy-start | bytes 2359300
  2.7 4.0 %collective-permute-start = (bf16[1024,384]{1,0:T(8,128)(2,1)S(1)}, bf16[1024,384]{1,0:T(8,128)(2,1)S(1)}, u32[]{:S(2)}, u32[]{:S(2)}) collective-permute-start(bf16[1024,384]{1,0:T(8,128)(2,1)S(1)} %get-tuple-element.86.refs_1_), channel_id=1, source_target_pairs={{0,1},{1,0},{2,3},{3,2},{4,5},{5,4},{6,7},{7,6},{8,9},{9,8},{10,11... | collective-permute-start | bytes 2359304 | tf_op jit(solution)/shard_map/ppermute | solution.py:605
  3.2 8.1 %collective-permute-start.1 = (bf16[3,32,384]{2,1,0:T(8,128)(2,1)S(1)}, bf16[3,32,384]{2,1,0:T(8,128)(2,1)S(1)}, u32[]{:S(2)}, u32[]{:S(2)}) collective-permute-start(bf16[3,32,384]{2,1,0:T(8,128)(2,1)S(1)} %get-tuple-element.88), channel_id=1, source_target_pairs={{0,8},{2,10},{4,12},{6,14},{8,0},{10,2},{12,4},{14,6},{1,9},{3,11}... | collective-permute-start | bytes 221192 | tf_op jit(solution)/shard_map/ppermute | solution.py:620
  12.2 5.2 %collective-permute-start.2 = (bf16[160,384]{1,0:T(8,128)(2,1)S(1)}, bf16[160,384]{1,0:T(8,128)(2,1)S(1)}, u32[]{:S(2)}, u32[]{:S(2)}) collective-permute-start(bf16[160,384]{1,0:T(8,128)(2,1)S(1)} %get-tuple-element.92), channel_id=1, source_target_pairs={{0,2},{2,0},{4,6},{6,4},{8,10},{10,8},{12,14},{14,12},{1,3},{3,1},... | collective-permute-start | bytes 368648 | tf_op jit(solution)/shard_map/ppermute | solution.py:620
  13.8 3.6 %collective-permute-start.3 = (bf16[160,384]{1,0:T(8,128)(2,1)S(1)}, bf16[160,384]{1,0:T(8,128)(2,1)S(1)}, u32[]{:S(2)}, u32[]{:S(2)}) collective-permute-start(bf16[160,384]{1,0:T(8,128)(2,1)S(1)} %get-tuple-element.93), channel_id=1, source_target_pairs={{2,4},{4,2},{10,12},{12,10},{3,5},{5,3},{11,13},{13,11},{18,20},{2... | collective-permute-start | bytes 368648 | tf_op jit(solution)/shard_map/ppermute | solution.py:620
  14.5 12.2 %copy-start.18 = (f32[1536]{0:T(1024)S(1)}, f32[1536]{0:T(1024)}, u32[]{:S(2)}) copy-start(f32[1536]{0:T(1024)} %param.19) | copy-start | bytes 18436
  26.6 26.5 %copy-start.3 = (bf16[4,8,2,16,384]{4,3,2,1,0:T(8,128)(2,1)}, bf16[4,8,2,16,384]{4,3,2,1,0:T(8,128)(2,1)S(1)}, u32[]{:S(2)}) copy-start(bf16[4,8,2,16,384]{4,3,2,1,0:T(8,128)(2,1)S(1)} %get-tuple-element.96) | copy-start | bytes 2359300
  26.6 2.4 %collective-permute-start.4 = (bf16[1024,384]{1,0:T(8,128)(2,1)S(1)}, bf16[1024,384]{1,0:T(8,128)(2,1)S(1)}, u32[]{:S(2)}, u32[]{:S(2)}) collective-permute-start(bf16[1024,384]{1,0:T(8,128)(2,1)S(1)} %bitcast.15), channel_id=1, source_target_pairs={{0,1},{1,0},{2,3},{3,2},{4,5},{5,4},{6,7},{7,6},{8,9},{9,8},{10,11... | collective-permute-start | bytes 2359304 | tf_op jit(solution)/shard_map/ppermute | solution.py:605
  30.6 22.5 %copy-start.4 = (f32[1024,128]{1,0:T(8,128)}, f32[1024,128]{1,0:T(8,128)S(1)}, u32[]{:S(2)}) copy-start(f32[1024,128]{1,0:T(8,128)S(1)} %get-tuple-element.107.refs_3_) | copy-start | bytes 1572868
  36.3 24.4 %collective-permute-start.5 = (bf16[2,384,512]{2,1,0:T(8,128)(2,1)}, bf16[2,384,512]{2,1,0:T(8,128)(2,1)S(1)}, u32[]{:S(2)}, u32[]{:S(2)}) collective-permute-start(bf16[2,384,512]{2,1,0:T(8,128)(2,1)} %get-tuple-element.113), channel_id=1, source_target_pairs={{0,2},{2,0},{4,6},{6,4},{8,10},{10,8},{12,14},{14,12},{1,3},{3,1},... | collective-permute-start | bytes 2359304 | tf_op jit(solution)/shard_map/ppermute | solution.py:608
  47.4 39.2 %collective-permute-start.9 = (bf16[2,384,512]{2,1,0:T(8,128)(2,1)}, bf16[2,384,512]{2,1,0:T(8,128)(2,1)}, u32[]{:S(2)}, u32[]{:S(2)}) collective-permute-start(bf16[2,384,512]{2,1,0:T(8,128)(2,1)} %get-tuple-element.126), channel_id=1, source_target_pairs={{0,2},{2,0},{4,6},{6,4},{8,10},{10,8},{12,14},{14,12},{1,3},{3,1},... | collective-permute-start | bytes 2359304 | tf_op jit(solution)/shard_map/ppermute | solution.py:608
  58.2 6.4 %collective-permute-start.6 = (bf16[1024,256]{1,0:T(8,128)(2,1)}, bf16[1024,256]{1,0:T(8,128)(2,1)}, u32[]{:S(2)}, u32[]{:S(2)}) collective-permute-start(bf16[1024,256]{1,0:T(8,128)(2,1)} %get-tuple-element.116), channel_id=1, source_target_pairs={{0,1},{1,0},{2,3},{3,2},{4,5},{5,4},{6,7},{7,6},{8,9},{9,8},{10,11... | collective-permute-start | bytes 1572872 | tf_op jit(solution)/shard_map/ppermute | solution.py:605
  58.3 6.3 %collective-permute-start.7 = (bf16[1024,256]{1,0:T(8,128)(2,1)}, bf16[1024,256]{1,0:T(8,128)(2,1)}, u32[]{:S(2)}, u32[]{:S(2)}) collective-permute-start(bf16[1024,256]{1,0:T(8,128)(2,1)} %get-tuple-element.117), channel_id=1, source_target_pairs={{0,1},{1,0},{2,3},{3,2},{4,5},{5,4},{6,7},{7,6},{8,9},{9,8},{10,11... | collective-permute-start | bytes 1572872 | tf_op jit(solution)/shard_map/ppermute | solution.py:605
  58.8 34.3 %collective-permute-start.11 = (bf16[2,384,512]{2,1,0:T(8,128)(2,1)}, bf16[2,384,512]{2,1,0:T(8,128)(2,1)}, u32[]{:S(2)}, u32[]{:S(2)}) collective-permute-start(bf16[2,384,512]{2,1,0:T(8,128)(2,1)} %get-tuple-element.131), channel_id=1, source_target_pairs={{0,2},{2,0},{4,6},{6,4},{8,10},{10,8},{12,14},{14,12},{1,3},{3,1},... | collective-permute-start | bytes 2359304 | tf_op jit(solution)/shard_map/ppermute | solution.py:608
  62.0 24.6 %collective-permute-start.10 = (bf16[2,2,96,512]{3,2,1,0:T(8,128)(2,1)}, bf16[2,2,96,512]{3,2,1,0:T(8,128)(2,1)}, u32[]{:S(2)}, u32[]{:S(2)}) collective-permute-start(bf16[2,2,96,512]{3,2,1,0:T(8,128)(2,1)} %get-tuple-element.128), channel_id=1, source_target_pairs={{0,8},{2,10},{4,12},{6,14},{8,0},{10,2},{12,4},{14,6},{1,9},{3,11}... | collective-permute-start | bytes 1179656 | tf_op jit(solution)/shard_map/ppermute | solution.py:608
  69.2 16.3 %collective-permute-start.8 = (bf16[3,32,384]{2,1,0:T(8,128)(2,1)S(1)}, bf16[3,32,384]{2,1,0:T(8,128)(2,1)S(1)}, u32[]{:S(2)}, u32[]{:S(2)}) collective-permute-start(bf16[3,32,384]{2,1,0:T(8,128)(2,1)S(1)} %get-tuple-element.123), channel_id=1, source_target_pairs={{0,8},{2,10},{4,12},{6,14},{8,0},{10,2},{12,4},{14,6},{1,9},{3,11}... | collective-permute-start | bytes 221192 | tf_op jit(solution)/shard_map/ppermute | solution.py:620
  69.5 17.0 %copy-start.12 = (bf16[2,384,512]{2,1,0:T(8,128)(2,1)S(1)}, bf16[2,384,512]{2,1,0:T(8,128)(2,1)}, u32[]{:S(2)}) copy-start(bf16[2,384,512]{2,1,0:T(8,128)(2,1)} %copy-done.11) | copy-start | bytes 2359300
  77.8 16.9 %copy-start.9 = (bf16[2,384,512]{2,1,0:T(8,128)(2,1)S(1)}, bf16[2,384,512]{2,1,0:T(8,128)(2,1)}, u32[]{:S(2)}) copy-start(bf16[2,384,512]{2,1,0:T(8,128)(2,1)} %copy-done.8) | copy-start | bytes 2359300
  89.2 20.6 %copy-start.5 = (bf16[1024,512]{1,0:T(8,128)(2,1)S(1)}, bf16[1024,512]{1,0:T(8,128)(2,1)}, u32[]{:S(2)}) copy-start(bf16[1024,512]{1,0:T(8,128)(2,1)} %get-tuple-element.138.refs_2_) | copy-start | bytes 3145732
  89.2 20.6 %copy-start.6 = (bf16[1024,512]{1,0:T(8,128)(2,1)S(1)}, bf16[1024,512]{1,0:T(8,128)(2,1)}, u32[]{:S(2)}) copy-start(bf16[1024,512]{1,0:T(8,128)(2,1)} %get-tuple-element.139.refs_3_) | copy-start | bytes 3145732
  89.2 20.6 %copy-start.7 = (bf16[1024,512]{1,0:T(8,128)(2,1)S(1)}, bf16[1024,512]{1,0:T(8,128)(2,1)}, u32[]{:S(2)}) copy-start(bf16[1024,512]{1,0:T(8,128)(2,1)} %get-tuple-element.140.refs_4_) | copy-start | bytes 3145732
  89.2 16.3 %collective-permute-start.13 = (bf16[2,3,96,512]{3,2,1,0:T(8,128)(2,1)S(1)}, bf16[2,3,96,512]{3,2,1,0:T(8,128)(2,1)S(1)}, u32[]{:S(2)}, u32[]{:S(2)}) collective-permute-start(bf16[2,3,96,512]{3,2,1,0:T(8,128)(2,1)S(1)} %get-tuple-element.135), channel_id=1, source_target_pairs={{0,4},{2,6},{4,0},{6,2},{8,12},{10,14},{12,8},{14,10},{1,5},{3,7},... | collective-permute-start | bytes 1769480 | tf_op jit(solution)/shard_map/ppermute | solution.py:608
  89.9 4.8 %collective-permute-start.12 = (f32[64,384]{1,0:T(8,128)S(1)}, f32[64,384]{1,0:T(8,128)S(1)}, u32[]{:S(2)}, u32[]{:S(2)}) collective-permute-start(f32[64,384]{1,0:T(8,128)S(1)} %get-tuple-element.132.refs_3_), channel_id=1, source_target_pairs={{0,2},{2,0},{4,6},{6,4},{8,10},{10,8},{12,14},{14,12},{1,3},{3,1},... | collective-permute-start | bytes 294920 | tf_op jit(solution)/shard_map/ppermute | solution.py:608
  96.0 22.7 %collective-permute-start.14 = (bf16[1728,128]{1,0:T(8,128)(2,1)S(1)}, bf16[1728,128]{1,0:T(8,128)(2,1)S(1)}, u32[]{:S(2)}, u32[]{:S(2)}) collective-permute-start(bf16[1728,128]{1,0:T(8,128)(2,1)S(1)} %get-tuple-element.143), channel_id=1, source_target_pairs={{0,4},{2,6},{4,0},{6,2},{8,12},{10,14},{12,8},{14,10},{1,5},{3,7},... | collective-permute-start | bytes 1327112 | tf_op jit(solution)/shard_map/ppermute | solution.py:608
  106.9 13.1 %collective-permute-start.15 = (bf16[2,96,512]{2,1,0:T(8,128)(2,1)S(1)}, bf16[2,96,512]{2,1,0:T(8,128)(2,1)S(1)}, u32[]{:S(2)}, u32[]{:S(2)}) collective-permute-start(bf16[2,96,512]{2,1,0:T(8,128)(2,1)S(1)} %get-tuple-element.147), channel_id=1, source_target_pairs={{0,8},{2,10},{4,12},{6,14},{8,0},{10,2},{12,4},{14,6},{1,9},{3,11}... | collective-permute-start | bytes 589832 | tf_op jit(solution)/shard_map/ppermute | solution.py:608
  108.8 11.2 %collective-permute-start.16 = (bf16[160,384]{1,0:T(8,128)(2,1)S(1)}, bf16[160,384]{1,0:T(8,128)(2,1)S(1)}, u32[]{:S(2)}, u32[]{:S(2)}) collective-permute-start(bf16[160,384]{1,0:T(8,128)(2,1)S(1)} %get-tuple-element.149), channel_id=1, source_target_pairs={{0,2},{2,0},{4,6},{6,4},{8,10},{10,8},{12,14},{14,12},{1,3},{3,1},... | collective-permute-start | bytes 368648 | tf_op jit(solution)/shard_map/ppermute | solution.py:620
  109.1 10.9 %collective-permute-start.17 = (bf16[160,384]{1,0:T(8,128)(2,1)S(1)}, bf16[160,384]{1,0:T(8,128)(2,1)S(1)}, u32[]{:S(2)}, u32[]{:S(2)}) collective-permute-start(bf16[160,384]{1,0:T(8,128)(2,1)S(1)} %get-tuple-element.150), channel_id=1, source_target_pairs={{2,4},{4,2},{10,12},{12,10},{3,5},{5,3},{11,13},{13,11},{18,20},{2... | collective-permute-start | bytes 368648 | tf_op jit(solution)/shard_map/ppermute | solution.py:620
  109.8 10.2 %copy-start.10 = (bf16[4,16,16,384]{3,2,1,0:T(8,128)(2,1)S(1)}, bf16[4,16,16,384]{3,2,1,0:T(8,128)(2,1)}, u32[]{:S(2)}) copy-start(bf16[4,16,16,384]{3,2,1,0:T(8,128)(2,1)} %param.23) | copy-start | bytes 2359300
  113.2 15.8 %collective-permute-start.18 = (bf16[1024,384]{1,0:T(8,128)(2,1)S(1)}, bf16[1024,384]{1,0:T(8,128)(2,1)S(1)}, u32[]{:S(2)}, u32[]{:S(2)}) collective-permute-start(bf16[1024,384]{1,0:T(8,128)(2,1)S(1)} %get-tuple-element.153), channel_id=1, source_target_pairs={{0,1},{1,0},{2,3},{3,2},{4,5},{5,4},{6,7},{7,6},{8,9},{9,8},{10,11... | collective-permute-start | bytes 2359304 | tf_op jit(solution)/shard_map/ppermute | solution.py:605
  118.9 12.5 %collective-permute-start.19 = (bf16[960,128]{1,0:T(8,128)(2,1)S(1)}, bf16[960,128]{1,0:T(8,128)(2,1)S(1)}, u32[]{:S(2)}, u32[]{:S(2)}) collective-permute-start(bf16[960,128]{1,0:T(8,128)(2,1)S(1)} %get-tuple-element.160), channel_id=1, source_target_pairs={{0,8},{2,10},{4,12},{6,14},{8,0},{10,2},{12,4},{14,6},{1,9},{3,11}... | collective-permute-start | bytes 737288 | tf_op jit(solution)/shard_map/ppermute | solution.py:608
  120.0 9.0 %copy-start.15 = (f32[384]{0:T(512)S(1)}, f32[384]{0:T(512)}, u32[]{:S(2)}) copy-start(f32[384]{0:T(512)} %refs_5_.3) | copy-start | bytes 4612
  120.0 8.9 %copy-start.17 = (f32[384]{0:T(512)S(1)}, f32[384]{0:T(512)}, u32[]{:S(2)}) copy-start(f32[384]{0:T(512)} %refs_6_.1) | copy-start | bytes 4612
  (8 other events, 35.5 us)
